TPU v7x, 128 devices: a whole 4x4x4 slice. The times are simulated.
128 devices in a mesh: slab: 32 (over y, z, core), sub: 4 (over x).
Axes of the slice: x: 4, y: 4, z: 4, core: 2. Of those that a mesh axis runs over, the one named last changes fastest.
Arguments:
- features: bfloat16 [512, 64, 96, 128], P('slab', 'sub'), may hold values from -6 to 6
- voxel_mask: int32 [512, 64, 128], P('slab', 'sub'), may hold values from 0 to 1, as said below
- weight: bfloat16 [27, 96, 96], replicated, may hold values from -0.125 to 0.125
- norm_gain: float32 [96], replicated, may hold values from 0.5 to 1.5
- norm_bias: float32 [96], replicated, may hold values from -1 to 1
- out_grad: bfloat16 [512, 64, 96, 128], P('slab', 'sub'), may hold values from -6 to 6
Outputs:
- normed_out: bfloat16 [512, 64, 96, 128], P('slab', 'sub')
- feature_grad: bfloat16 [512, 64, 96, 128], P('slab', 'sub')
- weight_grad: float32 [27, 96, 96], replicated
- gain_grad: float32 [96], replicated
- bias_grad: float32 [96], replicated
Inputs may be any that keep to these rules, and one draw needn't show every extreme that they name: `voxel_mask`: the grid is cut into pillars of 8 x 8 x 128 voxels aligned to multiples of 8 along x and y. For every two devices with sub indices 2k and 2k+1 and the same slab index, exactly two of their pillars hold active voxels; one device holds at most 2 of them, and some device holds 2.
All inputs are finite; a program needn't handle non-finite values.
Results may differ from a plain program's by a relative error of at most 0.0049.
Values may be sent and summed in bfloat16 or wider, within the bound.
No kernel may reach another device: no remote copies, remote signals or barrier semaphores. Data moves between devices by JAX's collectives and lax.ppermute only.
A program may use at most 384 MiB of HBM per device.

v0:
```python
import jax
import jax.numpy as jnp
from jax import lax
from jax.sharding import PartitionSpec as P

BRICK = 8
SLOTS = 2


EPSILON = 1e-05


def padded(cells, sides, width):
    for axis, dim in sides:
        count = lax.axis_size(axis)
        ends = count - 1
        head = lax.slice_in_dim(cells, 0, width, axis=dim)
        tail = lax.slice_in_dim(cells, cells.shape[dim] - width, cells.shape[dim], axis=dim)
        cells = jnp.concatenate(
            [
                lax.ppermute(tail, axis, [(i, (i + 1) % count) for i in range(ends)]),
                cells,
                lax.ppermute(head, axis, [((i + 1) % count, i) for i in range(ends)]),
            ],
            axis=dim,
        )
    return cells


def plane_columns(patches, flipped):
    pieces = []
    for first in range(3):
        for second in range(3):
            row = 2 - first if flipped else first
            col = 2 - second if flipped else second
            pieces.append(patches[:, row : row + BRICK, col : col + BRICK])
    stacked = jnp.stack(pieces, axis=3)
    shape = stacked.shape
    return stacked.reshape(shape[0], shape[1], shape[2], shape[3] * shape[4], shape[5])


def convolve(weight, patches):
    chans = weight.shape[1]
    depth = patches.shape[-1] - 2
    forward_w = (
        weight.reshape(9, 3, chans, chans).transpose(1, 2, 0, 3).reshape(3, chans, 9 * chans)
    )
    planes = jnp.einsum(
        "kom,nxymz->nxykoz",
        forward_w,
        plane_columns(patches, False),
        preferred_element_type=jnp.float32,
    )
    return (
        planes[:, :, :, 0, :, 0:depth]
        + planes[:, :, :, 1, :, 1 : 1 + depth]
        + planes[:, :, :, 2, :, 2 : 2 + depth]
    )


def transpose_conv(weight, patches):
    chans = weight.shape[1]
    depth = patches.shape[-1] - 2
    back_w = weight.reshape(9, 3, chans, chans).transpose(1, 3, 0, 2).reshape(3, chans, 9 * chans)
    planes = jnp.einsum(
        "kcm,nxymz->nxykcz",
        back_w,
        plane_columns(patches, True),
        preferred_element_type=jnp.float32,
    )
    return (
        planes[:, :, :, 0, :, 2 : 2 + depth]
        + planes[:, :, :, 1, :, 1 : 1 + depth]
        + planes[:, :, :, 2, :, 0:depth]
    )


def weight_terms(grads, patches):
    chans = grads.shape[3]
    shifted = jnp.stack(
        [jnp.pad(grads, ((0, 0), (0, 0), (0, 0), (0, 0), (lag, 2 - lag))) for lag in range(3)],
        axis=3,
    )
    terms = jnp.einsum(
        "nxykoz,nxymz->kom",
        shifted,
        plane_columns(patches, False),
        preferred_element_type=jnp.float32,
    )
    return terms.reshape(3, chans, 9, chans).transpose(2, 0, 1, 3).reshape(27, chans, chans)


def slot_starts(voxel_mask):
    across = voxel_mask.shape[0] // BRICK
    along = voxel_mask.shape[1] // BRICK
    flags = (
        voxel_mask.reshape(across, BRICK, along, BRICK, voxel_mask.shape[2])
        .max(axis=(1, 3, 4))
        .reshape(-1)
    )
    before = jnp.cumsum(flags) - flags
    position = jnp.arange(flags.shape[0], dtype=jnp.int32)
    occupied = jnp.sum(flags)
    rank = jnp.where(flags == 1, before, occupied + position - before)
    starts = []
    for slot in range(SLOTS):
        chosen = jnp.sum(jnp.where(rank == slot, position, 0))
        starts.append((chosen // along * BRICK, chosen % along * BRICK))
    return (starts, occupied)


def cut_block(field, start, size):
    zero = jnp.int32(0)
    return lax.dynamic_slice(
        field, (start[0], start[1]) + (zero,) * (field.ndim - 2), (size, size) + field.shape[2:]
    )


def place_blocks(shape, dtype, blocks, starts):
    zero = jnp.int32(0)
    field = jnp.zeros(shape, dtype)
    for block, start in zip(blocks, starts):
        field = lax.dynamic_update_slice(field, block, (start[0], start[1], zero, zero))
    return field


def body(features, voxel_mask, weight, norm_gain, norm_bias, out_grad):
    mask_bf = voxel_mask.astype(jnp.bfloat16)
    masked = features * mask_bf[:, :, None, :]
    widened = padded(masked, (("slab", 0), ("sub", 1)), 1)
    extended = jnp.pad(widened, ((0, 0), (0, 0), (0, 0), (1, 1)))
    starts, occupied = slot_starts(voxel_mask)
    span = BRICK + 2
    own_patches = jnp.stack([cut_block(extended, start, span) for start in starts])
    own_grads = jnp.stack([cut_block(out_grad, start, BRICK) for start in starts])
    own_masks = jnp.stack([cut_block(mask_bf, start, BRICK) for start in starts])
    work_patches, work_grads, work_masks = (own_patches, own_grads, own_masks)
    weights_f = work_masks.astype(jnp.float32)[:, :, :, None, :]
    conv_out = convolve(weight, work_patches) * weights_f
    count, total, squares = lax.psum(
        (
            jnp.sum(weights_f),
            jnp.sum(conv_out, axis=(0, 1, 2, 4)),
            jnp.sum(conv_out * conv_out, axis=(0, 1, 2, 4)),
        ),
        ("slab", "sub"),
    )
    mean = total / count
    inv_std = lax.rsqrt(squares / count - mean * mean + EPSILON)
    normed = (conv_out - mean[:, None]) * inv_std[:, None] * weights_f
    y_blocks = ((norm_gain[:, None] * normed + norm_bias[:, None]) * weights_f).astype(jnp.bfloat16)
    upstream = work_grads.astype(jnp.float32) * weights_f
    bias_grad, gain_grad = lax.psum(
        (jnp.sum(upstream, axis=(0, 1, 2, 4)), jnp.sum(upstream * normed, axis=(0, 1, 2, 4))),
        ("slab", "sub"),
    )
    scaled = (norm_gain * inv_std)[:, None]
    dh_blocks = (
        scaled
        * (upstream - (bias_grad / count)[:, None] - normed * (gain_grad / count)[:, None])
        * weights_f
    ).astype(jnp.bfloat16)
    weight_part = weight_terms(dh_blocks, work_patches)
    y_slots = [y_blocks[slot] for slot in range(SLOTS)]
    dh_slots = [dh_blocks[slot] for slot in range(SLOTS)]
    normed_out = place_blocks(features.shape, jnp.bfloat16, y_slots, starts)
    dh_dense = place_blocks(features.shape, jnp.bfloat16, dh_slots, starts)
    grad_wide = padded(dh_dense, (("slab", 0), ("sub", 1)), 1)
    grad_ext = jnp.pad(grad_wide, ((0, 0), (0, 0), (0, 0), (1, 1)))
    own_dpatches = jnp.stack([cut_block(grad_ext, start, span) for start in starts])
    dx_blocks = (transpose_conv(weight, own_dpatches) * weights_f).astype(jnp.bfloat16)
    dx_slots = [dx_blocks[slot] for slot in range(SLOTS)]
    feature_grad = place_blocks(features.shape, jnp.bfloat16, dx_slots, starts)
    weight_grad = lax.psum(weight_part, ("slab", "sub"))
    return (normed_out, feature_grad, weight_grad, gain_grad, bias_grad)


def solution(mesh):
    placed = (
        P("slab", "sub", None, None),
        P("slab", "sub", None),
        P(),
        P(),
        P(),
        P("slab", "sub", None, None),
    )
    return jax.shard_map(
        body,
        mesh=mesh,
        in_specs=placed,
        out_specs=(P("slab", "sub", None, None), P("slab", "sub", None, None), P(), P(), P()),
        check_vma=False,
    )
```

profile of v0, /device:TPU:14, one launch (start us, length us, event | category | flops | bytes accessed | tf_op | source)
XLA Modules:
  0.0 756.3 jit_solution(17684475009513428090)
XLA Ops:
  8.5 3.2 broadcast_multiply_fusion
  11.8 2.7 copy-done.2
  16.4 5.8 collective-permute-start.1
  23.4 2.3 collective-permute-done
  27.5 2.3 pad_maximum_fusion.8
  31.1 5.3 collective-permute-start.3
  42.9 2.2 constant_dynamic-slice_fusion.3
  45.1 2.9 copy.124
  48.0 2.9 copy.125
  53.7 20.2 %select_maximum_fusion.4 = bf16[18,18,96,130]{3,2,1,0:T(8,128)(2,1)} fusion(bf16[18,1,96,128]{3,2,1,0:T(8,128)(2,1)} %collective-permute-done.3, bf16[18,1,96,128]{3,2,1,0:T(8,128)(2,1)} %collective-permute-done.2, bf16[1,16,96,128]{3,2,1,0:T(8,128)(2,1)} %copy-done.12, bf16[16,16,96,128]{3,2,1,0:T(8,128)(2,1)} %copy-done.2, ...), kind=kLoop, calls=%fused_computation.14 | loop fusion | flops 72783360 | bytes 16049664 | tf_op jit(solution)/shard_map/concatenate | solution.py:19
  73.9 9.0 %constant_dynamic-slice_fusion.4 = (bf16[10,10,96,130]{3,2,1,0:T(8,128)(2,1)}, bf16[10,10,96,130]{3,2,1,0:T(8,128)(2,1)}) fusion(bf16[18,18,96,130]{3,2,1,0:T(8,128)(2,1)} %select_maximum_fusion.4, s32[]{:T(128)S(6)} %select_n.104, s32[]{:T(128)S(6)} %select_n.106, s32[]{:T(128)S(6)} %select_n.99, s32[]{:T(128)S(6)} %select_n.101), kind=kLoop, calls=%fused_computation.162 | loop fusion | bytes 9984016 | tf_op jit(solution)/shard_map/dynamic_slice | solution.py:114
  82.9 6.7 copy.111
  89.6 7.7 %copy.112 = bf16[10,10,96,130]{2,3,1,0:T(8,128)(2,1)} copy(bf16[10,10,96,130]{3,2,1,0:T(8,128)(2,1)} %get-tuple-element.22) | data formatting | bytes 4992000 | tf_op jit(solution)/shard_map/dynamic_slice | solution.py:114
  97.3 4.0 fusion.54
  101.3 2.5 fusion.57
  103.8 2.6 fusion.60
  106.4 2.6 fusion.63
  108.9 2.6 fusion.66
  111.5 2.6 fusion.69
  114.1 2.6 fusion.72
  116.7 2.6 fusion.51
  119.3 3.3 fusion.76
  122.6 35.8 %copy.142 = bf16[2,8,8,9,96,130]{4,3,2,5,1,0:T(8,128)(2,1)} copy(bf16[2,8,8,9,96,130]{4,5,3,2,1,0:T(8,128)(2,1)} %fusion.76) | data formatting | bytes 57507840 | tf_op jit(solution)/shard_map/stack | solution.py:37
  158.4 30.2 %fusion.7 = f32[2,8,8,3,96,130]{4,5,3,2,1,0:T(8,128)} fusion(bf16[2,8,8,9,96,130]{4,5,3,2,1,0:T(8,128)(2,1)} %fusion.76, bf16[9,3,96,96]{3,2,1,0:T(8,128)(2,1)S(1)} %bitcast.245), kind=kOutput, calls=%fused_computation.9 | convolution fusion | flops 8281128960 | bytes 48420864 | tf_op jit(solution)/shard_map/kom,nxymz->nxykoz/dot_general | solution.py:48
  188.7 12.8 %multiply_reduce_fusion.1 = (f32[96]{0:T(128)S(1)}, f32[96]{0:T(128)S(1)}, f32[2,8,8,96,128]{3,4,2,1,0:T(8,128)}) fusion(f32[2,8,8,128]{3,2,1,0:T(8,128)S(1)} %maximum_convert_fusion, f32[2,8,8,3,96,130]{4,5,3,2,1,0:T(8,128)} %fusion.7), kind=kLoop, calls=%fused_computation.71 | loop fusion | flops 9436992 | bytes 25232128 | tf_op jit(solution)/shard_map/reduce_sum | solution.py:144
  201.5 65.3 %all-reduce.6 = (f32[96]{0:T(128)S(1)}, f32[]{:T(128)}, f32[96]{0:T(128)S(1)}) all-reduce(f32[96]{0:T(128)S(1)} %get-tuple-element.6, f32[]{:T(128)} %convert_reduce_fusion, f32[96]{0:T(128)S(1)} %get-tuple-element.5), channel_id=1, replica_groups=mesh['slab'=32,'sub'=4] {'slab','sub'}, use_global_device_ids=true, to_apply=%region_7.8 | all-reduce | flops 193 | bytes 1544 | tf_op jit(solution)/shard_map/psum | solution.py:140
  267.5 6.2 fusion.24
  273.7 63.1 %all-reduce.5 = (f32[96]{0:T(128)S(1)}, f32[96]{0:T(128)S(1)}) all-reduce(f32[96]{0:T(128)S(1)} %get-tuple-element.8, f32[96]{0:T(128)S(1)} %get-tuple-element.7), channel_id=1, replica_groups=mesh['slab'=32,'sub'=4] {'slab','sub'}, use_global_device_ids=true, to_apply=%region_15.16 | all-reduce | flops 192 | bytes 1536 | tf_op jit(solution)/shard_map/psum | solution.py:153
  338.1 8.4 %multiply_convert_fusion = (bf16[2,8,8,96,128]{3,4,2,1,0:T(8,128)(2,1)S(1)}, bf16[2,8,8,96,128]{3,4,2,1,0:T(8,128)(2,1)}) fusion(f32[2,8,8,96,128]{3,4,2,1,0:T(8,128)} %get-tuple-element.19, f32[96]{0:T(128)S(1)} %broadcast_divide_fusion, f32[96]{0:T(128)S(1)} %broadcast_divide_fusion.1, f32[96]{0:T(128)S(1)} %get-tuple-element.16, ...), kind=kLoop, calls=%fused_computation.65 | loop fusion | flops 25165824 | bytes 15796864 | tf_op jit(solution)/shard_map/convert_element_type | solution.py:162
  346.5 6.4 pad_bitcast_fusion.2
  354.6 83.2 %reshape.143 = bf16[2,8,8,864,130]{3,2,4,1,0:T(8,128)(2,1)} reshape(bf16[2,8,8,9,96,130]{4,3,2,5,1,0:T(8,128)(2,1)} %copy.142) | data formatting | bytes 57507840 | tf_op jit(solution)/shard_map/reshape | solution.py:39
  437.9 89.4 %dot_general.16 = bf16[9,96,2,8,8,130]{1,0,4,5,3,2:T(8,128)(2,1)} reshape(bf16[864,2,8,8,130]{0,3,4,2,1:T(8,128)(2,1)} %bitcast.236) | data formatting | bytes 57507840 | tf_op jit(solution)/shard_map/nxykoz,nxymz->kom/dot_general | solution.py:84
  527.2 3.9 copy.126
  531.1 2.5 copy.127
  536.7 2.7 copy-done.3
  541.4 5.8 collective-permute-start.5
  547.1 47.2 %fusion.2 = f32[3,96,9,96,1,1,1]{3,1,6,5,0,2,4:T(8,128)} fusion(bf16[9,96,2,8,8,130,1]{1,0,4,5,3,2,6:T(8,128)(2,1)} %bitcast.74, bf16[2,8,8,1,96,130]{4,5,2,1,0,3:T(8,128)(2,1)} %get-tuple-element.37, bf16[2,8,8,1,96,130]{4,5,2,1,0,3:T(8,128)(2,1)} %get-tuple-element.38, bf16[2,8,8,1,96,130]{4,5,2,1,0,3:T(8,128)(2,1)} %get-tuple-element.36), kind=kOutput, calls=%fused_computation.4 | convolution fusion | flops 8290713600 | bytes 39333888 | tf_op jit(solution)/shard_map/nxykoz,nxymz->kom/dot_general | solution.py:84
  594.4 2.3 pad_maximum_fusion.5
  598.0 5.3 collective-permute-start.7
  603.4 2.5 slice_bitcast_fusion.4
  605.9 4.2 copy.122
  610.1 3.9 copy.123
  614.0 3.9 broadcast.120.clone.2
  617.9 2.8 constant_dynamic-update-slice_fusion.5
  620.8 19.6 %select_maximum_fusion = bf16[18,18,96,130]{3,2,1,0:T(8,128)(2,1)} fusion(bf16[18,1,96,128]{3,2,1,0:T(8,128)(2,1)} %collective-permute-done.7, bf16[18,1,96,128]{3,2,1,0:T(8,128)(2,1)S(1)} %collective-permute-done.6, bf16[1,16,96,128]{3,2,1,0:T(8,128)(2,1)S(1)} %collective-permute-done.5, bf16[16,16,96,128]{3,2,1,0:T(8,128)(2,1)S(1)} %bitcast.238, ...), kind=kLoop, calls=%fused_computation.10 | loop fusion | flops 72783360 | bytes 16049664 | tf_op jit(solution)/shard_map/concatenate | solution.py:19
  640.3 9.0 %constant_dynamic-slice_fusion = (bf16[10,10,96,130]{3,2,1,0:T(8,128)(2,1)}, bf16[10,10,96,130]{3,2,1,0:T(8,128)(2,1)}) fusion(bf16[18,18,96,130]{3,2,1,0:T(8,128)(2,1)} %select_maximum_fusion, s32[]{:T(128)S(6)} %select_n.104, s32[]{:T(128)S(6)} %select_n.106, s32[]{:T(128)S(6)} %select_n.99, s32[]{:T(128)S(6)} %select_n.101), kind=kLoop, calls=%fused_computation.154 | loop fusion | bytes 9984016 | tf_op jit(solution)/shard_map/dynamic_slice | solution.py:114
  649.3 6.7 copy.128
  656.0 7.8 %copy.129 = bf16[10,10,96,130]{2,3,1,0:T(8,128)(2,1)} copy(bf16[10,10,96,130]{3,2,1,0:T(8,128)(2,1)} %get-tuple-element.20) | data formatting | bytes 4992000 | tf_op jit(solution)/shard_map/dynamic_slice | solution.py:114
  663.7 4.0 fusion.30
  667.7 2.6 fusion.33
  670.3 2.7 fusion.36
  673.0 2.7 fusion.39
  675.6 2.6 fusion.42
  678.3 2.5 fusion.45
  680.8 2.6 fusion.48
  683.4 2.6 fusion.27
  686.1 3.3 fusion.74
  689.3 30.4 %fusion.16 = f32[2,8,8,3,96,130]{4,5,2,1,0,3:T(8,128)} fusion(bf16[2,8,8,9,96,130]{4,5,3,2,1,0:T(8,128)(2,1)} %fusion.74, bf16[9,3,96,96]{2,3,0,1:T(8,128)(2,1)} %copy.138), kind=kOutput, calls=%fused_computation.55 | convolution fusion | flops 8281128960 | bytes 48420864 | tf_op jit(solution)/shard_map/kcm,nxymz->nxykcz/dot_general | solution.py:65
  719.7 9.8 %fusion.21 = bf16[2,8,8,96,128]{3,4,2,1,0:T(8,128)(2,1)S(1)} fusion(f32[2,8,8,3,96,130]{4,5,2,1,0,3:T(8,128)} %fusion.16, f32[2,8,8,128]{3,2,1,0:T(8,128)S(1)} %copy-done.10), kind=kLoop, calls=%fused_computation.59 | loop fusion | flops 6291456 | bytes 22085632 | tf_op jit(solution)/shard_map/convert_element_type | solution.py:171
  731.3 3.9 copy.140
  735.1 2.5 copy.141
  737.6 3.9 broadcast.120.clone
  741.5 2.8 constant_dynamic-update-slice_fusion.1
  746.6 2.5 copy.193
  (77 shorter events, 25.8 us)
Async XLA Ops:
  7.2 739.4 %all-reduce.9.cloned.1.call-start = ((), (), s32[]{:S(2)}) async-start(), calls=%async_computation | async-start | bytes 2654208 | tf_op jit(solution)/shard_map/psum | solution.py:174
  11.8 2.7 copy-start.2
  14.5 11.2 %collective-permute-start = (bf16[1,16,96,128]{3,2,1,0:T(8,128)(2,1)S(1)}, bf16[1,16,96,128]{3,2,1,0:T(8,128)(2,1)S(1)}, u32[]{:S(2)}, u32[]{:S(2)}) collective-permute-start(bf16[1,16,96,128]{3,2,1,0:T(8,128)(2,1)S(1)} %get-tuple-element.34), channel_id=1, source_target_pairs={{0,4},{4,8},{8,12},{12,16},{16,20},{20,24},{24,28},{28,32},{32,36}... | collective-permute-start | bytes 1179656 | tf_op jit(solution)/shard_map/ppermute | solution.py:21
  16.4 11.0 %collective-permute-start.1 = (bf16[1,16,96,128]{3,2,1,0:T(8,128)(2,1)S(1)}, bf16[1,16,96,128]{3,2,1,0:T(8,128)(2,1)S(1)}, u32[]{:S(2)}, u32[]{:S(2)}) collective-permute-start(bf16[1,16,96,128]{3,2,1,0:T(8,128)(2,1)S(1)} %get-tuple-element.35), channel_id=1, source_target_pairs={{4,0},{8,4},{12,8},{16,12},{20,16},{24,20},{28,24},{32,28},{36,32}... | collective-permute-start | bytes 1179656 | tf_op jit(solution)/shard_map/ppermute | solution.py:23
  25.7 17.2 %copy-start.11 = (bf16[1,16,96,128]{3,2,1,0:T(8,128)(2,1)}, bf16[1,16,96,128]{3,2,1,0:T(8,128)(2,1)S(1)}, u32[]{:S(2)}) copy-start(bf16[1,16,96,128]{3,2,1,0:T(8,128)(2,1)S(1)} %collective-permute-done) | copy-start | bytes 1179652
  27.5 15.4 %copy-start.12 = (bf16[1,16,96,128]{3,2,1,0:T(8,128)(2,1)}, bf16[1,16,96,128]{3,2,1,0:T(8,128)(2,1)S(1)}, u32[]{:S(2)}) copy-start(bf16[1,16,96,128]{3,2,1,0:T(8,128)(2,1)S(1)} %collective-permute-done.1) | copy-start | bytes 1179652
  29.8 23.9 %collective-permute-start.2 = (bf16[18,1,96,128]{3,2,1,0:T(8,128)(2,1)}, bf16[18,1,96,128]{3,2,1,0:T(8,128)(2,1)}, u32[]{:S(2)}, u32[]{:S(2)}) collective-permute-start(bf16[18,1,96,128]{3,2,1,0:T(8,128)(2,1)} %get-tuple-element.28), channel_id=1, source_target_pairs={{0,1},{1,2},{2,3},{4,5},{5,6},{6,7},{8,9},{9,10},{10,11},{12,13},{... | collective-permute-start | bytes 1327112 | tf_op jit(solution)/shard_map/ppermute | solution.py:21
  31.1 22.7 %collective-permute-start.3 = (bf16[18,1,96,128]{3,2,1,0:T(8,128)(2,1)}, bf16[18,1,96,128]{3,2,1,0:T(8,128)(2,1)}, u32[]{:S(2)}, u32[]{:S(2)}) collective-permute-start(bf16[18,1,96,128]{3,2,1,0:T(8,128)(2,1)} %get-tuple-element.29), channel_id=1, source_target_pairs={{1,0},{2,1},{3,2},{5,4},{6,5},{7,6},{9,8},{10,9},{11,10},{13,12},{... | collective-permute-start | bytes 1327112 | tf_op jit(solution)/shard_map/ppermute | solution.py:23
  53.7 284.4 %copy-start.9 = (f32[2,8,8,128]{3,2,1,0:T(8,128)}, f32[2,8,8,128]{3,2,1,0:T(8,128)S(1)}, u32[]{:S(2)}) copy-start(f32[2,8,8,128]{3,2,1,0:T(8,128)S(1)} %maximum_convert_fusion) | copy-start | bytes 196612
  97.3 4.0 copy-start
  122.6 35.8 %copy-start.13 = (bf16[27,96,96]{2,1,0:T(8,128)(2,1)S(1)}, bf16[27,96,96]{2,1,0:T(8,128)(2,1)}, u32[]{:S(2)}) copy-start(bf16[27,96,96]{2,1,0:T(8,128)(2,1)} %param.8) | copy-start | bytes 1492996
  188.6 78.2 %copy-start.14 = (f32[96]{0:T(128)S(1)}, f32[96]{0:T(128)}, u32[]{:S(2)}) copy-start(f32[96]{0:T(128)} %param.9) | copy-start | bytes 1156
  188.7 78.8 %copy-start.4 = (bf16[8,8,96,128]{2,3,1,0:T(8,128)(2,1)S(1)}, bf16[8,8,96,128]{2,3,1,0:T(8,128)(2,1)}, u32[]{:S(2)}) copy-start(bf16[8,8,96,128]{2,3,1,0:T(8,128)(2,1)} %copy.124) | copy-start | bytes 4718596
  201.5 136.6 %copy-start.15 = (f32[96]{0:T(128)S(1)}, f32[96]{0:T(128)}, u32[]{:S(2)}) copy-start(f32[96]{0:T(128)} %param.10) | copy-start | bytes 1156
  336.8 9.7 %copy-start.16 = (f32[96]{0:T(128)}, f32[96]{0:T(128)S(1)}, u32[]{:S(2)}) copy-start(f32[96]{0:T(128)S(1)} %get-tuple-element.56) | copy-start | bytes 1156
  336.8 9.7 %copy-start.17 = (f32[96]{0:T(128)}, f32[96]{0:T(128)S(1)}, u32[]{:S(2)}) copy-start(f32[96]{0:T(128)S(1)} %get-tuple-element.57) | copy-start | bytes 1156
  533.6 2.9 copy-start.6
  536.7 2.7 copy-start.3
  539.4 54.9 %collective-permute-start.4 = (bf16[1,16,96,128]{3,2,1,0:T(8,128)(2,1)S(1)}, bf16[1,16,96,128]{3,2,1,0:T(8,128)(2,1)S(1)}, u32[]{:S(2)}, u32[]{:S(2)}) collective-permute-start(bf16[1,16,96,128]{3,2,1,0:T(8,128)(2,1)S(1)} %get-tuple-element.30), channel_id=1, source_target_pairs={{0,4},{4,8},{8,12},{12,16},{16,20},{20,24},{24,28},{28,32},{32,36}... | collective-permute-start | bytes 1179656 | tf_op jit(solution)/shard_map/ppermute | solution.py:21
  541.4 53.0 %collective-permute-start.5 = (bf16[1,16,96,128]{3,2,1,0:T(8,128)(2,1)S(1)}, bf16[1,16,96,128]{3,2,1,0:T(8,128)(2,1)S(1)}, u32[]{:S(2)}, u32[]{:S(2)}) collective-permute-start(bf16[1,16,96,128]{3,2,1,0:T(8,128)(2,1)S(1)} %get-tuple-element.31), channel_id=1, source_target_pairs={{4,0},{8,4},{12,8},{16,12},{20,16},{24,20},{28,24},{32,28},{36,32}... | collective-permute-start | bytes 1179656 | tf_op jit(solution)/shard_map/ppermute | solution.py:23
  594.4 9.0 %copy-start.5 = (bf16[2,8,8,96,128]{3,4,2,1,0:T(8,128)(2,1)S(1)}, bf16[2,8,8,96,128]{3,4,2,1,0:T(8,128)(2,1)}, u32[]{:S(2)}) copy-start(bf16[2,8,8,96,128]{3,4,2,1,0:T(8,128)(2,1)} %get-tuple-element.25) | copy-start | bytes 9437188
  596.7 24.0 %collective-permute-start.6 = (bf16[18,1,96,128]{3,2,1,0:T(8,128)(2,1)}, bf16[18,1,96,128]{3,2,1,0:T(8,128)(2,1)S(1)}, u32[]{:S(2)}, u32[]{:S(2)}) collective-permute-start(bf16[18,1,96,128]{3,2,1,0:T(8,128)(2,1)} %get-tuple-element.26), channel_id=1, source_target_pairs={{0,1},{1,2},{2,3},{4,5},{5,6},{6,7},{8,9},{9,10},{10,11},{12,13},{... | collective-permute-start | bytes 1327112 | tf_op jit(solution)/shard_map/ppermute | solution.py:21
  598.0 22.7 %collective-permute-start.7 = (bf16[18,1,96,128]{3,2,1,0:T(8,128)(2,1)}, bf16[18,1,96,128]{3,2,1,0:T(8,128)(2,1)}, u32[]{:S(2)}, u32[]{:S(2)}) collective-permute-start(bf16[18,1,96,128]{3,2,1,0:T(8,128)(2,1)} %get-tuple-element.27), channel_id=1, source_target_pairs={{1,0},{2,1},{3,2},{5,4},{6,5},{7,6},{9,8},{10,9},{11,10},{13,12},{... | collective-permute-start | bytes 1327112 | tf_op jit(solution)/shard_map/ppermute | solution.py:23
  605.9 14.8 %slice-start = ((s8[6291456]{0:T(1024)(128)(4,1)}), s8[2097152]{0:T(1024)(128)(4,1)S(1)}, s32[]{:S(2)}) async-start(s8[6291456]{0:T(1024)(128)(4,1)} %bitcast.237), calls=%async_computation.1 | async-start | bytes 4194304
  614.0 6.8 slice-start.1
  663.7 4.0 copy-start.1
  689.3 30.4 %copy-start.10 = (f32[2,8,8,128]{3,2,1,0:T(8,128)S(1)}, f32[2,8,8,128]{3,2,1,0:T(8,128)}, u32[]{:S(2)}) copy-start(f32[2,8,8,128]{3,2,1,0:T(8,128)} %copy-done.9) | copy-start | bytes 196612
  737.6 6.7 copy-start.7
  737.6 6.7 copy-start.8
Sparse Core Ops, SparseCore 0:
  594.5 145.6 all-reduce.8
where the time goes:
time: 771 us; the launch traced here: 756 us
  local copies, waits for them, and re-layouts  325 us (42%)
  other arithmetic  142 us (18%)
  blocking collectives  128 us (17%)
  matrix products  108 us (14%)
  starting transfers between devices  28.6 us (4%)
  between operations  20 us (3%)
    dot_general x1, local copies, waits for them, and re-layouts, weight_terms(): jnp.einsum('nxykoz,nxymz->kom', shifted, plane_columns(patches, False), p...  89.4 us
    reshape x1, local copies, waits for them, and re-layouts, plane_columns(): stacked.reshape(shape[0], shape[1], shape[2], shape[3] * shape[4], shape[5])  83.2 us
    psum x1, blocking collectives, body(): lax.psum((jnp.sum(weights_f), jnp.sum(conv_out, axis=(0, 1, 2, 4)), jnp.s...  65.3 us
    psum x1, blocking collectives, body(): lax.psum((jnp.sum(upstream, axis=(0, 1, 2, 4)), jnp.sum(upstream * normed...  63.1 us
    dynamic_slice x9, local copies, waits for them, and re-layouts, cut_block(): lax.dynamic_slice(field, (start[0], start[1]) + (zero,) * (field.ndim - 2...  54.7 us
    dot_general x1, matrix products, weight_terms(): jnp.einsum('nxykoz,nxymz->kom', shifted, plane_columns(patches, False), p...  47.2 us
    unnamed x17, other arithmetic  44.4 us
    concatenate x2, other arithmetic, padded(): jnp.concatenate([lax.ppermute(tail, axis, [(i, (i + 1) % count) for i in...  39.7 us
  transfers between devices with their start and end apart: 9, of which 2 were waited for; matrix products, arithmetic and copies ran while one was open for 27% of the time, Pallas kernels for 0%

commit v1 on v0

v1 whole, which is shorter than its diff:
```python
import functools

import jax
import jax.numpy as jnp
from jax import lax
from jax.experimental import pallas as pl
from jax.experimental.pallas import tpu as pltpu
from jax.sharding import PartitionSpec as P

BRICK = 8
SLOTS = 2
EPSILON = 1e-05
DEVICES = 128
CHANS = 96
DEPTH = 128
TILES = 7
ROWS = 3 * CHANS
COLS = TILES * DEPTH
F32 = jnp.float32
BF16 = jnp.bfloat16
VMEM_LIMIT = 56 * 1024 * 1024

ANY = pl.BlockSpec(memory_space=pl.ANY)
VMEM = pl.BlockSpec(memory_space=pltpu.VMEM)
SMEM = pl.BlockSpec(memory_space=pltpu.SMEM)


def slot_table(voxel_mask):
    across = voxel_mask.shape[0] // BRICK
    along = voxel_mask.shape[1] // BRICK
    flags = (
        voxel_mask.reshape(across, BRICK, along, BRICK, voxel_mask.shape[2])
        .max(axis=(1, 3, 4))
        .reshape(-1)
    )
    before = jnp.cumsum(flags) - flags
    position = jnp.arange(flags.shape[0], dtype=jnp.int32)
    occupied = jnp.sum(flags)
    rank = jnp.where(flags == 1, before, occupied + position - before)
    order = jnp.sum(jnp.where(rank[None, :] == position[:, None], position[None, :], 0), axis=1)
    table = jnp.stack([order // along * BRICK, order % along * BRICK], axis=1).reshape(-1)
    return jnp.concatenate([table, occupied[None]]).astype(jnp.int32)


def corner(meta, slot):
    return (pl.multiple_of(meta[2 * slot], BRICK), pl.multiple_of(meta[2 * slot + 1], BRICK))


def rim_copies(rims, field, sems):
    xm, xp, ym, yp = rims
    return [
        pltpu.make_async_copy(xm, field.at[0, pl.ds(1, 16)], sems.at[0]),
        pltpu.make_async_copy(xp, field.at[17, pl.ds(1, 16)], sems.at[1]),
        pltpu.make_async_copy(ym, field.at[:, 0], sems.at[2]),
        pltpu.make_async_copy(yp, field.at[:, 17], sems.at[3]),
    ]


def zero_pillars(meta, field, edge):
    occupied = meta[8]
    for slot in range(4):

        @pl.when(slot >= occupied)
        def _():
            x0, y0 = corner(meta, slot)

            def clear(row, carry):
                for col in range(BRICK):
                    field[x0 + row + edge, y0 + col + edge] = jnp.zeros((CHANS, DEPTH), field.dtype)
                return carry

            lax.fori_loop(0, BRICK, clear, 0)


def mask_pillar(meta, slot, mask, field):
    x0, y0 = corner(meta, slot)

    def apply(row, carry):
        active = mask[x0 + row, pl.ds(y0, BRICK), :]
        for col in range(BRICK):
            keep = jnp.broadcast_to(active[col : col + 1], (CHANS, DEPTH)).astype(BF16)
            at = (x0 + row + 1, y0 + col + 1)
            field[at] = field[at] * keep
        return carry

    lax.fori_loop(0, BRICK, apply, 0)


def column_convs(field, kernel_ref, x, y0, flipped):
    lane = lax.broadcasted_iota(jnp.int32, (CHANS, DEPTH), 1)
    up, down = (2, 0) if flipped else (0, 2)
    outs = []
    for pair in range(BRICK // 2):
        pieces = []
        for a in range(3):
            for b in range(3):
                col = y0 + 2 * pair + b
                pieces.append(jnp.concatenate([field[x + a, col], field[x + a, col + 1]], axis=1))
        pieces.append(jnp.zeros((COLS - 9 * CHANS, 2 * DEPTH), BF16))
        planes = jnp.dot(
            kernel_ref[...], jnp.concatenate(pieces, axis=0), preferred_element_type=F32
        )
        for half in range(2):
            part = [
                planes[CHANS * e : CHANS * (e + 1), DEPTH * half : DEPTH * (half + 1)]
                for e in range(3)
            ]
            outs.append(
                part[1]
                + jnp.where(lane == 0, 0.0, pltpu.roll(part[up], 1, 1))
                + jnp.where(lane == DEPTH - 1, 0.0, pltpu.roll(part[down], DEPTH - 1, 1))
            )
    return outs


def forward_kernel(
    meta, features, out_grad, mask, xm, xp, ym, yp, kernel_ref, conv_out, stats, field, grads, convs, sums, sem_rim, sem_in, sem_og, sem_out
):
    occupied = meta[8]
    rims = rim_copies((xm, xp, ym, yp), field, sem_rim)
    for copy in rims:
        copy.start()
    loads = []
    for slot in range(SLOTS):
        x0, y0 = corner(meta, slot)
        loads.append(
            (
                pltpu.make_async_copy(
                    features.at[pl.ds(x0, BRICK), pl.ds(y0, BRICK)],
                    field.at[pl.ds(x0 + 1, BRICK), pl.ds(y0 + 1, BRICK)],
                    sem_in.at[slot],
                ),
                pltpu.make_async_copy(
                    out_grad.at[pl.ds(x0, BRICK), pl.ds(y0, BRICK)], grads.at[slot], sem_og.at[slot]
                ),
            )
        )
    for slot in range(SLOTS):

        @pl.when(slot < occupied)
        def _():
            loads[slot][0].start()

    for slot in range(SLOTS):

        @pl.when(slot < occupied)
        def _():
            loads[slot][1].start()

    zero_pillars(meta, field, 1)
    sums[...] = jnp.zeros(sums.shape, F32)
    for copy in rims:
        copy.wait()
    for slot in range(SLOTS):

        @pl.when(slot < occupied)
        def _():
            loads[slot][0].wait()
            mask_pillar(meta, slot, mask, field)

    for slot in range(SLOTS):

        @pl.when(slot < occupied)
        def _():
            x0, y0 = corner(meta, slot)
            loads[slot][1].wait()

            def row(x, carry):
                active = mask[x0 + x, pl.ds(y0, BRICK), :]
                outs = column_convs(field, kernel_ref, x0 + x, y0, False)
                total, square, upsum, cross = [sums[k] for k in range(4)]
                for col in range(BRICK):
                    keep = active[col : col + 1]
                    conv = outs[col] * keep
                    convs[slot, x, col] = conv
                    up = grads[slot, x, col].astype(F32) * keep
                    total = total + conv
                    square = square + conv * conv
                    upsum = upsum + up
                    cross = cross + up * conv
                for k, value in enumerate((total, square, upsum, cross)):
                    sums[k] = value
                sums[4, 0:BRICK] = sums[4, 0:BRICK] + active
                pltpu.make_async_copy(
                    convs.at[slot, x], conv_out.at[slot, x], sem_out.at[slot, x]
                ).start()
                return carry

            lax.fori_loop(0, BRICK, row, 0)

    ones = jnp.ones((8, DEPTH), F32)
    stats[...] = jnp.zeros(stats.shape, F32)
    for k in range(5):
        flat = lax.dot_general(
            ones,
            sums[k],
            (((1,), (1,)), ((), ())),
            precision=lax.Precision.HIGHEST,
            preferred_element_type=F32,
        )
        stats[k : k + 1, 0:CHANS] = flat[0:1]
    for slot in range(SLOTS):

        @pl.when(slot < occupied)
        def _():
            def drain(x, carry):
                pltpu.make_async_copy(
                    convs.at[slot, x], conv_out.at[slot, x], sem_out.at[slot, x]
                ).wait()
                return carry

            lax.fori_loop(0, BRICK, drain, 0)


def forward(meta, features, out_grad, mask, rims, kernel):
    return pl.pallas_call(
        forward_kernel,
        name="forward",
        out_shape=(
            jax.ShapeDtypeStruct((SLOTS, BRICK, BRICK, CHANS, DEPTH), F32),
            jax.ShapeDtypeStruct((8, DEPTH), F32),
        ),
        in_specs=[SMEM, ANY, ANY, VMEM, ANY, ANY, ANY, ANY, VMEM],
        out_specs=(ANY, VMEM),
        scratch_shapes=[
            pltpu.VMEM((18, 18, CHANS, DEPTH), BF16),
            pltpu.VMEM((SLOTS, BRICK, BRICK, CHANS, DEPTH), BF16),
            pltpu.VMEM((SLOTS, BRICK, BRICK, CHANS, DEPTH), F32),
            pltpu.VMEM((5, CHANS, DEPTH), F32),
            pltpu.SemaphoreType.DMA((4,)),
            pltpu.SemaphoreType.DMA((SLOTS,)),
            pltpu.SemaphoreType.DMA((SLOTS,)),
            pltpu.SemaphoreType.DMA((SLOTS, BRICK)),
        ],
        compiler_params=pltpu.CompilerParams(vmem_limit_bytes=VMEM_LIMIT),
        cost_estimate=pl.CostEstimate(flops=8_200_000_000, bytes_accessed=14_000_000, transcendentals=0),
    )(meta, features, out_grad, mask, *rims, kernel)


def spread(row):
    return jnp.transpose(jnp.broadcast_to(row, (DEPTH, DEPTH)))[0:CHANS]


def norm_kernel(
    meta, totals, params, conv, out_grad, mask, normed_out, dh_out, x_low, x_high, y_low, y_high, sums_out, convs, grads, ys, dense, blank, sem_conv, sem_og, sem_y, sem_dh, sem_zero, sem_rim
):
    occupied = meta[8]

    def conv_copy(slot, x):
        return pltpu.make_async_copy(conv.at[slot, x], convs.at[slot, x], sem_conv.at[slot, x])

    def og_copy(slot, x):
        x0, y0 = corner(meta, slot)
        return pltpu.make_async_copy(
            out_grad.at[x0 + x, pl.ds(y0, BRICK)], grads.at[slot, x], sem_og.at[slot, x]
        )

    def y_copy(slot, x):
        x0, y0 = corner(meta, slot)
        return pltpu.make_async_copy(
            ys.at[slot, x], normed_out.at[x0 + x, pl.ds(y0, BRICK)], sem_y.at[slot, x]
        )

    def dh_copy(slot, x):
        x0, y0 = corner(meta, slot)
        return pltpu.make_async_copy(
            dense.at[x0 + x, pl.ds(y0, BRICK)], dh_out.at[slot, x], sem_dh.at[slot, x]
        )

    for slot in range(SLOTS):

        @pl.when(slot < occupied)
        def _():
            def begin(x, carry):
                conv_copy(slot, x).start()
                og_copy(slot, x).start()
                return carry

            lax.fori_loop(0, BRICK, begin, 0)

    def clear(x, carry):
        for col in range(BRICK):
            blank[x, col] = jnp.zeros((CHANS, DEPTH), BF16)
        return carry

    lax.fori_loop(0, BRICK, clear, 0)

    def zero_copy(slot):
        x0, y0 = corner(meta, slot)
        return pltpu.make_async_copy(
            blank, normed_out.at[pl.ds(x0, BRICK), pl.ds(y0, BRICK)], sem_zero.at[slot]
        )

    for slot in range(4):

        @pl.when(slot >= occupied)
        def _():
            zero_copy(slot).start()

    zero_pillars(meta, dense, 0)

    total, square, upsum, cross = [totals[k : k + 1] for k in range(4)]
    count = jnp.sum(totals[4:5])
    gain, bias = params[0:1], params[1:2]
    mean = total / count
    inv_std = lax.rsqrt(square / count - mean * mean + EPSILON)
    gain_grad = inv_std * (cross - mean * upsum)
    sums_out[...] = jnp.zeros(sums_out.shape, F32)
    sums_out[0:1] = gain_grad
    sums_out[1:2] = upsum
    mean_c, inv_c, gain_c, bias_c = spread(mean), spread(inv_std), spread(gain), spread(bias)
    up_c, cross_c = spread(upsum / count), spread(gain_grad / count)
    scale_c = spread(gain * inv_std)

    for slot in range(SLOTS):

        @pl.when(slot < occupied)
        def _():
            x0, y0 = corner(meta, slot)

            def row(x, carry):
                conv_copy(slot, x).wait()
                og_copy(slot, x).wait()
                active = mask[x0 + x, pl.ds(y0, BRICK), :]
                for col in range(BRICK):
                    keep = active[col : col + 1]
                    normed = (convs[slot, x, col] - mean_c) * inv_c
                    ys[slot, x, col] = ((gain_c * normed + bias_c) * keep).astype(BF16)
                    up = grads[slot, x, col].astype(F32)
                    dense[x0 + x, y0 + col] = (
                        scale_c * (up - up_c - normed * cross_c) * keep
                    ).astype(BF16)
                y_copy(slot, x).start()
                dh_copy(slot, x).start()
                return carry

            lax.fori_loop(0, BRICK, row, 0)

    rims = [
        pltpu.make_async_copy(dense.at[0], x_low, sem_rim.at[0]),
        pltpu.make_async_copy(dense.at[15], x_high, sem_rim.at[1]),
        pltpu.make_async_copy(dense.at[:, 0], y_low, sem_rim.at[2]),
        pltpu.make_async_copy(dense.at[:, 15], y_high, sem_rim.at[3]),
    ]
    for copy in rims:
        copy.start()
    for copy in rims:
        copy.wait()
    for slot in range(4):

        @pl.when(slot >= occupied)
        def _():
            zero_copy(slot).wait()

    for slot in range(SLOTS):

        @pl.when(slot < occupied)
        def _():
            def drain(x, carry):
                y_copy(slot, x).wait()
                dh_copy(slot, x).wait()
                return carry

            lax.fori_loop(0, BRICK, drain, 0)


def normalize(meta, totals, params, conv, out_grad, mask):
    block = (SLOTS, BRICK, BRICK, CHANS, DEPTH)
    rim = jax.ShapeDtypeStruct((16, CHANS, DEPTH), BF16)
    return pl.pallas_call(
        norm_kernel,
        name="normalize",
        out_shape=(
            jax.ShapeDtypeStruct((16, 16, CHANS, DEPTH), BF16),
            jax.ShapeDtypeStruct(block, BF16),
            rim,
            rim,
            rim,
            rim,
            jax.ShapeDtypeStruct((8, DEPTH), F32),
        ),
        in_specs=[SMEM, VMEM, VMEM, ANY, ANY, VMEM],
        out_specs=(ANY, ANY, ANY, ANY, ANY, ANY, VMEM),
        scratch_shapes=[
            pltpu.VMEM(block, F32),
            pltpu.VMEM(block, BF16),
            pltpu.VMEM(block, BF16),
            pltpu.VMEM((16, 16, CHANS, DEPTH), BF16),
            pltpu.VMEM((BRICK, BRICK, CHANS, DEPTH), BF16),
            pltpu.SemaphoreType.DMA((SLOTS, BRICK)),
            pltpu.SemaphoreType.DMA((SLOTS, BRICK)),
            pltpu.SemaphoreType.DMA((SLOTS, BRICK)),
            pltpu.SemaphoreType.DMA((SLOTS, BRICK)),
            pltpu.SemaphoreType.DMA((4,)),
            pltpu.SemaphoreType.DMA((4,)),
        ],
        compiler_params=pltpu.CompilerParams(vmem_limit_bytes=VMEM_LIMIT),
        cost_estimate=pl.CostEstimate(flops=30_000_000, bytes_accessed=20_000_000, transcendentals=0),
    )(meta, totals, params, conv, out_grad, mask)


def weight_kernel(
    meta, features, mask, xm, xp, ym, yp, dh, out, field, grads, acc, sem_rim, sem_in, sem_dh
):
    occupied = meta[8]
    rims = rim_copies((xm, xp, ym, yp), field, sem_rim)
    for copy in rims:
        copy.start()
    loads = []
    for slot in range(SLOTS):
        x0, y0 = corner(meta, slot)
        loads.append(
            (
                pltpu.make_async_copy(
                    features.at[pl.ds(x0, BRICK), pl.ds(y0, BRICK)],
                    field.at[pl.ds(x0 + 1, BRICK), pl.ds(y0 + 1, BRICK)],
                    sem_in.at[slot],
                ),
                pltpu.make_async_copy(dh.at[slot], grads.at[slot], sem_dh.at[slot]),
            )
        )
    for slot in range(SLOTS):

        @pl.when(slot < occupied)
        def _():
            loads[slot][0].start()
            loads[slot][1].start()

    zero_pillars(meta, field, 1)
    acc[...] = jnp.zeros(acc.shape, F32)
    for copy in rims:
        copy.wait()
    for slot in range(SLOTS):

        @pl.when(slot < occupied)
        def _():
            loads[slot][0].wait()
            mask_pillar(meta, slot, mask, field)

    lane = lax.broadcasted_iota(jnp.int32, (CHANS, DEPTH), 1)
    for slot in range(SLOTS):

        @pl.when(slot < occupied)
        def _():
            x0, y0 = corner(meta, slot)
            loads[slot][1].wait()

            def row(x, carry):
                shifted = [[], [], []]
                for col in range(BRICK):
                    here = grads[slot, x, col]
                    wide = here.astype(F32)
                    shifted[0].append(
                        jnp.where(lane == DEPTH - 1, 0.0, pltpu.roll(wide, DEPTH - 1, 1)).astype(BF16)
                    )
                    shifted[1].append(here)
                    shifted[2].append(
                        jnp.where(lane == 0, 0.0, pltpu.roll(wide, 1, 1)).astype(BF16)
                    )
                left = jnp.concatenate([jnp.concatenate(s, axis=1) for s in shifted], axis=0)
                right = []
                for a in range(3):
                    for b in range(3):
                        right.append(
                            jnp.concatenate(
                                [field[x0 + x + a, y0 + b + col] for col in range(BRICK)], axis=1
                            )
                        )
                right.append(jnp.zeros((COLS - 9 * CHANS, BRICK * DEPTH), BF16))
                acc[...] += lax.dot_general(
                    left,
                    jnp.concatenate(right, axis=0),
                    (((1,), (1,)), ((), ())),
                    preferred_element_type=F32,
                )
                return carry

            lax.fori_loop(0, BRICK, row, 0)

    for tile in range(TILES):
        out[ROWS * tile : ROWS * (tile + 1)] = acc[:, DEPTH * tile : DEPTH * (tile + 1)]
    out[ROWS * TILES :] = jnp.zeros((2048 - ROWS * TILES, DEPTH), F32)


def weight_terms(meta, features, mask, rims, dh):
    return pl.pallas_call(
        weight_kernel,
        name="weight_terms",
        out_shape=jax.ShapeDtypeStruct((2048, DEPTH), F32),
        in_specs=[SMEM, ANY, VMEM, ANY, ANY, ANY, ANY, ANY],
        out_specs=VMEM,
        scratch_shapes=[
            pltpu.VMEM((18, 18, CHANS, DEPTH), BF16),
            pltpu.VMEM((SLOTS, BRICK, BRICK, CHANS, DEPTH), BF16),
            pltpu.VMEM((ROWS, COLS), F32),
            pltpu.SemaphoreType.DMA((4,)),
            pltpu.SemaphoreType.DMA((SLOTS,)),
            pltpu.SemaphoreType.DMA((SLOTS,)),
        ],
        compiler_params=pltpu.CompilerParams(vmem_limit_bytes=VMEM_LIMIT),
        cost_estimate=pl.CostEstimate(flops=8_200_000_000, bytes_accessed=8_000_000, transcendentals=0),
    )(meta, features, mask, *rims, dh)


def backward_kernel(
    meta, dh, mask, xm, xp, ym, yp, kernel_ref, out, field, results, blank, sem_rim, sem_in, sem_out, sem_zero
):
    occupied = meta[8]
    rims = rim_copies((xm, xp, ym, yp), field, sem_rim)
    for copy in rims:
        copy.start()
    loads = []
    for slot in range(SLOTS):
        x0, y0 = corner(meta, slot)
        loads.append(
            pltpu.make_async_copy(
                dh.at[slot], field.at[pl.ds(x0 + 1, BRICK), pl.ds(y0 + 1, BRICK)], sem_in.at[slot]
            )
        )
    for slot in range(SLOTS):

        @pl.when(slot < occupied)
        def _():
            loads[slot].start()

    def clear(x, carry):
        for col in range(BRICK):
            blank[x, col] = jnp.zeros((CHANS, DEPTH), BF16)
        return carry

    lax.fori_loop(0, BRICK, clear, 0)

    def zero_copy(slot):
        x0, y0 = corner(meta, slot)
        return pltpu.make_async_copy(
            blank, out.at[pl.ds(x0, BRICK), pl.ds(y0, BRICK)], sem_zero.at[slot]
        )

    for slot in range(4):

        @pl.when(slot >= occupied)
        def _():
            zero_copy(slot).start()

    zero_pillars(meta, field, 1)
    for copy in rims:
        copy.wait()
    for slot in range(SLOTS):

        @pl.when(slot < occupied)
        def _():
            loads[slot].wait()

    def out_copy(slot, x):
        x0, y0 = corner(meta, slot)
        return pltpu.make_async_copy(
            results.at[slot, x], out.at[x0 + x, pl.ds(y0, BRICK)], sem_out.at[slot, x]
        )

    for slot in range(SLOTS):

        @pl.when(slot < occupied)
        def _():
            x0, y0 = corner(meta, slot)

            def row(x, carry):
                active = mask[x0 + x, pl.ds(y0, BRICK), :]
                outs = column_convs(field, kernel_ref, x0 + x, y0, True)
                for col in range(BRICK):
                    results[slot, x, col] = (outs[col] * active[col : col + 1]).astype(BF16)
                out_copy(slot, x).start()
                return carry

            lax.fori_loop(0, BRICK, row, 0)

    for slot in range(4):

        @pl.when(slot >= occupied)
        def _():
            zero_copy(slot).wait()

    for slot in range(SLOTS):

        @pl.when(slot < occupied)
        def _():
            def drain(x, carry):
                out_copy(slot, x).wait()
                return carry

            lax.fori_loop(0, BRICK, drain, 0)


def backward(meta, dh, mask, rims, kernel):
    return pl.pallas_call(
        backward_kernel,
        name="backward",
        out_shape=jax.ShapeDtypeStruct((16, 16, CHANS, DEPTH), BF16),
        in_specs=[SMEM, ANY, VMEM, ANY, ANY, ANY, ANY, VMEM],
        out_specs=ANY,
        scratch_shapes=[
            pltpu.VMEM((18, 18, CHANS, DEPTH), BF16),
            pltpu.VMEM((SLOTS, BRICK, BRICK, CHANS, DEPTH), BF16),
            pltpu.VMEM((BRICK, BRICK, CHANS, DEPTH), BF16),
            pltpu.SemaphoreType.DMA((4,)),
            pltpu.SemaphoreType.DMA((SLOTS,)),
            pltpu.SemaphoreType.DMA((SLOTS, BRICK)),
            pltpu.SemaphoreType.DMA((4,)),
        ],
        compiler_params=pltpu.CompilerParams(vmem_limit_bytes=VMEM_LIMIT),
        cost_estimate=pl.CostEstimate(flops=8_200_000_000, bytes_accessed=14_000_000, transcendentals=0),
    )(meta, dh, mask, *rims, kernel)


def exchange(x_low, x_high, y_low, y_high):
    slabs, subs = lax.axis_size("slab"), lax.axis_size("sub")
    ahead = [(i, i + 1) for i in range(slabs - 1)]
    behind = [(i + 1, i) for i in range(slabs - 1)]
    xm = lax.ppermute(x_high, "slab", ahead)
    xp = lax.ppermute(x_low, "slab", behind)
    ahead = [(i, i + 1) for i in range(subs - 1)]
    behind = [(i + 1, i) for i in range(subs - 1)]
    first, last = slice(0, 1), slice(15, 16)
    ym = lax.ppermute(jnp.concatenate([xm[last], y_high, xp[last]]), "sub", ahead)
    yp = lax.ppermute(jnp.concatenate([xm[first], y_low, xp[first]]), "sub", behind)
    return (xm, xp, ym, yp)


def all_sum(rows):
    spread_rows = jnp.broadcast_to(rows[None], (DEVICES,) + rows.shape)
    gathered = lax.all_to_all(spread_rows, ("slab", "sub"), 0, 0, tiled=True)
    return jnp.sum(gathered, axis=0)


def all_sum_big(terms):
    pieces = terms.reshape(DEVICES, 16, DEPTH)
    mine = jnp.sum(lax.all_to_all(pieces, ("slab", "sub"), 0, 0, tiled=True), axis=0)
    copies = jnp.broadcast_to(mine[None], pieces.shape)
    return lax.all_to_all(copies, ("slab", "sub"), 0, 0, tiled=True).reshape(terms.shape)


def tap_kernels(weight):
    taps = weight.reshape(3, 3, 3, CHANS, CHANS)
    ahead = taps.transpose(2, 3, 0, 1, 4).reshape(ROWS, 9 * CHANS)
    back = taps[::-1, ::-1].transpose(2, 4, 0, 1, 3).reshape(ROWS, 9 * CHANS)
    edge = ((0, 0), (0, COLS - 9 * CHANS))
    return jnp.pad(ahead, edge), jnp.pad(back, edge)


def body(features, voxel_mask, weight, norm_gain, norm_bias, out_grad):
    mask = voxel_mask.astype(F32)
    mask_bf = voxel_mask.astype(BF16)[:, :, None, :]
    meta = slot_table(voxel_mask)
    rims = exchange(
        features[0] * mask_bf[0],
        features[15] * mask_bf[15],
        features[:, 0] * mask_bf[:, 0],
        features[:, 15] * mask_bf[:, 15],
    )
    ahead, back = tap_kernels(weight)
    conv, stats = forward(meta, features, out_grad, mask, rims, ahead)
    totals = all_sum(stats)
    params = jnp.pad(jnp.stack([norm_gain, norm_bias]), ((0, 6), (0, DEPTH - CHANS)))
    normed_out, dh, x_low, x_high, y_low, y_high, sums = normalize(
        meta, totals, params, conv, out_grad, mask
    )
    grad_rims = exchange(x_low, x_high, y_low, y_high)
    terms = weight_terms(meta, features, mask, rims, dh)
    feature_grad = backward(meta, dh, mask, grad_rims, back)
    summed = all_sum_big(terms)
    flat = summed[: ROWS * TILES].reshape(TILES, 3, CHANS, DEPTH).transpose(1, 2, 0, 3)
    flat = flat.reshape(3, CHANS, COLS)[:, :, : 9 * CHANS].reshape(3, CHANS, 9, CHANS)
    weight_grad = flat.transpose(2, 0, 1, 3).reshape(27, CHANS, CHANS)
    return (normed_out, feature_grad, weight_grad, sums[0, :CHANS], sums[1, :CHANS])


def solution(mesh):
    placed = (
        P("slab", "sub", None, None),
        P("slab", "sub", None),
        P(),
        P(),
        P(),
        P("slab", "sub", None, None),
    )
    return jax.shard_map(
        body,
        mesh=mesh,
        in_specs=placed,
        out_specs=(P("slab", "sub", None, None), P("slab", "sub", None, None), P(), P(), P()),
        check_vma=False,
    )
```

time: 771 us -> 181 us (0.23)
  the two profiles are of different devices: /device:TPU:14 before, /device:TPU:3 now
where the time goes in v1:
time: 181 us
  Pallas kernels  68.2 us (38%)
  starting transfers between devices  49.6 us (27%)
  waiting for transfers between devices  35.7 us (20%)
  local copies, waits for them, and re-layouts  16.4 us (9%)
  other arithmetic  9.69 us (5%)
    ppermute x2, waiting for transfers between devices, exchange(): xp = lax.ppermute(x_low, 'slab', behind)  20.9 us
    pallas_call x1, Pallas kernels, forward(): pl.pallas_call(forward_kernel, name='forward', out_shape=(jax.ShapeDtypeS...  20 us
    pallas_call x1, Pallas kernels, backward(): pl.pallas_call(backward_kernel, name='backward', out_shape=jax.ShapeDtype...  19.6 us
    pallas_call x1, Pallas kernels, weight_terms(): pl.pallas_call(weight_kernel, name='weight_terms', out_shape=jax.ShapeDty...  18.6 us
    all_to_all x1, starting transfers between devices, all_sum(): gathered = lax.all_to_all(spread_rows, ('slab', 'sub'), 0, 0, tiled=True)  14.5 us
    all_to_all x1, waiting for transfers between devices, all_sum(): gathered = lax.all_to_all(spread_rows, ('slab', 'sub'), 0, 0, tiled=True)  12.4 us
    pallas_call x1, Pallas kernels, normalize(): pl.pallas_call(norm_kernel, name='normalize', out_shape=(jax.ShapeDtypeSt...  10.1 us
    all_to_all x1, starting transfers between devices, all_sum_big(): lax.all_to_all(copies, ('slab', 'sub'), 0, 0, tiled=True)  8.66 us
  transfers between devices with their start and end apart: 11, of which 5 were waited for; matrix products, arithmetic and copies ran while one was open for 10% of the time, Pallas kernels for 21%

profile of v1, /device:TPU:3, one launch (start us, length us, event | category | flops | bytes accessed | tf_op | source)
XLA Modules:
  0.0 180.6 jit_solution(2198709157249985154)
XLA Ops:
  0.6 2.0 %fusion.6 = (bf16[16,16,128]{2,1,0:T(8,128)(2,1)S(1)}, s32[16,16]{1,0:T(8,128)S(1)}, f32[16,16,128]{2,1,0:T(8,128)}) fusion(s32[16,16,128]{2,1,0:T(8,128)} %param.7), kind=kLoop, calls=%fused_computation.36 | loop fusion | flops 98048 | bytes 328704 | tf_op jit(solution)/shard_map/convert_element_type | solution.py:651
  2.7 1.5 bitcast_multiply_fusion
  4.1 4.1 %collective-permute-start = (bf16[16,96,128]{2,1,0:T(8,128)(2,1)S(1)}, bf16[16,96,128]{2,1,0:T(8,128)(2,1)S(1)}, u32[]{:S(2)}, u32[]{:S(2)}) collective-permute-start(bf16[16,96,128]{2,1,0:T(8,128)(2,1)S(1)} %get-tuple-element.26), channel_id=1, source_target_pairs={{0,4},{4,8},{8,12},{12,16},{16,20},{20,24},{24,28},{28,32},{32,36}... | collective-permute-start | bytes 1179656 | tf_op jit(solution)/shard_map/ppermute | solution.py:618
  8.3 1.9 %collective-permute-start.1 = (bf16[16,96,128]{2,1,0:T(8,128)(2,1)S(1)}, bf16[16,96,128]{2,1,0:T(8,128)(2,1)S(1)}, u32[]{:S(2)}, u32[]{:S(2)}) collective-permute-start(bf16[16,96,128]{2,1,0:T(8,128)(2,1)S(1)} %get-tuple-element.25), channel_id=1, source_target_pairs={{4,0},{8,4},{12,8},{16,12},{20,16},{24,20},{28,24},{32,28},{36,32}... | collective-permute-start | bytes 1179656 | tf_op jit(solution)/shard_map/ppermute | solution.py:619
  10.2 0.1 reduce_max.14
  10.3 0.1 reduce_max.18
  10.4 0.1 reshape.176
  10.5 0.1 reshape.175
  10.6 0.6 reduce_sum.38
  11.2 0.2 reduce-window.8
  11.4 0.6 compare_select_fusion
  12.0 0.1 select_reduce_fusion
  12.2 0.8 collective-permute-done.xm
  13.0 4.8 %collective-permute-done.1.xp = bf16[16,96,128]{2,1,0:T(8,128)(2,1)S(1)} collective-permute-done((bf16[16,96,128]{2,1,0:T(8,128)(2,1)S(1)}, bf16[16,96,128]{2,1,0:T(8,128)(2,1)S(1)}, u32[]{:S(2)}, u32[]{:S(2)}) %collective-permute-start.1) | collective-permute-done | bytes 393248 | tf_op jit(solution)/shard_map/ppermute | solution.py:619
  17.8 0.1 pad_maximum_fusion.1
  17.8 2.2 %collective-permute-start.3 = (bf16[18,96,128]{2,1,0:T(8,128)(2,1)S(1)}, bf16[18,96,128]{2,1,0:T(8,128)(2,1)}, u32[]{:S(2)}, u32[]{:S(2)}) collective-permute-start(bf16[18,96,128]{2,1,0:T(8,128)(2,1)S(1)} %pad_maximum_fusion.1), channel_id=1, source_target_pairs={{1,0},{2,1},{3,2},{5,4},{6,5},{7,6},{9,8},{10,9},{11,10},{13,12},{... | collective-permute-start | bytes 1327112 | tf_op jit(solution)/shard_map/ppermute | solution.py:624
  20.0 0.1 pad_maximum_fusion
  20.1 3.1 %collective-permute-start.2 = (bf16[18,96,128]{2,1,0:T(8,128)(2,1)S(1)}, bf16[18,96,128]{2,1,0:T(8,128)(2,1)}, u32[]{:S(2)}, u32[]{:S(2)}) collective-permute-start(bf16[18,96,128]{2,1,0:T(8,128)(2,1)S(1)} %pad_maximum_fusion), channel_id=1, source_target_pairs={{0,1},{1,2},{2,3},{4,5},{5,6},{6,7},{8,9},{9,10},{10,11},{12,13},{... | collective-permute-start | bytes 1327112 | tf_op jit(solution)/shard_map/ppermute | solution.py:623
  23.2 0.1 copy.40
  23.3 0.1 reshape.178
  23.4 1.5 copy.60
  25.0 0.6 reshape.180
  25.6 0.8 pad.11.kernel_ref
  26.4 1.2 pad_add_fusion.1.meta
  27.6 0.0 collective-permute-done.3.yp
  27.6 1.6 collective-permute-done.2.ym
  29.2 20.0 %forward.1 = (f32[2,8,8,96,128]{4,3,2,1,0:T(8,128)}, f32[8,128]{1,0:T(8,128)}) custom-call(s32[9]{0:T(128)} %pad_add_fusion.1.meta, bf16[16,16,96,128]{3,2,1,0:T(8,128)(2,1)} %features.3, bf16[16,16,96,128]{3,2,1,0:T(8,128)(2,1)} %out_grad.3, f32[16,16,128]{2,1,0:T(8,128)} %get-tuple-element.37.mask, bf16[16,96,128]{2,1,0:T(8,128)(2,1)} %copy-done.3, ...), custom_call_target="tpu_custom_call" | custom-call | flops 8200000000 | bytes 14000000 | tf_op jit(solution)/shard_map/forward/pallas_call | solution.py:216
  49.2 1.5 broadcast_in_dim.37
  50.7 14.5 %all-to-all-start = ((f32[128,8,128]{2,1,0:T(8,128)}), f32[128,8,128]{2,1,0:T(8,128)S(1)}, u32[]{:S(2)}, u32[]{:S(2)}) async-start(f32[128,8,128]{2,1,0:T(8,128)} %broadcast_in_dim.37), calls=%async_computation | async-start | bytes 1048576 | tf_op jit(solution)/shard_map/all_to_all | solution.py:630
  65.2 0.6 select_maximum_fusion.params
  65.8 12.4 %all-to-all-done = f32[128,8,128]{2,1,0:T(8,128)S(1)} async-done(((f32[128,8,128]{2,1,0:T(8,128)}), f32[128,8,128]{2,1,0:T(8,128)S(1)}, u32[]{:S(2)}, u32[]{:S(2)}) %all-to-all-start) | async-done | bytes 524320 | tf_op jit(solution)/shard_map/all_to_all | solution.py:630
  78.3 0.7 reduce_sum.41.totals
  79.0 10.1 %normalize.1 = (bf16[16,16,96,128]{3,2,1,0:T(8,128)(2,1)}, bf16[2,8,8,96,128]{4,3,2,1,0:T(8,128)(2,1)}, bf16[16,96,128]{2,1,0:T(8,128)(2,1)}, bf16[16,96,128]{2,...) custom-call(s32[9]{0:T(128)} %pad_add_fusion.1.meta, ...), custom_call_target="tpu_custom_call" | custom-call | flops 30000000 | bytes 20000000 | tf_op jit(solution)/shard_map/normalize/pallas_call | solution.py:370
  89.1 1.9 %collective-permute-start.4 = (bf16[16,96,128]{2,1,0:T(8,128)(2,1)}, bf16[16,96,128]{2,1,0:T(8,128)(2,1)S(1)}, u32[]{:S(2)}, u32[]{:S(2)}) collective-permute-start(bf16[16,96,128]{2,1,0:T(8,128)(2,1)} %get-tuple-element.18), channel_id=1, source_target_pairs={{0,4},{4,8},{8,12},{12,16},{16,20},{20,24},{24,28},{28,32},{32,36}... | collective-permute-start | bytes 1179656 | tf_op jit(solution)/shard_map/ppermute | solution.py:618
  91.0 18.6 %weight_terms.1 = f32[2048,128]{1,0:T(8,128)} custom-call(s32[9]{0:T(128)} %pad_add_fusion.1.meta, bf16[16,16,96,128]{3,2,1,0:T(8,128)(2,1)} %features.3, f32[16,16,128]{2,1,0:T(8,128)} %get-tuple-element.37.mask, bf16[16,96,128]{2,1,0:T(8,128)(2,1)} %copy-done.3, bf16[16,96,128]{2,1,0:T(8,128)(2,1)} %copy-done.4, ...), custom_call_target="tpu_custom_call" | custom-call | flops 8200000000 | bytes 8000000 | tf_op jit(solution)/shard_map/weight_terms/pallas_call | solution.py:486
  109.6 0.0 copy-start
  109.6 5.6 %all-to-all-start.1 = ((f32[128,16,128]{2,1,0:T(8,128)}), f32[128,16,128]{2,1,0:T(8,128)S(1)}, u32[]{:S(2)}, u32[]{:S(2)}) async-start(f32[128,16,128]{2,1,0:T(8,128)} %bitcast.73), calls=%async_computation.1 | async-start | bytes 2097152 | tf_op jit(solution)/shard_map/all_to_all | solution.py:636
  115.3 2.3 %collective-permute-start.5 = (bf16[16,96,128]{2,1,0:T(8,128)(2,1)S(1)}, bf16[16,96,128]{2,1,0:T(8,128)(2,1)S(1)}, u32[]{:S(2)}, u32[]{:S(2)}) collective-permute-start(bf16[16,96,128]{2,1,0:T(8,128)(2,1)S(1)} %copy-done.9), channel_id=1, source_target_pairs={{4,0},{8,4},{12,8},{16,12},{20,16},{24,20},{28,24},{32,28},{36,32}... | collective-permute-start | bytes 1179656 | tf_op jit(solution)/shard_map/ppermute | solution.py:619
  117.6 0.0 collective-permute-done.4.xm
  117.6 0.0 copy-start.5
  117.6 16.1 %collective-permute-done.5.xp = bf16[16,96,128]{2,1,0:T(8,128)(2,1)S(1)} collective-permute-done((bf16[16,96,128]{2,1,0:T(8,128)(2,1)S(1)}, bf16[16,96,128]{2,1,0:T(8,128)(2,1)S(1)}, u32[]{:S(2)}, u32[]{:S(2)}) %collective-permute-start.5) | collective-permute-done | bytes 393248 | tf_op jit(solution)/shard_map/ppermute | solution.py:619
  133.7 0.7 copy-done.6
  134.5 0.8 pad_maximum_fusion.3
  135.3 2.4 %collective-permute-start.7 = (bf16[18,96,128]{2,1,0:T(8,128)(2,1)}, bf16[18,96,128]{2,1,0:T(8,128)(2,1)}, u32[]{:S(2)}, u32[]{:S(2)}) collective-permute-start(bf16[18,96,128]{2,1,0:T(8,128)(2,1)} %pad_maximum_fusion.3), channel_id=1, source_target_pairs={{1,0},{2,1},{3,2},{5,4},{6,5},{7,6},{9,8},{10,9},{11,10},{13,12},{... | collective-permute-start | bytes 1327112 | tf_op jit(solution)/shard_map/ppermute | solution.py:624
  137.7 0.0 copy-done.1
  137.7 0.8 pad_maximum_fusion.2
  138.5 2.9 %collective-permute-start.6 = (bf16[18,96,128]{2,1,0:T(8,128)(2,1)}, bf16[18,96,128]{2,1,0:T(8,128)(2,1)}, u32[]{:S(2)}, u32[]{:S(2)}) collective-permute-start(bf16[18,96,128]{2,1,0:T(8,128)(2,1)} %pad_maximum_fusion.2), channel_id=1, source_target_pairs={{0,1},{1,2},{2,3},{4,5},{5,6},{6,7},{8,9},{9,10},{10,11},{12,13},{... | collective-permute-start | bytes 1327112 | tf_op jit(solution)/shard_map/ppermute | solution.py:623
  141.4 0.0 all-to-all-done.1
  141.4 0.1 reduce_sum.42
  141.6 1.0 broadcast_in_dim.38
  142.6 8.7 %all-to-all-start.2 = ((f32[128,16,128]{2,1,0:T(8,128)}), f32[128,16,128]{2,1,0:T(8,128)S(1)}, u32[]{:S(2)}, u32[]{:S(2)}) async-start(f32[128,16,128]{2,1,0:T(8,128)} %broadcast_in_dim.38), calls=%async_computation.2 | async-start | bytes 2097152 | tf_op jit(solution)/shard_map/all_to_all | solution.py:638
  151.3 0.7 copy.44
  152.0 4.2 %rev.3 = bf16[3,3,3,96,96]{3,1,0,4,2:T(4,128)(2,1)S(1)} reverse(bf16[3,3,3,96,96]{3,1,0,4,2:T(4,128)(2,1)S(1)} %copy.44), dimensions={0,1} | reverse | bytes 995328 | tf_op jit(solution)/shard_map/rev | solution.py:644
  156.2 0.6 reshape.181
  156.8 0.9 pad.13.kernel_ref
  157.6 1.3 slice_bitcast_fusion.2
  158.9 0.0 collective-permute-done.7.yp
  158.9 0.0 collective-permute-done.6.ym
  158.9 19.6 %backward.1 = bf16[16,16,96,128]{3,2,1,0:T(8,128)(2,1)} custom-call(s32[9]{0:T(128)} %pad_add_fusion.1.meta, bf16[2,8,8,96,128]{4,3,2,1,0:T(8,128)(2,1)} %get-tuple-element.17.dh, f32[16,16,128]{2,1,0:T(8,128)} %get-tuple-element.37.mask, bf16[16,96,128]{2,1,0:T(8,128)(2,1)} %copy-done.5, bf16[16,96,128]{2,1,0:T(8,128)(2,1)} %copy-done.6, ...), custom_call_target="tpu_custom_call" | custom-call | flops 8200000000 | bytes 14000000 | tf_op jit(solution)/shard_map/backward/pallas_call | solution.py:594
  178.5 0.0 all-to-all-done.2
  178.5 0.1 slice.95
  178.6 0.1 copy.59
  178.7 0.4 copy.46
  179.1 1.5 copy.47
  (25 shorter events, 0.1 us)
Async XLA Ops:
  4.1 8.8 %collective-permute-start = (bf16[16,96,128]{2,1,0:T(8,128)(2,1)S(1)}, bf16[16,96,128]{2,1,0:T(8,128)(2,1)S(1)}, u32[]{:S(2)}, u32[]{:S(2)}) collective-permute-start(bf16[16,96,128]{2,1,0:T(8,128)(2,1)S(1)} %get-tuple-element.26), channel_id=1, source_target_pairs={{0,4},{4,8},{8,12},{12,16},{16,20},{20,24},{24,28},{28,32},{32,36}... | collective-permute-start | bytes 1179656 | tf_op jit(solution)/shard_map/ppermute | solution.py:618
  8.3 9.5 %collective-permute-start.1 = (bf16[16,96,128]{2,1,0:T(8,128)(2,1)S(1)}, bf16[16,96,128]{2,1,0:T(8,128)(2,1)S(1)}, u32[]{:S(2)}, u32[]{:S(2)}) collective-permute-start(bf16[16,96,128]{2,1,0:T(8,128)(2,1)S(1)} %get-tuple-element.25), channel_id=1, source_target_pairs={{4,0},{8,4},{12,8},{16,12},{20,16},{24,20},{28,24},{32,28},{36,32}... | collective-permute-start | bytes 1179656 | tf_op jit(solution)/shard_map/ppermute | solution.py:619
  13.0 16.3 %copy-start.3 = (bf16[16,96,128]{2,1,0:T(8,128)(2,1)}, bf16[16,96,128]{2,1,0:T(8,128)(2,1)S(1)}, u32[]{:S(2)}) copy-start(bf16[16,96,128]{2,1,0:T(8,128)(2,1)S(1)} %collective-permute-done.xm) | copy-start | bytes 1179652
  17.8 11.5 %copy-start.4 = (bf16[16,96,128]{2,1,0:T(8,128)(2,1)}, bf16[16,96,128]{2,1,0:T(8,128)(2,1)S(1)}, u32[]{:S(2)}) copy-start(bf16[16,96,128]{2,1,0:T(8,128)(2,1)S(1)} %collective-permute-done.1.xp) | copy-start | bytes 1179652
  17.8 9.8 %collective-permute-start.3 = (bf16[18,96,128]{2,1,0:T(8,128)(2,1)S(1)}, bf16[18,96,128]{2,1,0:T(8,128)(2,1)}, u32[]{:S(2)}, u32[]{:S(2)}) collective-permute-start(bf16[18,96,128]{2,1,0:T(8,128)(2,1)S(1)} %pad_maximum_fusion.1), channel_id=1, source_target_pairs={{1,0},{2,1},{3,2},{5,4},{6,5},{7,6},{9,8},{10,9},{11,10},{13,12},{... | collective-permute-start | bytes 1327112 | tf_op jit(solution)/shard_map/ppermute | solution.py:624
  20.1 9.2 %collective-permute-start.2 = (bf16[18,96,128]{2,1,0:T(8,128)(2,1)S(1)}, bf16[18,96,128]{2,1,0:T(8,128)(2,1)}, u32[]{:S(2)}, u32[]{:S(2)}) collective-permute-start(bf16[18,96,128]{2,1,0:T(8,128)(2,1)S(1)} %pad_maximum_fusion), channel_id=1, source_target_pairs={{0,1},{1,2},{2,3},{4,5},{5,6},{6,7},{8,9},{9,10},{10,11},{12,13},{... | collective-permute-start | bytes 1327112 | tf_op jit(solution)/shard_map/ppermute | solution.py:623
  29.2 36.0 %copy-start.7 = (f32[96]{0:T(128)S(1)}, f32[96]{0:T(128)}, u32[]{:S(2)}) copy-start(f32[96]{0:T(128)} %param.10) | copy-start | bytes 1156
  29.2 36.0 %copy-start.8 = (f32[96]{0:T(128)S(1)}, f32[96]{0:T(128)}, u32[]{:S(2)}) copy-start(f32[96]{0:T(128)} %param.9) | copy-start | bytes 1156
  50.7 27.5 %all-to-all-start = ((f32[128,8,128]{2,1,0:T(8,128)}), f32[128,8,128]{2,1,0:T(8,128)S(1)}, u32[]{:S(2)}, u32[]{:S(2)}) async-start(f32[128,8,128]{2,1,0:T(8,128)} %broadcast_in_dim.37), calls=%async_computation | async-start | bytes 1048576 | tf_op jit(solution)/shard_map/all_to_all | solution.py:630
  89.1 28.5 %collective-permute-start.4 = (bf16[16,96,128]{2,1,0:T(8,128)(2,1)}, bf16[16,96,128]{2,1,0:T(8,128)(2,1)S(1)}, u32[]{:S(2)}, u32[]{:S(2)}) collective-permute-start(bf16[16,96,128]{2,1,0:T(8,128)(2,1)} %get-tuple-element.18), channel_id=1, source_target_pairs={{0,4},{4,8},{8,12},{12,16},{16,20},{20,24},{24,28},{28,32},{32,36}... | collective-permute-start | bytes 1179656 | tf_op jit(solution)/shard_map/ppermute | solution.py:618
  91.0 24.3 %copy-start.9 = (bf16[16,96,128]{2,1,0:T(8,128)(2,1)S(1)}, bf16[16,96,128]{2,1,0:T(8,128)(2,1)}, u32[]{:S(2)}) copy-start(bf16[16,96,128]{2,1,0:T(8,128)(2,1)} %get-tuple-element.19) | copy-start | bytes 1179652
  91.0 43.5 %copy-start.2 = (bf16[16,96,128]{2,1,0:T(8,128)(2,1)S(1)}, bf16[16,96,128]{2,1,0:T(8,128)(2,1)}, u32[]{:S(2)}) copy-start(bf16[16,96,128]{2,1,0:T(8,128)(2,1)} %get-tuple-element.21) | copy-start | bytes 1179652
  91.0 46.7 %copy-start.1 = (bf16[16,96,128]{2,1,0:T(8,128)(2,1)S(1)}, bf16[16,96,128]{2,1,0:T(8,128)(2,1)}, u32[]{:S(2)}) copy-start(bf16[16,96,128]{2,1,0:T(8,128)(2,1)} %get-tuple-element.20) | copy-start | bytes 1179652
  109.6 41.7 %copy-start = (bf16[27,96,96]{2,1,0:T(8,128)(2,1)S(1)}, bf16[27,96,96]{2,1,0:T(8,128)(2,1)}, u32[]{:S(2)}) copy-start(bf16[27,96,96]{2,1,0:T(8,128)(2,1)} %param.8) | copy-start | bytes 1492996
  109.6 31.8 %all-to-all-start.1 = ((f32[128,16,128]{2,1,0:T(8,128)}), f32[128,16,128]{2,1,0:T(8,128)S(1)}, u32[]{:S(2)}, u32[]{:S(2)}) async-start(f32[128,16,128]{2,1,0:T(8,128)} %bitcast.73), calls=%async_computation.1 | async-start | bytes 2097152 | tf_op jit(solution)/shard_map/all_to_all | solution.py:636
  115.3 18.4 %collective-permute-start.5 = (bf16[16,96,128]{2,1,0:T(8,128)(2,1)S(1)}, bf16[16,96,128]{2,1,0:T(8,128)(2,1)S(1)}, u32[]{:S(2)}, u32[]{:S(2)}) collective-permute-start(bf16[16,96,128]{2,1,0:T(8,128)(2,1)S(1)} %copy-done.9), channel_id=1, source_target_pairs={{4,0},{8,4},{12,8},{16,12},{20,16},{24,20},{28,24},{32,28},{36,32}... | collective-permute-start | bytes 1179656 | tf_op jit(solution)/shard_map/ppermute | solution.py:619
  117.6 25.0 %copy-start.5 = (bf16[16,96,128]{2,1,0:T(8,128)(2,1)}, bf16[16,96,128]{2,1,0:T(8,128)(2,1)S(1)}, u32[]{:S(2)}) copy-start(bf16[16,96,128]{2,1,0:T(8,128)(2,1)S(1)} %collective-permute-done.4.xm) | copy-start | bytes 1179652
  133.7 0.7 copy-start.6
  135.3 23.6 %collective-permute-start.7 = (bf16[18,96,128]{2,1,0:T(8,128)(2,1)}, bf16[18,96,128]{2,1,0:T(8,128)(2,1)}, u32[]{:S(2)}, u32[]{:S(2)}) collective-permute-start(bf16[18,96,128]{2,1,0:T(8,128)(2,1)} %pad_maximum_fusion.3), channel_id=1, source_target_pairs={{1,0},{2,1},{3,2},{5,4},{6,5},{7,6},{9,8},{10,9},{11,10},{13,12},{... | collective-permute-start | bytes 1327112 | tf_op jit(solution)/shard_map/ppermute | solution.py:624
  138.5 20.3 %collective-permute-start.6 = (bf16[18,96,128]{2,1,0:T(8,128)(2,1)}, bf16[18,96,128]{2,1,0:T(8,128)(2,1)}, u32[]{:S(2)}, u32[]{:S(2)}) collective-permute-start(bf16[18,96,128]{2,1,0:T(8,128)(2,1)} %pad_maximum_fusion.2), channel_id=1, source_target_pairs={{0,1},{1,2},{2,3},{4,5},{5,6},{6,7},{8,9},{9,10},{10,11},{12,13},{... | collective-permute-start | bytes 1327112 | tf_op jit(solution)/shard_map/ppermute | solution.py:623
  142.6 35.9 %all-to-all-start.2 = ((f32[128,16,128]{2,1,0:T(8,128)}), f32[128,16,128]{2,1,0:T(8,128)S(1)}, u32[]{:S(2)}, u32[]{:S(2)}) async-start(f32[128,16,128]{2,1,0:T(8,128)} %broadcast_in_dim.38), calls=%async_computation.2 | async-start | bytes 2097152 | tf_op jit(solution)/shard_map/all_to_all | solution.py:638

commit v2 on v0

v2 whole, which is shorter than its diff:
```python
import functools

import jax
import jax.numpy as jnp
from jax import lax
from jax.experimental import pallas as pl
from jax.experimental.pallas import tpu as pltpu
from jax.sharding import PartitionSpec as P

BRICK = 8
SLOTS = 2
EPSILON = 1e-05
DEVICES = 128
CHANS = 96
DEPTH = 128
TILES = 7
ROWS = 3 * CHANS
COLS = TILES * DEPTH
F32 = jnp.float32
BF16 = jnp.bfloat16
FIELD = (18, 18, CHANS, DEPTH)
BLOCKS = (SLOTS, BRICK, BRICK, CHANS, DEPTH)
MIB = 1024 * 1024
WIDE_CONVS = (24,) + BLOCKS[1:]
WIDE_SLOPES = (48,) + BLOCKS[1:]

ANY = pl.BlockSpec(memory_space=pl.ANY)
VMEM = pl.BlockSpec(memory_space=pltpu.VMEM)
SMEM = pl.BlockSpec(memory_space=pltpu.SMEM)
HBM = pl.BlockSpec(memory_space=pltpu.HBM)


def params_of(mib, **more):
    return pltpu.CompilerParams(vmem_limit_bytes=mib * MIB, **more)


def cost(flops, moved):
    return pl.CostEstimate(flops=flops, bytes_accessed=moved, transcendentals=0)


def corner(meta, slot):
    return (pl.multiple_of(meta[2 * slot], BRICK), pl.multiple_of(meta[2 * slot + 1], BRICK))


def active_rows(mask, x, y0):
    return mask[x, pl.ds(y0, BRICK), :].astype(F32)


def each_row(occupied, step):
    for slot in range(SLOTS):

        @pl.when(slot < occupied)
        def _():
            lax.fori_loop(0, BRICK, lambda x, carry: (step(slot, x), carry)[1], 0)


def clear_pillars(meta, field):
    for slot in range(4):

        @pl.when(slot >= meta[8])
        def _():
            x0, y0 = corner(meta, slot)

            def clear(row, carry):
                for col in range(BRICK):
                    field[x0 + row + 1, y0 + col + 1] = jnp.zeros((CHANS, DEPTH), BF16)
                return carry

            lax.fori_loop(0, BRICK, clear, 0)


def fill_rims(field, rims, sems):
    xm, xp, ym, yp = rims
    copies = [
        pltpu.make_async_copy(xm, field.at[0, pl.ds(1, 16)], sems.at[0]),
        pltpu.make_async_copy(xp, field.at[17, pl.ds(1, 16)], sems.at[1]),
        pltpu.make_async_copy(ym, field.at[:, 0], sems.at[2]),
        pltpu.make_async_copy(yp, field.at[:, 17], sems.at[3]),
    ]
    for copy in copies:
        copy.start()
    return copies


def take_rims(field, rims, sems):
    inner = pl.ds(1, 16)
    copies = [
        pltpu.make_async_copy(field.at[1, inner], rims[0], sems.at[0]),
        pltpu.make_async_copy(field.at[16, inner], rims[1], sems.at[1]),
        pltpu.make_async_copy(field.at[inner, 1], rims[2].at[inner], sems.at[2]),
        pltpu.make_async_copy(field.at[inner, 16], rims[3].at[inner], sems.at[3]),
    ]
    for copy in copies:
        copy.start()
    for copy in copies:
        copy.wait()


RIM = jax.ShapeDtypeStruct((16, CHANS, DEPTH), BF16)
LONG = jax.ShapeDtypeStruct((18, CHANS, DEPTH), BF16)


def prepare_kernel(features, mask, x_low, x_high, y_low, y_high, meta, faces, sides, sem_in, sem_out):
    loads = [
        pltpu.make_async_copy(features.at[0], faces.at[0], sem_in.at[0]),
        pltpu.make_async_copy(features.at[15], faces.at[1], sem_in.at[1]),
        pltpu.make_async_copy(features.at[:, 0], sides.at[0], sem_in.at[2]),
        pltpu.make_async_copy(features.at[:, 15], sides.at[1], sem_in.at[3]),
    ]
    inner = pl.ds(1, 16)
    stores = [
        pltpu.make_async_copy(faces.at[0], x_low, sem_out.at[0]),
        pltpu.make_async_copy(faces.at[1], x_high, sem_out.at[1]),
        pltpu.make_async_copy(sides.at[0], y_low.at[inner], sem_out.at[2]),
        pltpu.make_async_copy(sides.at[1], y_high.at[inner], sem_out.at[3]),
    ]
    for load in loads:
        load.start()

    flags = []
    for px in range(2):
        for py in range(2):
            cells = mask[BRICK * px : BRICK * (px + 1), BRICK * py : BRICK * (py + 1), :]
            flags.append(jnp.max(cells))
    taken = jnp.int32(0)
    for flag in flags:
        taken = taken + flag
    meta[8] = taken
    full, free = jnp.int32(0), taken
    for place, flag in enumerate(flags):
        rank = jnp.where(flag == 1, full, free)
        meta[2 * rank] = jnp.int32(place // 2 * BRICK)
        meta[2 * rank + 1] = jnp.int32(place % 2 * BRICK)
        full = full + flag
        free = free + 1 - flag

    for which in range(2):
        loads[which].wait()
        for col in range(16):
            keep = jnp.broadcast_to(mask[15 * which, col : col + 1, :], (CHANS, DEPTH))
            faces[which, col] = faces[which, col] * keep.astype(F32).astype(BF16)
        stores[which].start()
    for which in range(2):
        loads[2 + which].wait()
        for row in range(16):
            keep = jnp.broadcast_to(mask[row, 15 * which : 15 * which + 1, :], (CHANS, DEPTH))
            sides[which, row] = sides[which, row] * keep.astype(F32).astype(BF16)
        stores[2 + which].start()
    for store in stores:
        store.wait()


def prepare(features, voxel_mask):
    return pl.pallas_call(
        prepare_kernel,
        name="prepare",
        out_shape=(RIM, RIM, LONG, LONG, jax.ShapeDtypeStruct((9,), jnp.int32)),
        in_specs=[HBM, VMEM],
        out_specs=(ANY, ANY, ANY, ANY, SMEM),
        scratch_shapes=[
            pltpu.VMEM((2, 16, CHANS, DEPTH), BF16),
            pltpu.VMEM((2, 16, CHANS, DEPTH), BF16),
            pltpu.SemaphoreType.DMA((4,)),
            pltpu.SemaphoreType.DMA((4,)),
        ],
        compiler_params=params_of(54),
        cost_estimate=cost(3_000_000, 3_000_000),
    )(features, voxel_mask)


def build_kernel(meta, features, mask, *refs):
    *rims, field, sem_rim = refs
    copies = fill_rims(field, rims, sem_rim) if rims else []

    def mask_row(slot, x):
        x0, y0 = corner(meta, slot)
        active = active_rows(mask, x0 + x, y0)
        for col in range(BRICK):
            keep = jnp.broadcast_to(active[col : col + 1], (CHANS, DEPTH)).astype(BF16)
            field[x0 + x + 1, y0 + col + 1] = features[x0 + x, y0 + col] * keep

    clear_pillars(meta, field)
    each_row(meta[8], mask_row)
    for copy in copies:
        copy.wait()


def build(meta, features, voxel_mask, rims=()):
    return pl.pallas_call(
        build_kernel,
        name="build_whole" if rims else "build",
        out_shape=jax.ShapeDtypeStruct(FIELD, BF16),
        in_specs=[SMEM, VMEM, VMEM] + [ANY] * len(rims),
        out_specs=VMEM,
        scratch_shapes=[pltpu.SemaphoreType.DMA((4,))],
        compiler_params=params_of(2),
        cost_estimate=cost(3_000_000, 6_000_000),
    )(meta, features, voxel_mask, *rims)


def column_convs(field, kernel_ref, x, y0, flipped):
    lane = lax.broadcasted_iota(jnp.int32, (CHANS, DEPTH), 1)
    up, down = (2, 0) if flipped else (0, 2)
    outs = []
    for pair in range(BRICK // 2):
        pieces = []
        for a in range(3):
            for b in range(3):
                col = y0 + 2 * pair + b
                pieces.append(jnp.concatenate([field[x + a, col], field[x + a, col + 1]], axis=1))
        pieces.append(jnp.zeros((COLS - 9 * CHANS, 2 * DEPTH), BF16))
        planes = jnp.dot(
            kernel_ref[...], jnp.concatenate(pieces, axis=0), preferred_element_type=F32
        )
        for half in range(2):
            part = [
                planes[CHANS * e : CHANS * (e + 1), DEPTH * half : DEPTH * (half + 1)]
                for e in range(3)
            ]
            outs.append(
                part[1]
                + jnp.where(lane == 0, 0.0, pltpu.roll(part[up], 1, 1))
                + jnp.where(lane == DEPTH - 1, 0.0, pltpu.roll(part[down], DEPTH - 1, 1))
            )
    return outs


def forward_kernel(
    meta, before, grads, mask, xm, xp, ym, yp, taps, field, conv_out, stats, convs, sums, sem_rim, sem_out
):
    def conv_copy(slot, x):
        return pltpu.make_async_copy(convs.at[slot, x], conv_out.at[slot, x], sem_out.at[slot, x])

    rims = fill_rims(field, (xm, xp, ym, yp), sem_rim)
    for copy in rims:
        copy.wait()
    sums[...] = jnp.zeros(sums.shape, F32)

    def row(slot, x):
        x0, y0 = corner(meta, slot)
        active = active_rows(mask, x0 + x, y0)
        outs = column_convs(field, taps, x0 + x, y0, False)
        total, square, upsum, cross = [sums[k] for k in range(4)]
        for col in range(BRICK):
            keep = active[col : col + 1]
            conv = outs[col] * keep
            convs[slot, x, col] = conv
            up = grads[x0 + x, y0 + col].astype(F32) * keep
            total = total + conv
            square = square + conv * conv
            upsum = upsum + up
            cross = cross + up * conv
        for k, value in enumerate((total, square, upsum, cross)):
            sums[k] = value
        sums[4, 0:BRICK] = sums[4, 0:BRICK] + active
        conv_copy(slot, x).start()

    each_row(meta[8], row)

    ones = jnp.ones((8, DEPTH), F32)
    rows = []
    for k in range(5):
        flat = lax.dot_general(
            ones,
            sums[k],
            (((1,), (1,)), ((), ())),
            precision=lax.Precision.HIGHEST,
            preferred_element_type=F32,
        )
        rows.append(flat[0:1])
    rows.append(jnp.zeros((3, CHANS), F32))
    packed = jnp.concatenate(
        [jnp.concatenate(rows, axis=0), jnp.zeros((8, DEPTH - CHANS), F32)], axis=1
    )
    stats[...] = jnp.broadcast_to(packed[None], stats.shape)
    each_row(meta[8], lambda slot, x: conv_copy(slot, x).wait())


def forward(meta, field, out_grad, voxel_mask, rims, taps):
    return pl.pallas_call(
        forward_kernel,
        name="forward",
        out_shape=(
            jax.ShapeDtypeStruct(FIELD, BF16),
            jax.ShapeDtypeStruct(WIDE_CONVS, F32),
            jax.ShapeDtypeStruct((DEVICES, 8, DEPTH), F32),
        ),
        in_specs=[SMEM, VMEM, VMEM, VMEM, ANY, ANY, ANY, ANY, VMEM],
        out_specs=(VMEM, HBM, VMEM),
        scratch_shapes=[
            pltpu.VMEM(BLOCKS, F32),
            pltpu.VMEM((5, CHANS, DEPTH), F32),
            pltpu.SemaphoreType.DMA((4,)),
            pltpu.SemaphoreType.DMA((SLOTS, BRICK)),
        ],
        input_output_aliases={1: 0},
        compiler_params=params_of(10),
        cost_estimate=cost(16_000_000_000, 4_000_000),
    )(meta, field, out_grad, voxel_mask, *rims, taps)[1:]


def spread(row):
    return jnp.transpose(jnp.broadcast_to(row, (DEPTH, DEPTH)))[0:CHANS]


def blank_kernel(meta, normed, feature, blank, sems):
    occupied = meta[8]

    def clear(x, carry):
        for col in range(BRICK):
            blank[x, col] = jnp.zeros((CHANS, DEPTH), BF16)
        return carry

    lax.fori_loop(0, BRICK, clear, 0)

    def copies(slot):
        x0, y0 = corner(meta, slot)
        spot = (pl.ds(x0, BRICK), pl.ds(y0, BRICK))
        return (
            pltpu.make_async_copy(blank, normed.at[spot], sems.at[slot, 0]),
            pltpu.make_async_copy(blank, feature.at[spot], sems.at[slot, 1]),
        )

    for slot in range(4):

        @pl.when(slot >= occupied)
        def _():
            for copy in copies(slot):
                copy.start()

    for slot in range(4):

        @pl.when(slot >= occupied)
        def _():
            for copy in copies(slot):
                copy.wait()


def blanks(meta):
    dense = jax.ShapeDtypeStruct((16, 16, CHANS, DEPTH), BF16)
    return pl.pallas_call(
        blank_kernel,
        name="blanks",
        out_shape=(dense, dense),
        in_specs=[SMEM],
        out_specs=(HBM, HBM),
        scratch_shapes=[
            pltpu.VMEM((BRICK, BRICK, CHANS, DEPTH), BF16),
            pltpu.SemaphoreType.DMA((4, 2)),
        ],
        compiler_params=params_of(3),
        cost_estimate=cost(1_000, 8_000_000),
    )(meta)


def norm_rows(totals):
    total, square, upsum, cross = [totals[k : k + 1] for k in range(4)]
    count = jnp.sum(totals[4:5])
    mean = total / count
    inv_std = lax.rsqrt(square / count - mean * mean + EPSILON)
    return count, mean, inv_std, upsum, cross


def slope_kernel(
    meta, gathered, params, conv, out_grad, mask, field, kept, x_low, x_high, y_low, y_high, sums_out, totals_out, convs, grads, sem_conv, sem_og, sem_kept, sem_rim
):
    occupied = meta[8]

    def loads(slot, x):
        x0, y0 = corner(meta, slot)
        return (
            pltpu.make_async_copy(conv.at[slot, x], convs.at[slot, x], sem_conv.at[slot, x]),
            pltpu.make_async_copy(
                out_grad.at[x0 + x, pl.ds(y0, BRICK)], grads.at[slot, x], sem_og.at[slot, x]
            ),
        )

    def begin(slot, x):
        for copy in loads(slot, x):
            copy.start()

    each_row(occupied, begin)

    def keep_row(slot, x):
        x0, y0 = corner(meta, slot)
        return pltpu.make_async_copy(
            field.at[x0 + x + 1, pl.ds(y0 + 1, BRICK)], kept.at[slot, x], sem_kept.at[slot, x]
        )

    clear_pillars(meta, field)
    totals = jnp.sum(gathered[...], axis=0)
    totals_out[...] = totals
    count, mean, inv_std, upsum, cross = norm_rows(totals)
    gain_grad = inv_std * (cross - mean * upsum)
    sums_out[...] = jnp.zeros(sums_out.shape, F32)
    sums_out[0:1] = gain_grad
    sums_out[1:2] = upsum
    mean_c, inv_c = spread(mean), spread(inv_std)
    up_c, cross_c = spread(upsum / count), spread(gain_grad / count)
    scale_c = spread(params[0:1] * inv_std)

    def row(slot, x):
        x0, y0 = corner(meta, slot)
        for copy in loads(slot, x):
            copy.wait()
        active = active_rows(mask, x0 + x, y0)
        for col in range(BRICK):
            keep = active[col : col + 1]
            normed = (convs[slot, x, col] - mean_c) * inv_c
            up = grads[slot, x, col].astype(F32)
            field[x0 + x + 1, y0 + col + 1] = (
                scale_c * (up - up_c - normed * cross_c) * keep
            ).astype(BF16)
        keep_row(slot, x).start()

    each_row(occupied, row)
    take_rims(field, (x_low, x_high, y_low, y_high), sem_rim)
    each_row(occupied, lambda slot, x: keep_row(slot, x).wait())


def slopes(meta, gathered, params, conv, out_grad, voxel_mask):
    small = jax.ShapeDtypeStruct((8, DEPTH), F32)
    kept = jax.ShapeDtypeStruct(WIDE_SLOPES, BF16)
    return pl.pallas_call(
        slope_kernel,
        name="slopes",
        out_shape=(jax.ShapeDtypeStruct(FIELD, BF16), kept, RIM, RIM, LONG, LONG, small, small),
        in_specs=[SMEM, VMEM, VMEM, HBM, HBM, VMEM],
        out_specs=(VMEM, HBM, ANY, ANY, ANY, ANY, VMEM, VMEM),
        scratch_shapes=[
            pltpu.VMEM(BLOCKS, F32),
            pltpu.VMEM(BLOCKS, BF16),
            pltpu.SemaphoreType.DMA((SLOTS, BRICK)),
            pltpu.SemaphoreType.DMA((SLOTS, BRICK)),
            pltpu.SemaphoreType.DMA((SLOTS, BRICK)),
            pltpu.SemaphoreType.DMA((4,)),
        ],
        compiler_params=params_of(46),
        cost_estimate=cost(30_000_000, 12_000_000),
    )(meta, gathered, params, conv, out_grad, voxel_mask)


def normed_kernel(meta, totals, params, conv, mask, base, out, convs, ys, sem_conv, sems):
    def load(slot, x):
        return pltpu.make_async_copy(conv.at[slot, x], convs.at[slot, x], sem_conv.at[slot, x])

    each_row(meta[8], lambda slot, x: load(slot, x).start())
    _, mean, inv_std, _, _ = norm_rows(totals)
    mean_c, inv_c = spread(mean), spread(inv_std)
    gain_c, bias_c = spread(params[0:1]), spread(params[1:2])

    def copy(slot, x):
        x0, y0 = corner(meta, slot)
        return pltpu.make_async_copy(
            ys.at[slot, x], out.at[x0 + x, pl.ds(y0, BRICK)], sems.at[slot, x]
        )

    def row(slot, x):
        x0, y0 = corner(meta, slot)
        active = active_rows(mask, x0 + x, y0)
        load(slot, x).wait()
        for col in range(BRICK):
            normed = (convs[slot, x, col] - mean_c) * inv_c
            ys[slot, x, col] = ((gain_c * normed + bias_c) * active[col : col + 1]).astype(BF16)
        copy(slot, x).start()

    each_row(meta[8], row)
    each_row(meta[8], lambda slot, x: copy(slot, x).wait())


def normed_values(meta, totals, params, convs, voxel_mask, base):
    return pl.pallas_call(
        normed_kernel,
        name="normed_values",
        out_shape=jax.ShapeDtypeStruct((16, 16, CHANS, DEPTH), BF16),
        in_specs=[SMEM, VMEM, VMEM, HBM, VMEM, HBM],
        out_specs=HBM,
        scratch_shapes=[
            pltpu.VMEM(BLOCKS, F32),
            pltpu.VMEM(BLOCKS, BF16),
            pltpu.SemaphoreType.DMA((SLOTS, BRICK)),
            pltpu.SemaphoreType.DMA((SLOTS, BRICK)),
        ],
        input_output_aliases={5: 0},
        compiler_params=params_of(12),
        cost_estimate=cost(30_000_000, 8_000_000),
    )(meta, totals, params, convs, voxel_mask, base)


def weight_kernel(meta, field, slope, out, acc):
    acc[...] = jnp.zeros(acc.shape, F32)
    lane = lax.broadcasted_iota(jnp.int32, (CHANS, DEPTH), 1)

    def row(slot, x):
        x0, y0 = corner(meta, slot)
        shifted = [[], [], []]
        for col in range(BRICK):
            here = slope[x0 + x + 1, y0 + col + 1]
            wide = here.astype(F32)
            shifted[0].append(
                jnp.where(lane == DEPTH - 1, 0.0, pltpu.roll(wide, DEPTH - 1, 1)).astype(BF16)
            )
            shifted[1].append(here)
            shifted[2].append(jnp.where(lane == 0, 0.0, pltpu.roll(wide, 1, 1)).astype(BF16))
        left = jnp.concatenate([jnp.concatenate(s, axis=1) for s in shifted], axis=0)
        right = []
        for a in range(3):
            for b in range(3):
                cols = [field[x0 + x + a, y0 + b + col] for col in range(BRICK)]
                right.append(jnp.concatenate(cols, axis=1))
        right.append(jnp.zeros((COLS - 9 * CHANS, BRICK * DEPTH), BF16))
        acc[...] += lax.dot_general(
            left,
            jnp.concatenate(right, axis=0),
            (((1,), (1,)), ((), ())),
            preferred_element_type=F32,
        )

    each_row(meta[8], row)
    for tile in range(TILES):
        out[ROWS * tile : ROWS * (tile + 1)] = acc[:, DEPTH * tile : DEPTH * (tile + 1)]
    out[ROWS * TILES :] = jnp.zeros((2048 - ROWS * TILES, DEPTH), F32)


def weight_terms(meta, field, slope):
    return pl.pallas_call(
        weight_kernel,
        name="weight_terms",
        out_shape=jax.ShapeDtypeStruct((2048, DEPTH), F32),
        in_specs=[SMEM, VMEM, VMEM],
        out_specs=VMEM,
        scratch_shapes=[pltpu.VMEM((ROWS, COLS), F32)],
        compiler_params=params_of(4),
        cost_estimate=cost(16_000_000_000, 2_000_000),
    )(meta, field, slope)


def share_kernel(parts, out):
    mine = jnp.sum(parts[...], axis=0).astype(BF16)
    out[...] = jnp.broadcast_to(mine[None], out.shape)


def share(parts):
    return pl.pallas_call(
        share_kernel,
        name="share",
        out_shape=jax.ShapeDtypeStruct((DEVICES, 16, DEPTH), BF16),
        in_specs=[VMEM],
        out_specs=VMEM,
        compiler_params=params_of(2),
        cost_estimate=cost(300_000, 1_500_000),
    )(parts)


def arrange_kernel(flat, out):
    tiles = [flat[ROWS * t : ROWS * (t + 1)].astype(F32) for t in range(TILES)]
    for plane in range(9):
        tile, shift = CHANS * plane // DEPTH, CHANS * plane % DEPTH
        both = jnp.concatenate([tiles[tile], tiles[min(tile + 1, TILES - 1)]], axis=1)
        if shift:
            both = pltpu.roll(both, 2 * DEPTH - shift, 1)
        for e in range(3):
            out[3 * plane + e] = both[CHANS * e : CHANS * (e + 1), 0:CHANS]


def arrange(flat):
    return pl.pallas_call(
        arrange_kernel,
        name="arrange",
        out_shape=jax.ShapeDtypeStruct((27, CHANS, CHANS), F32),
        in_specs=[VMEM],
        out_specs=VMEM,
        compiler_params=params_of(4),
        cost_estimate=cost(300_000, 1_500_000),
    )(flat)


def backward_kernel(
    meta, kept, mask, xm, xp, ym, yp, taps, base, out, field, results, sem_rim, sem_in, sem_out
):
    occupied = meta[8]
    for slot in range(4):
        x0, y0 = corner(meta, slot)

        if slot < SLOTS:

            @pl.when(slot < occupied)
            def _():
                pltpu.make_async_copy(
                    kept.at[slot],
                    field.at[pl.ds(x0 + 1, BRICK), pl.ds(y0 + 1, BRICK)],
                    sem_in.at[slot],
                ).start()

    rims = fill_rims(field, (xm, xp, ym, yp), sem_rim)
    clear_pillars(meta, field)
    for copy in rims:
        copy.wait()
    for slot in range(SLOTS):
        x0, y0 = corner(meta, slot)

        @pl.when(slot < occupied)
        def _():
            pltpu.make_async_copy(
                kept.at[slot],
                field.at[pl.ds(x0 + 1, BRICK), pl.ds(y0 + 1, BRICK)],
                sem_in.at[slot],
            ).wait()

    def copy(slot, x):
        x0, y0 = corner(meta, slot)
        return pltpu.make_async_copy(
            results.at[slot, x], out.at[x0 + x, pl.ds(y0, BRICK)], sem_out.at[slot, x]
        )

    def row(slot, x):
        x0, y0 = corner(meta, slot)
        active = active_rows(mask, x0 + x, y0)
        outs = column_convs(field, taps, x0 + x, y0, True)
        for col in range(BRICK):
            results[slot, x, col] = (outs[col] * active[col : col + 1]).astype(BF16)
        copy(slot, x).start()

    each_row(occupied, row)
    each_row(occupied, lambda slot, x: copy(slot, x).wait())


def backward(meta, kept, voxel_mask, rims, taps, base):
    return pl.pallas_call(
        backward_kernel,
        name="backward",
        out_shape=jax.ShapeDtypeStruct((16, 16, CHANS, DEPTH), BF16),
        in_specs=[SMEM, HBM, VMEM, ANY, ANY, ANY, ANY, VMEM, HBM],
        out_specs=HBM,
        scratch_shapes=[
            pltpu.VMEM(FIELD, BF16),
            pltpu.VMEM(BLOCKS, BF16),
            pltpu.SemaphoreType.DMA((4,)),
            pltpu.SemaphoreType.DMA((SLOTS,)),
            pltpu.SemaphoreType.DMA((SLOTS, BRICK)),
        ],
        input_output_aliases={8: 0},
        compiler_params=params_of(15),
        cost_estimate=cost(16_000_000_000, 5_000_000),
    )(meta, kept, voxel_mask, *rims, taps, base)


def stitch_kernel(high, low, xm, xp, upper, lower, sems):
    copies = [
        pltpu.make_async_copy(xm.at[15], upper.at[0], sems.at[0]),
        pltpu.make_async_copy(xp.at[15], upper.at[17], sems.at[1]),
        pltpu.make_async_copy(xm.at[0], lower.at[0], sems.at[2]),
        pltpu.make_async_copy(xp.at[0], lower.at[17], sems.at[3]),
    ]
    for copy in copies:
        copy.start()
    for copy in copies:
        copy.wait()


def stitch(high, low, xm, xp):
    return pl.pallas_call(
        stitch_kernel,
        name="stitch",
        out_shape=(LONG, LONG),
        in_specs=[ANY, ANY, ANY, ANY],
        out_specs=(ANY, ANY),
        scratch_shapes=[pltpu.SemaphoreType.DMA((4,))],
        input_output_aliases={0: 0, 1: 1},
        compiler_params=params_of(1),
        cost_estimate=cost(1_000, 200_000),
    )(high, low, xm, xp)


def taps_kernel(weight, ahead, back):
    lane = lax.broadcasted_iota(jnp.int32, (CHANS, DEPTH), 1)
    side = jnp.zeros((CHANS, DEPTH - CHANS), F32)
    wide = [jnp.concatenate([weight[t].astype(F32), side], axis=1) for t in range(27)]
    below = jnp.zeros((DEPTH - CHANS, DEPTH), F32)

    def pack(blocks):
        tiles = []
        for tile in range(TILES):
            value = jnp.zeros((CHANS, DEPTH), F32)
            for place, block in enumerate(blocks):
                start = CHANS * place - DEPTH * tile
                if start >= DEPTH or start + CHANS <= 0:
                    continue
                moved = pltpu.roll(block, start % DEPTH, 1) if start % DEPTH else block
                here = jnp.logical_and(lane >= start, lane < start + CHANS)
                value = jnp.where(here, moved, value)
            tiles.append(value)
        return jnp.concatenate(tiles, axis=1).astype(BF16)

    for e in range(3):
        rows = slice(CHANS * e, CHANS * (e + 1))
        ahead[rows] = pack([wide[3 * plane + e] for plane in range(9)])
        turned = [
            jnp.transpose(jnp.concatenate([wide[3 * plane + e], below], axis=0))[0:CHANS]
            for plane in reversed(range(9))
        ]
        back[rows] = pack(turned)


def tap_kernels(weight):
    packed = jax.ShapeDtypeStruct((ROWS, COLS), BF16)
    return pl.pallas_call(
        taps_kernel,
        name="tap_kernels",
        out_shape=(packed, packed),
        in_specs=[VMEM],
        out_specs=(VMEM, VMEM),
        compiler_params=params_of(6),
        cost_estimate=cost(1_000_000, 2_000_000),
    )(weight)


def exchange_slabs(x_low, x_high):
    slabs = lax.axis_size("slab")
    xm = lax.ppermute(x_high, "slab", [(i, i + 1) for i in range(slabs - 1)])
    xp = lax.ppermute(x_low, "slab", [(i + 1, i) for i in range(slabs - 1)])
    return xm, xp


def exchange_subs(xm, xp, y_low, y_high):
    subs = lax.axis_size("sub")
    upper, lower = stitch(y_high, y_low, xm, xp)
    ym = lax.ppermute(upper, "sub", [(i, i + 1) for i in range(subs - 1)])
    yp = lax.ppermute(lower, "sub", [(i + 1, i) for i in range(subs - 1)])
    return ym, yp


def swap_all(pieces):
    return lax.all_to_all(pieces, ("slab", "sub"), 0, 0, tiled=True)


def body(features, voxel_mask, weight, norm_gain, norm_bias, out_grad):
    x_low, x_high, y_low, y_high, meta = prepare(features, voxel_mask)
    xm, xp = exchange_slabs(x_low, x_high)
    ym, yp = exchange_subs(xm, xp, y_low, y_high)
    rims = (xm, xp, ym, yp)
    field = build(meta, features, voxel_mask)
    ahead, back = tap_kernels(weight)
    params = jnp.pad(jnp.stack([norm_gain, norm_bias]), ((0, 6), (0, DEPTH - CHANS)))
    normed_base, feature_base = blanks(meta)
    field, normed_base, feature_base, params, back = lax.optimization_barrier(
        (field, normed_base, feature_base, params, back)
    )
    conv, stats = forward(meta, field, out_grad, voxel_mask, rims, ahead)
    slope, kept, x_low, x_high, y_low, y_high, sums, totals = slopes(
        meta, swap_all(stats), params, conv, out_grad, voxel_mask
    )
    xm, xp = exchange_slabs(x_low, x_high)
    rims, x_low = lax.optimization_barrier((rims, x_low))
    field = build(meta, features, voxel_mask, rims)
    xm, xp, slope, field = lax.optimization_barrier((xm, xp, slope, field))
    ym, yp = exchange_subs(xm, xp, y_low, y_high)
    terms = weight_terms(meta, field, slope)
    parts = swap_all(terms.reshape(DEVICES, 16, DEPTH))
    normed_out = normed_values(meta, totals, params, conv, voxel_mask, normed_base)
    shared = swap_all(share(parts))
    feature_grad = backward(meta, kept, voxel_mask, (xm, xp, ym, yp), back, feature_base)
    weight_grad = arrange(shared.reshape(2048, DEPTH))
    return (normed_out, feature_grad, weight_grad, sums[0, :CHANS], sums[1, :CHANS])


def solution(mesh):
    placed = (
        P("slab", "sub", None, None),
        P("slab", "sub", None),
        P(),
        P(),
        P(),
        P("slab", "sub", None, None),
    )
    return jax.shard_map(
        body,
        mesh=mesh,
        in_specs=placed,
        out_specs=(P("slab", "sub", None, None), P("slab", "sub", None, None), P(), P(), P()),
        check_vma=False,
    )
```

time: 771 us -> 164 us (0.21)
  the two profiles are of different devices: /device:TPU:14 before, /device:TPU:3 now
where the time goes in v2:
time: 164 us; the launch traced here: 163 us
  Pallas kernels  79.6 us (49%)
  starting transfers between devices  32.5 us (20%)
  blocking collectives  26.2 us (16%)
  waiting for transfers between devices  19.7 us (12%)
  local copies, waits for them, and re-layouts  3.92 us (2%)
    all_to_all x1, blocking collectives, swap_all(): return lax.all_to_all(pieces, ('slab', 'sub'), 0, 0, tiled=True)  26.2 us
    pallas_call x1, Pallas kernels, backward(): pl.pallas_call(backward_kernel, name='backward', out_shape=jax.ShapeDtype...  17.4 us
    pallas_call x1, Pallas kernels, forward(): pl.pallas_call(forward_kernel, name='forward', out_shape=(jax.ShapeDtypeS...  16.2 us
    pallas_call x1, Pallas kernels, weight_terms(): pl.pallas_call(weight_kernel, name='weight_terms', out_shape=jax.ShapeDty...  15 us
    all_to_all x2, starting transfers between devices, swap_all(): return lax.all_to_all(pieces, ('slab', 'sub'), 0, 0, tiled=True)  11 us
    pallas_call x1, Pallas kernels, slopes(): pl.pallas_call(slope_kernel, name='slopes', out_shape=(jax.ShapeDtypeStru...  10 us
    ppermute x2, waiting for transfers between devices, exchange_slabs(): xp = lax.ppermute(x_low, 'slab', [(i + 1, i) for i in range(slabs - 1)])  8.97 us
    all_to_all x2, waiting for transfers between devices, swap_all(): return lax.all_to_all(pieces, ('slab', 'sub'), 0, 0, tiled=True)  6.79 us
  transfers between devices with their start and end apart: 10, of which 6 were waited for; matrix products, arithmetic and copies ran while one was open for 0% of the time, Pallas kernels for 19%

profile of v2, /device:TPU:3, one launch (start us, length us, event | category | flops | bytes accessed | tf_op | source)
XLA Modules:
  0.0 163.0 jit_solution(16730379069890734837)
XLA Ops:
  0.6 0.0 copy-start.1
  0.6 0.0 copy-start
  0.7 0.0 copy-start.2
  0.7 4.6 %prepare.1 = (bf16[16,96,128]{2,1,0:T(8,128)(2,1)}, bf16[16,96,128]{2,1,0:T(8,128)(2,1)}, bf16[18,96,128]{2,1,0:T(8,128)(2,1)}, bf16[18,96,128]{2,1,0:T(8,128)(2,1)}, s32[9]{0:T(128)}) custom-call(bf16[16,16,96,128]{3,2,1,0:T(8,128)(2,1)} %features.5, s32[16,16,128]{2,1,0:T(8,128)} %mask.13), custom_call_target="tpu_custom_call" | custom-call | flops 3000000 | bytes 3000000 | tf_op jit(solution)/shard_map/prepare/pallas_call | solution.py:154
  5.3 4.1 %collective-permute-start = (bf16[16,96,128]{2,1,0:T(8,128)(2,1)}, bf16[16,96,128]{2,1,0:T(8,128)(2,1)S(1)}, u32[]{:S(2)}, u32[]{:S(2)}) collective-permute-start(bf16[16,96,128]{2,1,0:T(8,128)(2,1)} %get-tuple-element.46), channel_id=1, source_target_pairs={{0,4},{4,8},{8,12},{12,16},{16,20},{20,24},{24,28},{28,32},{32,36}... | collective-permute-start | bytes 1179656 | tf_op jit(solution)/shard_map/ppermute | solution.py:720
  9.4 1.9 %collective-permute-start.1 = (bf16[16,96,128]{2,1,0:T(8,128)(2,1)}, bf16[16,96,128]{2,1,0:T(8,128)(2,1)S(1)}, u32[]{:S(2)}, u32[]{:S(2)}) collective-permute-start(bf16[16,96,128]{2,1,0:T(8,128)(2,1)} %get-tuple-element.47), channel_id=1, source_target_pairs={{4,0},{8,4},{12,8},{16,12},{20,16},{24,20},{28,24},{32,28},{36,32}... | collective-permute-start | bytes 1179656 | tf_op jit(solution)/shard_map/ppermute | solution.py:721
  11.3 3.1 %collective-permute-done.xm.refs_0_ = bf16[16,96,128]{2,1,0:T(8,128)(2,1)S(1)} collective-permute-done((bf16[16,96,128]{2,1,0:T(8,128)(2,1)}, bf16[16,96,128]{2,1,0:T(8,128)(2,1)S(1)}, u32[]{:S(2)}, u32[]{:S(2)}) %collective-permute-start) | collective-permute-done | bytes 393248 | tf_op jit(solution)/shard_map/ppermute | solution.py:720
  14.4 4.3 %collective-permute-done.1.xp.refs_1_ = bf16[16,96,128]{2,1,0:T(8,128)(2,1)S(1)} collective-permute-done((bf16[16,96,128]{2,1,0:T(8,128)(2,1)}, bf16[16,96,128]{2,1,0:T(8,128)(2,1)S(1)}, u32[]{:S(2)}, u32[]{:S(2)}) %collective-permute-start.1) | collective-permute-done | bytes 393248 | tf_op jit(solution)/shard_map/ppermute | solution.py:721
  18.7 0.0 copy-start.4
  18.7 1.0 copy-done.4
  19.7 0.7 stitch.2
  20.4 0.0 copy-start.5
  20.4 0.8 copy-done.5
  21.1 3.1 %collective-permute-start.2 = (bf16[18,96,128]{2,1,0:T(8,128)(2,1)}, bf16[18,96,128]{2,1,0:T(8,128)(2,1)S(1)}, u32[]{:S(2)}, u32[]{:S(2)}) collective-permute-start(bf16[18,96,128]{2,1,0:T(8,128)(2,1)} %copy-done.5), channel_id=1, source_target_pairs={{0,1},{1,2},{2,3},{4,5},{5,6},{6,7},{8,9},{9,10},{10,11},{12,13},{... | collective-permute-start | bytes 1327112 | tf_op jit(solution)/shard_map/ppermute | solution.py:728
  24.3 2.2 %collective-permute-start.3 = (bf16[18,96,128]{2,1,0:T(8,128)(2,1)}, bf16[18,96,128]{2,1,0:T(8,128)(2,1)S(1)}, u32[]{:S(2)}, u32[]{:S(2)}) collective-permute-start(bf16[18,96,128]{2,1,0:T(8,128)(2,1)} %get-tuple-element.51), channel_id=1, source_target_pairs={{1,0},{2,1},{3,2},{5,4},{6,5},{7,6},{9,8},{10,9},{11,10},{13,12},{... | collective-permute-start | bytes 1327112 | tf_op jit(solution)/shard_map/ppermute | solution.py:729
  26.5 0.0 copy-start.6
  26.5 0.6 copy-done.6
  27.1 3.5 %blanks.1 = (bf16[16,16,96,128]{3,2,1,0:T(8,128)(2,1)}, bf16[16,16,96,128]{3,2,1,0:T(8,128)(2,1)}) custom-call(s32[9]{0:T(128)S(1)} %copy-done.6), custom_call_target="tpu_custom_call" | custom-call | flops 1000 | bytes 8000000 | tf_op jit(solution)/shard_map/blanks/pallas_call | solution.py:341
  30.6 0.0 copy-done.2
  30.7 0.0 slice-start
  30.7 0.5 tap_kernels.1
  31.2 0.0 copy-done.1
  31.2 0.0 copy-done
  31.2 0.0 copy-start.8
  31.2 0.0 copy-start.9
  31.3 0.0 slice-start.1
  31.3 1.6 build.1.before
  32.9 0.0 copy-done.8
  32.9 0.0 copy-done.9
  32.9 0.0 collective-permute-done.2.ym.refs_2_
  32.9 0.6 collective-permute-done.3.yp.refs_3_
  33.5 0.0 slice-done
  33.5 0.2 slice-done.1
  33.7 16.2 %forward.1 = (bf16[18,18,96,128]{3,2,1,0:T(8,128)(2,1)S(1)}, f32[24,8,8,96,128]{4,3,2,1,0:T(8,128)}, f32[128,8,128]{2,1,0:T(8,128)S(1)}) custom-call(s32[9]{0:T(128)S(1)} %copy-done.6, bf16[18,18,96,128]{3,2,1,0:T(8,128)(2,1)S(1)} %build.1.before, bf16[16,16,96,128]{3,2,1,0:T(8,128)(2,1)S(1)} %bitcast.9, ...), custom_call_target="tpu_custom_call", output_to_operand_aliasing={{0}: (1, {})} | custom-call | flops 16000000000 | bytes 4000000 | tf_op jit(solution)/shard_map/forward/pallas_call | solution.py:280
  49.9 26.2 %all_to_all.15.gathered = f32[128,8,128]{2,1,0:T(8,128)S(1)} all-to-all(f32[128,8,128]{2,1,0:T(8,128)S(1)} %get-tuple-element.53), channel_id=1, replica_groups=mesh['slab'=32,'sub'=4] {'slab','sub'}, dimensions={0} | all-to-all | bytes 1048576 | tf_op jit(solution)/shard_map/all_to_all | solution.py:734
  76.1 10.0 %slopes.1 = (bf16[18,18,96,128]{3,2,1,0:T(8,128)(2,1)}, bf16[48,8,8,96,128]{4,3,2,1,0:T(8,128)(2,1)}, bf16[16,96,128]{2,1,0:T(8,128)(2,1)S(1)}, bf16[16,96,128]{...) custom-call(s32[9]{0:T(128)S(1)} %copy-done.6, ...), custom_call_target="tpu_custom_call" | custom-call | flops 30000000 | bytes 12000000 | tf_op jit(solution)/shard_map/slopes/pallas_call | solution.py:424
  86.1 2.6 %collective-permute-start.4 = (bf16[16,96,128]{2,1,0:T(8,128)(2,1)S(1)}, bf16[16,96,128]{2,1,0:T(8,128)(2,1)S(1)}, u32[]{:S(2)}, u32[]{:S(2)}) collective-permute-start(bf16[16,96,128]{2,1,0:T(8,128)(2,1)S(1)} %get-tuple-element.59), channel_id=1, source_target_pairs={{0,4},{4,8},{8,12},{12,16},{16,20},{20,24},{24,28},{28,32},{32,36}... | collective-permute-start | bytes 1179656 | tf_op jit(solution)/shard_map/ppermute | solution.py:720
  88.7 0.0 slice-start.2
  88.7 0.0 slice-start.3
  88.7 2.3 %collective-permute-start.5 = (bf16[16,96,128]{2,1,0:T(8,128)(2,1)S(1)}, bf16[16,96,128]{2,1,0:T(8,128)(2,1)S(1)}, u32[]{:S(2)}, u32[]{:S(2)}) collective-permute-start(bf16[16,96,128]{2,1,0:T(8,128)(2,1)S(1)} %get-tuple-element.60), channel_id=1, source_target_pairs={{4,0},{8,4},{12,8},{16,12},{20,16},{24,20},{28,24},{32,28},{36,32}... | collective-permute-start | bytes 1179656 | tf_op jit(solution)/shard_map/ppermute | solution.py:721
  91.1 2.1 %build_whole.1.field = bf16[18,18,96,128]{3,2,1,0:T(8,128)(2,1)S(1)} custom-call(s32[9]{0:T(128)S(1)} %copy-done.6, bf16[16,16,96,128]{3,2,1,0:T(8,128)(2,1)S(1)} %copy-done, s32[16,16,128]{2,1,0:T(8,128)S(1)} %copy-done.1, bf16[16,96,128]{2,1,0:T(8,128)(2,1)S(1)} %collective-permute-done.xm.refs_0_, ...), custom_call_target="tpu_custom_call" | custom-call | flops 3000000 | bytes 6000000 | tf_op jit(solution)/shard_map/build_whole/pallas_call | solution.py:189
  93.1 0.3 collective-permute-done.4.xm
  93.4 4.7 %collective-permute-done.5.xp = bf16[16,96,128]{2,1,0:T(8,128)(2,1)S(1)} collective-permute-done((bf16[16,96,128]{2,1,0:T(8,128)(2,1)S(1)}, bf16[16,96,128]{2,1,0:T(8,128)(2,1)S(1)}, u32[]{:S(2)}, u32[]{:S(2)}) %collective-permute-start.5) | collective-permute-done | bytes 393248 | tf_op jit(solution)/shard_map/ppermute | solution.py:721
  98.1 0.0 slice-done.2
  98.1 0.0 slice-done.3
  98.1 0.0 copy-start.7
  98.1 15.0 %weight_terms.1 = f32[2048,128]{1,0:T(8,128)} custom-call(s32[9]{0:T(128)S(1)} %copy-done.6, bf16[18,18,96,128]{3,2,1,0:T(8,128)(2,1)S(1)} %build_whole.1.field, bf16[18,18,96,128]{3,2,1,0:T(8,128)(2,1)S(1)} %bitcast.12), custom_call_target="tpu_custom_call" | custom-call | flops 16000000000 | bytes 2000000 | tf_op jit(solution)/shard_map/weight_terms/pallas_call | solution.py:526
  113.1 6.7 %all-to-all-start.1 = ((f32[128,16,128]{2,1,0:T(8,128)}), f32[128,16,128]{2,1,0:T(8,128)S(1)}, u32[]{:S(2)}, u32[]{:S(2)}) async-start(f32[128,16,128]{2,1,0:T(8,128)} %bitcast.2), calls=%async_computation.1 | async-start | bytes 2097152 | tf_op jit(solution)/shard_map/all_to_all | solution.py:734
  119.8 0.7 stitch.3
  120.4 0.0 copy-start.3
  120.5 0.8 copy-done.3
  121.2 3.1 %collective-permute-start.6 = (bf16[18,96,128]{2,1,0:T(8,128)(2,1)}, bf16[18,96,128]{2,1,0:T(8,128)(2,1)S(1)}, u32[]{:S(2)}, u32[]{:S(2)}) collective-permute-start(bf16[18,96,128]{2,1,0:T(8,128)(2,1)} %get-tuple-element.70), channel_id=1, source_target_pairs={{0,1},{1,2},{2,3},{4,5},{5,6},{6,7},{8,9},{9,10},{10,11},{12,13},{... | collective-permute-start | bytes 1327112 | tf_op jit(solution)/shard_map/ppermute | solution.py:728
  124.3 2.2 %collective-permute-start.7 = (bf16[18,96,128]{2,1,0:T(8,128)(2,1)}, bf16[18,96,128]{2,1,0:T(8,128)(2,1)S(1)}, u32[]{:S(2)}, u32[]{:S(2)}) collective-permute-start(bf16[18,96,128]{2,1,0:T(8,128)(2,1)} %copy-done.3), channel_id=1, source_target_pairs={{1,0},{2,1},{3,2},{5,4},{6,5},{7,6},{9,8},{10,9},{11,10},{13,12},{... | collective-permute-start | bytes 1327112 | tf_op jit(solution)/shard_map/ppermute | solution.py:729
  126.5 0.0 copy-done.7
  126.5 5.1 %normed_values.1 = bf16[16,16,96,128]{3,2,1,0:T(8,128)(2,1)} custom-call(s32[9]{0:T(128)S(1)} %copy-done.7, f32[8,128]{1,0:T(8,128)S(1)} %get-tuple-element.56.totals, f32[8,128]{1,0:T(8,128)S(1)} %select_maximum_fusion.params, f32[24,8,8,96,128]{4,3,2,1,0:T(8,128)} %get-tuple-element.55.conv, ...), custom_call_target="tpu_custom_call", output_to_operand_aliasing={{}: (5, {})} | custom-call | flops 30000000 | bytes 8000000 | tf_op jit(solution)/shard_map/normed_values/pallas_call | solution.py:472
  131.6 0.5 slice_bitcast_fusion
  132.1 6.8 %all-to-all-done.1.parts = f32[128,16,128]{2,1,0:T(8,128)S(1)} async-done(((f32[128,16,128]{2,1,0:T(8,128)}), f32[128,16,128]{2,1,0:T(8,128)S(1)}, u32[]{:S(2)}, u32[]{:S(2)}) %all-to-all-start.1) | async-done | bytes 1048608 | tf_op jit(solution)/shard_map/all_to_all | solution.py:734
  138.9 1.0 share.1
  139.9 4.3 %all-to-all-start.2 = ((bf16[128,16,128]{2,1,0:T(8,128)(2,1)}), bf16[128,16,128]{2,1,0:T(8,128)(2,1)S(1)}, u32[]{:S(2)}, u32[]{:S(2)}) async-start(bf16[128,16,128]{2,1,0:T(8,128)(2,1)} %share.1), calls=%async_computation.2 | async-start | bytes 1048576 | tf_op jit(solution)/shard_map/all_to_all | solution.py:734
  144.2 0.0 collective-permute-done.6.ym
  144.2 0.0 collective-permute-done.7.yp
  144.2 17.4 %backward.1 = bf16[16,16,96,128]{3,2,1,0:T(8,128)(2,1)} custom-call(s32[9]{0:T(128)S(1)} %copy-done.7, bf16[48,8,8,96,128]{4,3,2,1,0:T(8,128)(2,1)} %get-tuple-element.58.kept, s32[16,16,128]{2,1,0:T(8,128)S(1)} %copy-done.1, bf16[16,96,128]{2,1,0:T(8,128)(2,1)S(1)} %collective-permute-done.4.xm, ...), custom_call_target="tpu_custom_call", output_to_operand_aliasing={{}: (8, {})} | custom-call | flops 16000000000 | bytes 5000000 | tf_op jit(solution)/shard_map/backward/pallas_call | solution.py:629
  161.6 0.0 all-to-all-done.2
  161.6 1.4 arrange.1
  (3 shorter events, 0.0 us)
Async XLA Ops:
  0.6 30.6 %copy-start.1 = (s32[16,16,128]{2,1,0:T(8,128)S(1)}, s32[16,16,128]{2,1,0:T(8,128)}, u32[]{:S(2)}) copy-start(s32[16,16,128]{2,1,0:T(8,128)} %mask.13) | copy-start | bytes 393220
  0.6 30.6 %copy-start = (bf16[16,16,96,128]{3,2,1,0:T(8,128)(2,1)S(1)}, bf16[16,16,96,128]{3,2,1,0:T(8,128)(2,1)}, u32[]{:S(2)}) copy-start(bf16[16,16,96,128]{3,2,1,0:T(8,128)(2,1)} %features.5) | copy-start | bytes 18874372
  0.7 30.0 %copy-start.2 = (bf16[27,96,96]{2,1,0:T(8,128)(2,1)S(1)}, bf16[27,96,96]{2,1,0:T(8,128)(2,1)}, u32[]{:S(2)}) copy-start(bf16[27,96,96]{2,1,0:T(8,128)(2,1)} %weight.1) | copy-start | bytes 1492996
  5.3 9.1 %collective-permute-start = (bf16[16,96,128]{2,1,0:T(8,128)(2,1)}, bf16[16,96,128]{2,1,0:T(8,128)(2,1)S(1)}, u32[]{:S(2)}, u32[]{:S(2)}) collective-permute-start(bf16[16,96,128]{2,1,0:T(8,128)(2,1)} %get-tuple-element.46), channel_id=1, source_target_pairs={{0,4},{4,8},{8,12},{12,16},{16,20},{20,24},{24,28},{28,32},{32,36}... | collective-permute-start | bytes 1179656 | tf_op jit(solution)/shard_map/ppermute | solution.py:720
  9.4 9.3 %collective-permute-start.1 = (bf16[16,96,128]{2,1,0:T(8,128)(2,1)}, bf16[16,96,128]{2,1,0:T(8,128)(2,1)S(1)}, u32[]{:S(2)}, u32[]{:S(2)}) collective-permute-start(bf16[16,96,128]{2,1,0:T(8,128)(2,1)} %get-tuple-element.47), channel_id=1, source_target_pairs={{4,0},{8,4},{12,8},{16,12},{20,16},{24,20},{28,24},{32,28},{36,32}... | collective-permute-start | bytes 1179656 | tf_op jit(solution)/shard_map/ppermute | solution.py:721
  18.7 1.0 copy-start.4
  20.4 0.8 copy-start.5
  21.1 11.8 %collective-permute-start.2 = (bf16[18,96,128]{2,1,0:T(8,128)(2,1)}, bf16[18,96,128]{2,1,0:T(8,128)(2,1)S(1)}, u32[]{:S(2)}, u32[]{:S(2)}) collective-permute-start(bf16[18,96,128]{2,1,0:T(8,128)(2,1)} %copy-done.5), channel_id=1, source_target_pairs={{0,1},{1,2},{2,3},{4,5},{5,6},{6,7},{8,9},{9,10},{10,11},{12,13},{... | collective-permute-start | bytes 1327112 | tf_op jit(solution)/shard_map/ppermute | solution.py:728
  24.3 9.3 %collective-permute-start.3 = (bf16[18,96,128]{2,1,0:T(8,128)(2,1)}, bf16[18,96,128]{2,1,0:T(8,128)(2,1)S(1)}, u32[]{:S(2)}, u32[]{:S(2)}) collective-permute-start(bf16[18,96,128]{2,1,0:T(8,128)(2,1)} %get-tuple-element.51), channel_id=1, source_target_pairs={{1,0},{2,1},{3,2},{5,4},{6,5},{7,6},{9,8},{10,9},{11,10},{13,12},{... | collective-permute-start | bytes 1327112 | tf_op jit(solution)/shard_map/ppermute | solution.py:729
  26.5 0.7 copy-start.6
  30.7 2.9 %slice-start = ((s8[6291456]{0:T(1024)(128)(4,1)}), s8[4194304]{0:T(1024)(128)(4,1)S(1)}, s32[]{:S(2)}) async-start(s8[6291456]{0:T(1024)(128)(4,1)} %bitcast.8), calls=%async_computation.3 | async-start | bytes 8388608
  31.2 1.7 %copy-start.8 = (f32[96]{0:T(128)S(1)}, f32[96]{0:T(128)}, u32[]{:S(2)}) copy-start(f32[96]{0:T(128)} %param.10) | copy-start | bytes 1156
  31.2 1.7 %copy-start.9 = (f32[96]{0:T(128)S(1)}, f32[96]{0:T(128)}, u32[]{:S(2)}) copy-start(f32[96]{0:T(128)} %param.9) | copy-start | bytes 1156
  31.3 2.4 %slice-start.1 = ((s8[6291456]{0:T(1024)(128)(4,1)}), s8[2097152]{0:T(1024)(128)(4,1)S(1)}, s32[]{:S(2)}) async-start(s8[6291456]{0:T(1024)(128)(4,1)} %bitcast.8), calls=%async_computation.4 | async-start | bytes 4194304
  86.1 7.3 %collective-permute-start.4 = (bf16[16,96,128]{2,1,0:T(8,128)(2,1)S(1)}, bf16[16,96,128]{2,1,0:T(8,128)(2,1)S(1)}, u32[]{:S(2)}, u32[]{:S(2)}) collective-permute-start(bf16[16,96,128]{2,1,0:T(8,128)(2,1)S(1)} %get-tuple-element.59), channel_id=1, source_target_pairs={{0,4},{4,8},{8,12},{12,16},{16,20},{20,24},{24,28},{28,32},{32,36}... | collective-permute-start | bytes 1179656 | tf_op jit(solution)/shard_map/ppermute | solution.py:720
  88.7 9.4 %slice-start.2 = ((s8[7962624]{0:T(1024)(128)(4,1)}), s8[4194304]{0:T(1024)(128)(4,1)S(1)}, s32[]{:S(2)}) async-start(s8[7962624]{0:T(1024)(128)(4,1)} %bitcast.11), calls=%async_computation.5 | async-start | bytes 8388608
  88.7 9.4 %slice-start.3 = ((s8[7962624]{0:T(1024)(128)(4,1)}), s8[3768320]{0:T(1024)(128)(4,1)S(1)}, s32[]{:S(2)}) async-start(s8[7962624]{0:T(1024)(128)(4,1)} %bitcast.11), calls=%async_computation.6 | async-start | bytes 7536640
  88.7 9.4 %collective-permute-start.5 = (bf16[16,96,128]{2,1,0:T(8,128)(2,1)S(1)}, bf16[16,96,128]{2,1,0:T(8,128)(2,1)S(1)}, u32[]{:S(2)}, u32[]{:S(2)}) collective-permute-start(bf16[16,96,128]{2,1,0:T(8,128)(2,1)S(1)} %get-tuple-element.60), channel_id=1, source_target_pairs={{4,0},{8,4},{12,8},{16,12},{20,16},{24,20},{28,24},{32,28},{36,32}... | collective-permute-start | bytes 1179656 | tf_op jit(solution)/shard_map/ppermute | solution.py:721
  98.1 28.4 %copy-start.7 = (s32[9]{0:T(128)S(1)}, s32[9]{0:T(128)}, u32[]{:S(2)}) copy-start(s32[9]{0:T(128)} %get-tuple-element.41.meta) | copy-start | bytes 112
  113.1 25.8 %all-to-all-start.1 = ((f32[128,16,128]{2,1,0:T(8,128)}), f32[128,16,128]{2,1,0:T(8,128)S(1)}, u32[]{:S(2)}, u32[]{:S(2)}) async-start(f32[128,16,128]{2,1,0:T(8,128)} %bitcast.2), calls=%async_computation.1 | async-start | bytes 2097152 | tf_op jit(solution)/shard_map/all_to_all | solution.py:734
  120.4 0.8 copy-start.3
  121.2 23.0 %collective-permute-start.6 = (bf16[18,96,128]{2,1,0:T(8,128)(2,1)}, bf16[18,96,128]{2,1,0:T(8,128)(2,1)S(1)}, u32[]{:S(2)}, u32[]{:S(2)}) collective-permute-start(bf16[18,96,128]{2,1,0:T(8,128)(2,1)} %get-tuple-element.70), channel_id=1, source_target_pairs={{0,1},{1,2},{2,3},{4,5},{5,6},{6,7},{8,9},{9,10},{10,11},{12,13},{... | collective-permute-start | bytes 1327112 | tf_op jit(solution)/shard_map/ppermute | solution.py:728
  124.3 19.9 %collective-permute-start.7 = (bf16[18,96,128]{2,1,0:T(8,128)(2,1)}, bf16[18,96,128]{2,1,0:T(8,128)(2,1)S(1)}, u32[]{:S(2)}, u32[]{:S(2)}) collective-permute-start(bf16[18,96,128]{2,1,0:T(8,128)(2,1)} %copy-done.3), channel_id=1, source_target_pairs={{1,0},{2,1},{3,2},{5,4},{6,5},{7,6},{9,8},{10,9},{11,10},{13,12},{... | collective-permute-start | bytes 1327112 | tf_op jit(solution)/shard_map/ppermute | solution.py:729
  139.9 21.7 %all-to-all-start.2 = ((bf16[128,16,128]{2,1,0:T(8,128)(2,1)}), bf16[128,16,128]{2,1,0:T(8,128)(2,1)S(1)}, u32[]{:S(2)}, u32[]{:S(2)}) async-start(bf16[128,16,128]{2,1,0:T(8,128)(2,1)} %share.1), calls=%async_computation.2 | async-start | bytes 1048576 | tf_op jit(solution)/shard_map/all_to_all | solution.py:734

commit v3 on v2

--- a/solution.py
+++ b/solution.py
@@ -70,13 +70,21 @@
 
 
 def fill_rims(field, rims, sems):
-    xm, xp, ym, yp = rims
+    xm, xp, ym, yp = rims[:4]
+    side = pl.ds(1, 16) if len(rims) > 4 else pl.ds(0, 18)
     copies = [
         pltpu.make_async_copy(xm, field.at[0, pl.ds(1, 16)], sems.at[0]),
         pltpu.make_async_copy(xp, field.at[17, pl.ds(1, 16)], sems.at[1]),
-        pltpu.make_async_copy(ym, field.at[:, 0], sems.at[2]),
-        pltpu.make_async_copy(yp, field.at[:, 17], sems.at[3]),
+        pltpu.make_async_copy(ym, field.at[side, 0], sems.at[2]),
+        pltpu.make_async_copy(yp, field.at[side, 17], sems.at[3]),
     ]
+    for which, corners in enumerate(rims[4:]):
+        for end in range(2):
+            copies.append(
+                pltpu.make_async_copy(
+                    corners.at[end], field.at[17 * end, 17 * which], sems.at[4 + 2 * which + end]
+                )
+            )
     for copy in copies:
         copy.start()
     return copies
@@ -100,19 +108,13 @@
 LONG = jax.ShapeDtypeStruct((18, CHANS, DEPTH), BF16)
 
 
-def prepare_kernel(features, mask, x_low, x_high, y_low, y_high, meta, faces, sides, sem_in, sem_out):
+def prepare_kernel(features, mask, x_low, x_high, y_low, y_high, meta, sem_in):
+    faces, sides = (x_low, x_high), (y_low, y_high)
     loads = [
-        pltpu.make_async_copy(features.at[0], faces.at[0], sem_in.at[0]),
-        pltpu.make_async_copy(features.at[15], faces.at[1], sem_in.at[1]),
-        pltpu.make_async_copy(features.at[:, 0], sides.at[0], sem_in.at[2]),
-        pltpu.make_async_copy(features.at[:, 15], sides.at[1], sem_in.at[3]),
-    ]
-    inner = pl.ds(1, 16)
-    stores = [
-        pltpu.make_async_copy(faces.at[0], x_low, sem_out.at[0]),
-        pltpu.make_async_copy(faces.at[1], x_high, sem_out.at[1]),
-        pltpu.make_async_copy(sides.at[0], y_low.at[inner], sem_out.at[2]),
-        pltpu.make_async_copy(sides.at[1], y_high.at[inner], sem_out.at[3]),
+        pltpu.make_async_copy(features.at[0], x_low, sem_in.at[0]),
+        pltpu.make_async_copy(features.at[15], x_high, sem_in.at[1]),
+        pltpu.make_async_copy(features.at[:, 0], y_low, sem_in.at[2]),
+        pltpu.make_async_copy(features.at[:, 15], y_high, sem_in.at[3]),
     ]
     for load in loads:
         load.start()
@@ -138,31 +140,22 @@
         loads[which].wait()
         for col in range(16):
             keep = jnp.broadcast_to(mask[15 * which, col : col + 1, :], (CHANS, DEPTH))
-            faces[which, col] = faces[which, col] * keep.astype(F32).astype(BF16)
-        stores[which].start()
+            faces[which][col] = faces[which][col] * keep.astype(F32).astype(BF16)
     for which in range(2):
         loads[2 + which].wait()
         for row in range(16):
             keep = jnp.broadcast_to(mask[row, 15 * which : 15 * which + 1, :], (CHANS, DEPTH))
-            sides[which, row] = sides[which, row] * keep.astype(F32).astype(BF16)
-        stores[2 + which].start()
-    for store in stores:
-        store.wait()
+            sides[which][row] = sides[which][row] * keep.astype(F32).astype(BF16)
 
 
 def prepare(features, voxel_mask):
     return pl.pallas_call(
         prepare_kernel,
         name="prepare",
-        out_shape=(RIM, RIM, LONG, LONG, jax.ShapeDtypeStruct((9,), jnp.int32)),
+        out_shape=(RIM, RIM, RIM, RIM, jax.ShapeDtypeStruct((9,), jnp.int32)),
         in_specs=[HBM, VMEM],
-        out_specs=(ANY, ANY, ANY, ANY, SMEM),
-        scratch_shapes=[
-            pltpu.VMEM((2, 16, CHANS, DEPTH), BF16),
-            pltpu.VMEM((2, 16, CHANS, DEPTH), BF16),
-            pltpu.SemaphoreType.DMA((4,)),
-            pltpu.SemaphoreType.DMA((4,)),
-        ],
+        out_specs=(VMEM, VMEM, VMEM, VMEM, SMEM),
+        scratch_shapes=[pltpu.SemaphoreType.DMA((4,))],
         compiler_params=params_of(54),
         cost_estimate=cost(3_000_000, 3_000_000),
     )(features, voxel_mask)
@@ -192,7 +185,7 @@
         out_shape=jax.ShapeDtypeStruct(FIELD, BF16),
         in_specs=[SMEM, VMEM, VMEM] + [ANY] * len(rims),
         out_specs=VMEM,
-        scratch_shapes=[pltpu.SemaphoreType.DMA((4,))],
+        scratch_shapes=[pltpu.SemaphoreType.DMA((8,))],
         compiler_params=params_of(2),
         cost_estimate=cost(3_000_000, 6_000_000),
     )(meta, features, voxel_mask, *rims)
@@ -226,12 +219,12 @@
 
 
 def forward_kernel(
-    meta, before, grads, mask, xm, xp, ym, yp, taps, field, conv_out, stats, convs, sums, sem_rim, sem_out
+    meta, before, grads, mask, xm, xp, ym, yp, cm, cp, taps, field, conv_out, stats, convs, sums, sem_rim, sem_out
 ):
     def conv_copy(slot, x):
         return pltpu.make_async_copy(convs.at[slot, x], conv_out.at[slot, x], sem_out.at[slot, x])
 
-    rims = fill_rims(field, (xm, xp, ym, yp), sem_rim)
+    rims = fill_rims(field, (xm, xp, ym, yp, cm, cp), sem_rim)
     for copy in rims:
         copy.wait()
     sums[...] = jnp.zeros(sums.shape, F32)
@@ -285,12 +278,12 @@
             jax.ShapeDtypeStruct(WIDE_CONVS, F32),
             jax.ShapeDtypeStruct((DEVICES, 8, DEPTH), F32),
         ),
-        in_specs=[SMEM, VMEM, VMEM, VMEM, ANY, ANY, ANY, ANY, VMEM],
+        in_specs=[SMEM, VMEM, VMEM, VMEM] + [ANY] * 6 + [VMEM],
         out_specs=(VMEM, HBM, VMEM),
         scratch_shapes=[
             pltpu.VMEM(BLOCKS, F32),
             pltpu.VMEM((5, CHANS, DEPTH), F32),
-            pltpu.SemaphoreType.DMA((4,)),
+            pltpu.SemaphoreType.DMA((8,)),
             pltpu.SemaphoreType.DMA((SLOTS, BRICK)),
         ],
         input_output_aliases={1: 0},
@@ -362,24 +355,14 @@
 
 
 def slope_kernel(
-    meta, gathered, params, conv, out_grad, mask, field, kept, x_low, x_high, y_low, y_high, sums_out, totals_out, convs, grads, sem_conv, sem_og, sem_kept, sem_rim
+    meta, gathered, params, conv, grads, mask, field, kept, x_low, x_high, y_low, y_high, sums_out, totals_out, convs, sem_conv, sem_kept, sem_rim
 ):
     occupied = meta[8]
 
-    def loads(slot, x):
-        x0, y0 = corner(meta, slot)
-        return (
-            pltpu.make_async_copy(conv.at[slot, x], convs.at[slot, x], sem_conv.at[slot, x]),
-            pltpu.make_async_copy(
-                out_grad.at[x0 + x, pl.ds(y0, BRICK)], grads.at[slot, x], sem_og.at[slot, x]
-            ),
-        )
-
-    def begin(slot, x):
-        for copy in loads(slot, x):
-            copy.start()
-
-    each_row(occupied, begin)
+    def load(slot, x):
+        return pltpu.make_async_copy(conv.at[slot, x], convs.at[slot, x], sem_conv.at[slot, x])
+
+    each_row(occupied, lambda slot, x: load(slot, x).start())
 
     def keep_row(slot, x):
         x0, y0 = corner(meta, slot)
@@ -401,13 +384,12 @@
 
     def row(slot, x):
         x0, y0 = corner(meta, slot)
-        for copy in loads(slot, x):
-            copy.wait()
+        load(slot, x).wait()
         active = active_rows(mask, x0 + x, y0)
         for col in range(BRICK):
             keep = active[col : col + 1]
             normed = (convs[slot, x, col] - mean_c) * inv_c
-            up = grads[slot, x, col].astype(F32)
+            up = grads[x0 + x, y0 + col].astype(F32)
             field[x0 + x + 1, y0 + col + 1] = (
                 scale_c * (up - up_c - normed * cross_c) * keep
             ).astype(BF16)
@@ -425,17 +407,15 @@
         slope_kernel,
         name="slopes",
         out_shape=(jax.ShapeDtypeStruct(FIELD, BF16), kept, RIM, RIM, LONG, LONG, small, small),
-        in_specs=[SMEM, VMEM, VMEM, HBM, HBM, VMEM],
+        in_specs=[SMEM, VMEM, VMEM, HBM, VMEM, VMEM],
         out_specs=(VMEM, HBM, ANY, ANY, ANY, ANY, VMEM, VMEM),
         scratch_shapes=[
             pltpu.VMEM(BLOCKS, F32),
-            pltpu.VMEM(BLOCKS, BF16),
-            pltpu.SemaphoreType.DMA((SLOTS, BRICK)),
             pltpu.SemaphoreType.DMA((SLOTS, BRICK)),
             pltpu.SemaphoreType.DMA((SLOTS, BRICK)),
             pltpu.SemaphoreType.DMA((4,)),
         ],
-        compiler_params=params_of(46),
+        compiler_params=params_of(9),
         cost_estimate=cost(30_000_000, 12_000_000),
     )(meta, gathered, params, conv, out_grad, voxel_mask)
 
@@ -645,6 +625,33 @@
     )(meta, kept, voxel_mask, *rims, taps, base)
 
 
+def corner_kernel(xm, xp, upper, lower, sems):
+    copies = [
+        pltpu.make_async_copy(xm.at[15], upper.at[0], sems.at[0]),
+        pltpu.make_async_copy(xp.at[15], upper.at[1], sems.at[1]),
+        pltpu.make_async_copy(xm.at[0], lower.at[0], sems.at[2]),
+        pltpu.make_async_copy(xp.at[0], lower.at[1], sems.at[3]),
+    ]
+    for copy in copies:
+        copy.start()
+    for copy in copies:
+        copy.wait()
+
+
+def corners_of(xm, xp):
+    pair = jax.ShapeDtypeStruct((2, CHANS, DEPTH), BF16)
+    return pl.pallas_call(
+        corner_kernel,
+        name="corners",
+        out_shape=(pair, pair),
+        in_specs=[ANY, ANY],
+        out_specs=(ANY, ANY),
+        scratch_shapes=[pltpu.SemaphoreType.DMA((4,))],
+        compiler_params=params_of(1),
+        cost_estimate=cost(1_000, 200_000),
+    )(xm, xp)
+
+
 def stitch_kernel(high, low, xm, xp, upper, lower, sems):
     copies = [
         pltpu.make_async_copy(xm.at[15], upper.at[0], sems.at[0]),
@@ -723,8 +730,11 @@
 
 
 def exchange_subs(xm, xp, y_low, y_high):
+    return shift_subs(*stitch(y_high, y_low, xm, xp))
+
+
+def shift_subs(upper, lower):
     subs = lax.axis_size("sub")
-    upper, lower = stitch(y_high, y_low, xm, xp)
     ym = lax.ppermute(upper, "sub", [(i, i + 1) for i in range(subs - 1)])
     yp = lax.ppermute(lower, "sub", [(i + 1, i) for i in range(subs - 1)])
     return ym, yp
@@ -737,15 +747,13 @@
 def body(features, voxel_mask, weight, norm_gain, norm_bias, out_grad):
     x_low, x_high, y_low, y_high, meta = prepare(features, voxel_mask)
     xm, xp = exchange_slabs(x_low, x_high)
-    ym, yp = exchange_subs(xm, xp, y_low, y_high)
-    rims = (xm, xp, ym, yp)
+    ym, yp = shift_subs(y_high, y_low)
+    cm, cp = shift_subs(*corners_of(xm, xp))
+    rims = (xm, xp, ym, yp, cm, cp)
     field = build(meta, features, voxel_mask)
     ahead, back = tap_kernels(weight)
     params = jnp.pad(jnp.stack([norm_gain, norm_bias]), ((0, 6), (0, DEPTH - CHANS)))
-    normed_base, feature_base = blanks(meta)
-    field, normed_base, feature_base, params, back = lax.optimization_barrier(
-        (field, normed_base, feature_base, params, back)
-    )
+    field, params, back = lax.optimization_barrier((field, params, back))
     conv, stats = forward(meta, field, out_grad, voxel_mask, rims, ahead)
     slope, kept, x_low, x_high, y_low, y_high, sums, totals = slopes(
         meta, swap_all(stats), params, conv, out_grad, voxel_mask
@@ -757,6 +765,7 @@
     ym, yp = exchange_subs(xm, xp, y_low, y_high)
     terms = weight_terms(meta, field, slope)
     parts = swap_all(terms.reshape(DEVICES, 16, DEPTH))
+    normed_base, feature_base = blanks(meta)
     normed_out = normed_values(meta, totals, params, conv, voxel_mask, normed_base)
     shared = swap_all(share(parts))
     feature_grad = backward(meta, kept, voxel_mask, (xm, xp, ym, yp), back, feature_base)

time: 164 us -> 153 us (0.933)
  the two profiles are of different devices: /device:TPU:3 before, /device:TPU:1 now
where the time goes in v3:
time: 153 us
  Pallas kernels  74.9 us (49%)
  starting transfers between devices  37.1 us (24%)
  blocking collectives  24.5 us (16%)
  waiting for transfers between devices  13 us (8%)
  local copies, waits for them, and re-layouts  2.26 us (1%)
    all_to_all x1, blocking collectives, swap_all(): return lax.all_to_all(pieces, ('slab', 'sub'), 0, 0, tiled=True)  24.5 us
    pallas_call x1, Pallas kernels, backward(): pl.pallas_call(backward_kernel, name='backward', out_shape=jax.ShapeDtype...  17.4 us
    pallas_call x1, Pallas kernels, forward(): pl.pallas_call(forward_kernel, name='forward', out_shape=(jax.ShapeDtypeS...  16.4 us
    pallas_call x1, Pallas kernels, weight_terms(): pl.pallas_call(weight_kernel, name='weight_terms', out_shape=jax.ShapeDty...  15.1 us
    all_to_all x2, starting transfers between devices, swap_all(): return lax.all_to_all(pieces, ('slab', 'sub'), 0, 0, tiled=True)  12.4 us
    ppermute x3, starting transfers between devices, shift_subs(): ym = lax.ppermute(upper, 'sub', [(i, i + 1) for i in range(subs - 1)])  9.56 us
    ppermute x2, waiting for transfers between devices, exchange_slabs(): xp = lax.ppermute(x_low, 'slab', [(i + 1, i) for i in range(slabs - 1)])  7.61 us
    ppermute x2, starting transfers between devices, exchange_slabs(): xm = lax.ppermute(x_high, 'slab', [(i, i + 1) for i in range(slabs - 1)])  6.86 us
  transfers between devices with their start and end apart: 12, of which 4 were waited for; matrix products, arithmetic and copies ran while one was open for 0% of the time, Pallas kernels for 21%

profile of v3, /device:TPU:1, one launch (start us, length us, event | category | flops | bytes accessed | tf_op | source)
XLA Modules:
  0.0 152.7 jit_solution(15286907996925963978)
XLA Ops:
  0.6 0.0 copy-start
  0.6 0.0 copy-start.1
  0.7 0.0 copy-start.7
  0.7 0.0 copy-start.6
  0.7 0.0 copy-start.2
  0.7 4.1 %prepare.1 = (bf16[16,96,128]{2,1,0:T(8,128)(2,1)}, bf16[16,96,128]{2,1,0:T(8,128)(2,1)}, bf16[16,96,128]{2,1,0:T(8,128)(2,1)}, bf16[16,96,128]{2,1,0:T(8,128)(2,1)}, s32[9]{0:T(128)}) custom-call(bf16[16,16,96,128]{3,2,1,0:T(8,128)(2,1)} %features.5, s32[16,16,128]{2,1,0:T(8,128)} %mask.13), custom_call_target="tpu_custom_call" | custom-call | flops 3000000 | bytes 3000000 | tf_op jit(solution)/shard_map/prepare/pallas_call | solution.py:152
  4.8 4.9 %collective-permute-start = (bf16[16,96,128]{2,1,0:T(8,128)(2,1)}, bf16[16,96,128]{2,1,0:T(8,128)(2,1)S(1)}, u32[]{:S(2)}, u32[]{:S(2)}) collective-permute-start(bf16[16,96,128]{2,1,0:T(8,128)(2,1)} %get-tuple-element.44), channel_id=1, source_target_pairs={{0,4},{4,8},{8,12},{12,16},{16,20},{20,24},{24,28},{28,32},{32,36}... | collective-permute-start | bytes 1179656 | tf_op jit(solution)/shard_map/ppermute | solution.py:727
  9.7 1.9 %collective-permute-start.1 = (bf16[16,96,128]{2,1,0:T(8,128)(2,1)}, bf16[16,96,128]{2,1,0:T(8,128)(2,1)S(1)}, u32[]{:S(2)}, u32[]{:S(2)}) collective-permute-start(bf16[16,96,128]{2,1,0:T(8,128)(2,1)} %get-tuple-element.45), channel_id=1, source_target_pairs={{4,0},{8,4},{12,8},{16,12},{20,16},{24,20},{28,24},{32,28},{36,32}... | collective-permute-start | bytes 1179656 | tf_op jit(solution)/shard_map/ppermute | solution.py:728
  11.7 3.1 %collective-permute-start.2 = (bf16[16,96,128]{2,1,0:T(8,128)(2,1)}, bf16[16,96,128]{2,1,0:T(8,128)(2,1)S(1)}, u32[]{:S(2)}, u32[]{:S(2)}) collective-permute-start(bf16[16,96,128]{2,1,0:T(8,128)(2,1)} %get-tuple-element.46), channel_id=1, source_target_pairs={{0,1},{1,2},{2,3},{4,5},{5,6},{6,7},{8,9},{9,10},{10,11},{12,13},{... | collective-permute-start | bytes 1179656 | tf_op jit(solution)/shard_map/ppermute | solution.py:738
  14.8 1.3 collective-permute-start.3
  16.1 0.0 collective-permute-done.xm.refs_0_
  16.1 3.2 %collective-permute-done.1.xp.refs_1_ = bf16[16,96,128]{2,1,0:T(8,128)(2,1)S(1)} collective-permute-done((bf16[16,96,128]{2,1,0:T(8,128)(2,1)}, bf16[16,96,128]{2,1,0:T(8,128)(2,1)S(1)}, u32[]{:S(2)}, u32[]{:S(2)}) %collective-permute-start.1) | collective-permute-done | bytes 393248 | tf_op jit(solution)/shard_map/ppermute | solution.py:728
  19.4 0.1 corners.1
  19.5 3.1 %collective-permute-start.4 = (bf16[2,96,128]{2,1,0:T(8,128)(2,1)S(1)}, bf16[2,96,128]{2,1,0:T(8,128)(2,1)S(1)}, u32[]{:S(2)}, u32[]{:S(2)}) collective-permute-start(bf16[2,96,128]{2,1,0:T(8,128)(2,1)S(1)} %get-tuple-element.48), channel_id=1, source_target_pairs={{0,1},{1,2},{2,3},{4,5},{5,6},{6,7},{8,9},{9,10},{10,11},{12,13},{... | collective-permute-start | bytes 147464 | tf_op jit(solution)/shard_map/ppermute | solution.py:738
  22.6 1.3 collective-permute-start.5
  23.9 0.0 copy-done.7
  23.9 0.0 copy-done.6
  24.0 0.0 copy-done.2
  24.0 0.0 slice-start
  24.0 0.5 tap_kernels.1
  24.5 0.0 copy-done
  24.5 0.0 copy-done.1
  24.5 0.0 copy-start.4
  24.6 0.9 copy-done.4
  25.5 0.0 slice-start.1
  25.5 1.6 %build.1.before = bf16[18,18,96,128]{3,2,1,0:T(8,128)(2,1)S(1)} custom-call(s32[9]{0:T(128)S(1)} %copy-done.4, bf16[16,16,96,128]{3,2,1,0:T(8,128)(2,1)S(1)} %copy-done, s32[16,16,128]{2,1,0:T(8,128)S(1)} %copy-done.1), custom_call_target="tpu_custom_call" | custom-call | flops 3000000 | bytes 6000000 | tf_op jit(solution)/shard_map/build/pallas_call | solution.py:182
  27.1 0.0 collective-permute-done.2.ym.refs_2_
  27.1 0.0 collective-permute-done.3.yp.refs_3_
  27.2 0.0 collective-permute-done.4.cm.refs_4_
  27.2 0.3 collective-permute-done.5.cp.refs_5_
  27.5 0.0 slice-done
  27.5 0.0 slice-done.1
  27.5 0.0 copy-start.5
  27.5 16.4 %forward.1 = (bf16[18,18,96,128]{3,2,1,0:T(8,128)(2,1)S(1)}, f32[24,8,8,96,128]{4,3,2,1,0:T(8,128)}, f32[128,8,128]{2,1,0:T(8,128)S(1)}) custom-call(s32[9]{0:T(128)S(1)} %copy-done.4, bf16[18,18,96,128]{3,2,1,0:T(8,128)(2,1)S(1)} %build.1.before, bf16[16,16,96,128]{3,2,1,0:T(8,128)(2,1)S(1)} %bitcast.9, ...), custom_call_target="tpu_custom_call", output_to_operand_aliasing={{0}: (1, {})} | custom-call | flops 16000000000 | bytes 4000000 | tf_op jit(solution)/shard_map/forward/pallas_call | solution.py:273
  43.9 24.5 %all_to_all.15.gathered = f32[128,8,128]{2,1,0:T(8,128)S(1)} all-to-all(f32[128,8,128]{2,1,0:T(8,128)S(1)} %get-tuple-element.51), channel_id=1, replica_groups=mesh['slab'=32,'sub'=4] {'slab','sub'}, dimensions={0} | all-to-all | bytes 1048576 | tf_op jit(solution)/shard_map/all_to_all | solution.py:744
  68.4 0.0 copy-done.5
  68.4 5.8 %slopes.1 = (bf16[18,18,96,128]{3,2,1,0:T(8,128)(2,1)S(1)}, bf16[48,8,8,96,128]{4,3,2,1,0:T(8,128)(2,1)}, bf16[16,96,128]{2,1,0:T(8,128)(2,1)S(1)}, bf16[16,96,1...) custom-call(s32[9]{0:T(128)S(1)} %copy-done.5, ...), custom_call_target="tpu_custom_call" | custom-call | flops 30000000 | bytes 12000000 | tf_op jit(solution)/shard_map/slopes/pallas_call | solution.py:406
  74.2 1.9 %collective-permute-start.6 = (bf16[16,96,128]{2,1,0:T(8,128)(2,1)S(1)}, bf16[16,96,128]{2,1,0:T(8,128)(2,1)S(1)}, u32[]{:S(2)}, u32[]{:S(2)}) collective-permute-start(bf16[16,96,128]{2,1,0:T(8,128)(2,1)S(1)} %get-tuple-element.57), channel_id=1, source_target_pairs={{0,4},{4,8},{8,12},{12,16},{16,20},{20,24},{24,28},{28,32},{32,36}... | collective-permute-start | bytes 1179656 | tf_op jit(solution)/shard_map/ppermute | solution.py:727
  76.1 2.4 %collective-permute-start.7 = (bf16[16,96,128]{2,1,0:T(8,128)(2,1)S(1)}, bf16[16,96,128]{2,1,0:T(8,128)(2,1)S(1)}, u32[]{:S(2)}, u32[]{:S(2)}) collective-permute-start(bf16[16,96,128]{2,1,0:T(8,128)(2,1)S(1)} %get-tuple-element.58), channel_id=1, source_target_pairs={{4,0},{8,4},{12,8},{16,12},{20,16},{24,20},{28,24},{32,28},{36,32}... | collective-permute-start | bytes 1179656 | tf_op jit(solution)/shard_map/ppermute | solution.py:728
  78.5 2.2 %build_whole.1.field = bf16[18,18,96,128]{3,2,1,0:T(8,128)(2,1)S(1)} custom-call(s32[9]{0:T(128)S(1)} %copy-done.5, bf16[16,16,96,128]{3,2,1,0:T(8,128)(2,1)S(1)} %copy-done, s32[16,16,128]{2,1,0:T(8,128)S(1)} %copy-done.1, bf16[16,96,128]{2,1,0:T(8,128)(2,1)S(1)} %collective-permute-done.xm.refs_0_, ...), custom_call_target="tpu_custom_call" | custom-call | flops 3000000 | bytes 6000000 | tf_op jit(solution)/shard_map/build_whole/pallas_call | solution.py:182
  80.8 0.0 collective-permute-done.6.xm
  80.8 4.4 %collective-permute-done.7.xp = bf16[16,96,128]{2,1,0:T(8,128)(2,1)S(1)} collective-permute-done((bf16[16,96,128]{2,1,0:T(8,128)(2,1)S(1)}, bf16[16,96,128]{2,1,0:T(8,128)(2,1)S(1)}, u32[]{:S(2)}, u32[]{:S(2)}) %collective-permute-start.7) | collective-permute-done | bytes 393248 | tf_op jit(solution)/shard_map/ppermute | solution.py:728
  85.2 15.1 %weight_terms.1 = f32[2048,128]{1,0:T(8,128)} custom-call(s32[9]{0:T(128)S(1)} %copy-done.5, bf16[18,18,96,128]{3,2,1,0:T(8,128)(2,1)S(1)} %build_whole.1.field, bf16[18,18,96,128]{3,2,1,0:T(8,128)(2,1)S(1)} %get-tuple-element.75.slope), custom_call_target="tpu_custom_call" | custom-call | flops 16000000000 | bytes 2000000 | tf_op jit(solution)/shard_map/weight_terms/pallas_call | solution.py:506
  100.3 6.5 %all-to-all-start.1 = ((f32[128,16,128]{2,1,0:T(8,128)}), f32[128,16,128]{2,1,0:T(8,128)S(1)}, u32[]{:S(2)}, u32[]{:S(2)}) async-start(f32[128,16,128]{2,1,0:T(8,128)} %bitcast.2), calls=%async_computation.1 | async-start | bytes 2097152 | tf_op jit(solution)/shard_map/all_to_all | solution.py:744
  106.8 0.7 stitch.1
  107.4 0.0 copy-start.3
  107.5 0.8 copy-done.3
  108.2 3.3 %collective-permute-start.8 = (bf16[18,96,128]{2,1,0:T(8,128)(2,1)}, bf16[18,96,128]{2,1,0:T(8,128)(2,1)S(1)}, u32[]{:S(2)}, u32[]{:S(2)}) collective-permute-start(bf16[18,96,128]{2,1,0:T(8,128)(2,1)} %get-tuple-element.70), channel_id=1, source_target_pairs={{0,1},{1,2},{2,3},{4,5},{5,6},{6,7},{8,9},{9,10},{10,11},{12,13},{... | collective-permute-start | bytes 1327112 | tf_op jit(solution)/shard_map/ppermute | solution.py:738
  111.5 1.3 collective-permute-start.9
  112.8 3.5 %blanks.1 = (bf16[16,16,96,128]{3,2,1,0:T(8,128)(2,1)}, bf16[16,16,96,128]{3,2,1,0:T(8,128)(2,1)}) custom-call(s32[9]{0:T(128)S(1)} %copy-done.5), custom_call_target="tpu_custom_call" | custom-call | flops 1000 | bytes 8000000 | tf_op jit(solution)/shard_map/blanks/pallas_call | solution.py:334
  116.4 5.1 %normed_values.1 = bf16[16,16,96,128]{3,2,1,0:T(8,128)(2,1)} custom-call(s32[9]{0:T(128)S(1)} %copy-done.5, f32[8,128]{1,0:T(8,128)S(1)} %get-tuple-element.54.totals, f32[8,128]{1,0:T(8,128)S(1)} %select_maximum_fusion.params, f32[24,8,8,96,128]{4,3,2,1,0:T(8,128)} %get-tuple-element.53.conv, ...), custom_call_target="tpu_custom_call", output_to_operand_aliasing={{}: (5, {})} | custom-call | flops 30000000 | bytes 8000000 | tf_op jit(solution)/shard_map/normed_values/pallas_call | solution.py:452
  121.5 0.5 slice_bitcast_fusion
  122.0 5.0 %all-to-all-done.1.parts = f32[128,16,128]{2,1,0:T(8,128)S(1)} async-done(((f32[128,16,128]{2,1,0:T(8,128)}), f32[128,16,128]{2,1,0:T(8,128)S(1)}, u32[]{:S(2)}, u32[]{:S(2)}) %all-to-all-start.1) | async-done | bytes 1048608 | tf_op jit(solution)/shard_map/all_to_all | solution.py:744
  127.0 1.0 share.1
  128.0 5.9 %all-to-all-start.2 = ((bf16[128,16,128]{2,1,0:T(8,128)(2,1)}), bf16[128,16,128]{2,1,0:T(8,128)(2,1)S(1)}, u32[]{:S(2)}, u32[]{:S(2)}) async-start(bf16[128,16,128]{2,1,0:T(8,128)(2,1)} %share.1), calls=%async_computation.2 | async-start | bytes 1048576 | tf_op jit(solution)/shard_map/all_to_all | solution.py:744
  133.9 0.0 collective-permute-done.8.ym
  133.9 0.0 collective-permute-done.9.yp
  133.9 17.4 %backward.1 = bf16[16,16,96,128]{3,2,1,0:T(8,128)(2,1)} custom-call(s32[9]{0:T(128)S(1)} %copy-done.5, bf16[48,8,8,96,128]{4,3,2,1,0:T(8,128)(2,1)} %get-tuple-element.56.kept, s32[16,16,128]{2,1,0:T(8,128)S(1)} %copy-done.1, bf16[16,96,128]{2,1,0:T(8,128)(2,1)S(1)} %collective-permute-done.6.xm, ...), custom_call_target="tpu_custom_call", output_to_operand_aliasing={{}: (8, {})} | custom-call | flops 16000000000 | bytes 5000000 | tf_op jit(solution)/shard_map/backward/pallas_call | solution.py:609
  151.3 0.0 all-to-all-done.2
  151.3 1.4 arrange.1
  (2 shorter events, 0.0 us)
Async XLA Ops:
  0.6 23.9 %copy-start = (bf16[16,16,96,128]{3,2,1,0:T(8,128)(2,1)S(1)}, bf16[16,16,96,128]{3,2,1,0:T(8,128)(2,1)}, u32[]{:S(2)}) copy-start(bf16[16,16,96,128]{3,2,1,0:T(8,128)(2,1)} %features.5) | copy-start | bytes 18874372
  0.6 23.9 %copy-start.1 = (s32[16,16,128]{2,1,0:T(8,128)S(1)}, s32[16,16,128]{2,1,0:T(8,128)}, u32[]{:S(2)}) copy-start(s32[16,16,128]{2,1,0:T(8,128)} %mask.13) | copy-start | bytes 393220
  0.7 23.3 %copy-start.7 = (f32[96]{0:T(128)S(1)}, f32[96]{0:T(128)}, u32[]{:S(2)}) copy-start(f32[96]{0:T(128)} %param.9) | copy-start | bytes 1156
  0.7 23.3 %copy-start.6 = (f32[96]{0:T(128)S(1)}, f32[96]{0:T(128)}, u32[]{:S(2)}) copy-start(f32[96]{0:T(128)} %param.10) | copy-start | bytes 1156
  0.7 23.3 %copy-start.2 = (bf16[27,96,96]{2,1,0:T(8,128)(2,1)S(1)}, bf16[27,96,96]{2,1,0:T(8,128)(2,1)}, u32[]{:S(2)}) copy-start(bf16[27,96,96]{2,1,0:T(8,128)(2,1)} %weight.1) | copy-start | bytes 1492996
  4.8 11.3 %collective-permute-start = (bf16[16,96,128]{2,1,0:T(8,128)(2,1)}, bf16[16,96,128]{2,1,0:T(8,128)(2,1)S(1)}, u32[]{:S(2)}, u32[]{:S(2)}) collective-permute-start(bf16[16,96,128]{2,1,0:T(8,128)(2,1)} %get-tuple-element.44), channel_id=1, source_target_pairs={{0,4},{4,8},{8,12},{12,16},{16,20},{20,24},{24,28},{28,32},{32,36}... | collective-permute-start | bytes 1179656 | tf_op jit(solution)/shard_map/ppermute | solution.py:727
  9.7 9.6 %collective-permute-start.1 = (bf16[16,96,128]{2,1,0:T(8,128)(2,1)}, bf16[16,96,128]{2,1,0:T(8,128)(2,1)S(1)}, u32[]{:S(2)}, u32[]{:S(2)}) collective-permute-start(bf16[16,96,128]{2,1,0:T(8,128)(2,1)} %get-tuple-element.45), channel_id=1, source_target_pairs={{4,0},{8,4},{12,8},{16,12},{20,16},{24,20},{28,24},{32,28},{36,32}... | collective-permute-start | bytes 1179656 | tf_op jit(solution)/shard_map/ppermute | solution.py:728
  11.7 15.5 %collective-permute-start.2 = (bf16[16,96,128]{2,1,0:T(8,128)(2,1)}, bf16[16,96,128]{2,1,0:T(8,128)(2,1)S(1)}, u32[]{:S(2)}, u32[]{:S(2)}) collective-permute-start(bf16[16,96,128]{2,1,0:T(8,128)(2,1)} %get-tuple-element.46), channel_id=1, source_target_pairs={{0,1},{1,2},{2,3},{4,5},{5,6},{6,7},{8,9},{9,10},{10,11},{12,13},{... | collective-permute-start | bytes 1179656 | tf_op jit(solution)/shard_map/ppermute | solution.py:738
  14.8 12.3 %collective-permute-start.3 = (bf16[16,96,128]{2,1,0:T(8,128)(2,1)}, bf16[16,96,128]{2,1,0:T(8,128)(2,1)S(1)}, u32[]{:S(2)}, u32[]{:S(2)}) collective-permute-start(bf16[16,96,128]{2,1,0:T(8,128)(2,1)} %get-tuple-element.47), channel_id=1, source_target_pairs={{1,0},{2,1},{3,2},{5,4},{6,5},{7,6},{9,8},{10,9},{11,10},{13,12},{... | collective-permute-start | bytes 1179656 | tf_op jit(solution)/shard_map/ppermute | solution.py:739
  19.5 7.7 %collective-permute-start.4 = (bf16[2,96,128]{2,1,0:T(8,128)(2,1)S(1)}, bf16[2,96,128]{2,1,0:T(8,128)(2,1)S(1)}, u32[]{:S(2)}, u32[]{:S(2)}) collective-permute-start(bf16[2,96,128]{2,1,0:T(8,128)(2,1)S(1)} %get-tuple-element.48), channel_id=1, source_target_pairs={{0,1},{1,2},{2,3},{4,5},{5,6},{6,7},{8,9},{9,10},{10,11},{12,13},{... | collective-permute-start | bytes 147464 | tf_op jit(solution)/shard_map/ppermute | solution.py:738
  22.6 4.8 %collective-permute-start.5 = (bf16[2,96,128]{2,1,0:T(8,128)(2,1)S(1)}, bf16[2,96,128]{2,1,0:T(8,128)(2,1)S(1)}, u32[]{:S(2)}, u32[]{:S(2)}) collective-permute-start(bf16[2,96,128]{2,1,0:T(8,128)(2,1)S(1)} %get-tuple-element.49), channel_id=1, source_target_pairs={{1,0},{2,1},{3,2},{5,4},{6,5},{7,6},{9,8},{10,9},{11,10},{13,12},{... | collective-permute-start | bytes 147464 | tf_op jit(solution)/shard_map/ppermute | solution.py:739
  24.0 3.5 %slice-start = ((s8[6291456]{0:T(1024)(128)(4,1)}), s8[4194304]{0:T(1024)(128)(4,1)S(1)}, s32[]{:S(2)}) async-start(s8[6291456]{0:T(1024)(128)(4,1)} %bitcast.8), calls=%async_computation.3 | async-start | bytes 8388608
  24.5 0.9 copy-start.4
  25.5 2.0 %slice-start.1 = ((s8[6291456]{0:T(1024)(128)(4,1)}), s8[2097152]{0:T(1024)(128)(4,1)S(1)}, s32[]{:S(2)}) async-start(s8[6291456]{0:T(1024)(128)(4,1)} %bitcast.8), calls=%async_computation.4 | async-start | bytes 4194304
  27.5 40.9 %copy-start.5 = (s32[9]{0:T(128)S(1)}, s32[9]{0:T(128)}, u32[]{:S(2)}) copy-start(s32[9]{0:T(128)} %get-tuple-element.41.meta) | copy-start | bytes 112
  74.2 6.6 %collective-permute-start.6 = (bf16[16,96,128]{2,1,0:T(8,128)(2,1)S(1)}, bf16[16,96,128]{2,1,0:T(8,128)(2,1)S(1)}, u32[]{:S(2)}, u32[]{:S(2)}) collective-permute-start(bf16[16,96,128]{2,1,0:T(8,128)(2,1)S(1)} %get-tuple-element.57), channel_id=1, source_target_pairs={{0,4},{4,8},{8,12},{12,16},{16,20},{20,24},{24,28},{28,32},{32,36}... | collective-permute-start | bytes 1179656 | tf_op jit(solution)/shard_map/ppermute | solution.py:727
  76.1 9.1 %collective-permute-start.7 = (bf16[16,96,128]{2,1,0:T(8,128)(2,1)S(1)}, bf16[16,96,128]{2,1,0:T(8,128)(2,1)S(1)}, u32[]{:S(2)}, u32[]{:S(2)}) collective-permute-start(bf16[16,96,128]{2,1,0:T(8,128)(2,1)S(1)} %get-tuple-element.58), channel_id=1, source_target_pairs={{4,0},{8,4},{12,8},{16,12},{20,16},{24,20},{28,24},{32,28},{36,32}... | collective-permute-start | bytes 1179656 | tf_op jit(solution)/shard_map/ppermute | solution.py:728
  100.3 26.7 %all-to-all-start.1 = ((f32[128,16,128]{2,1,0:T(8,128)}), f32[128,16,128]{2,1,0:T(8,128)S(1)}, u32[]{:S(2)}, u32[]{:S(2)}) async-start(f32[128,16,128]{2,1,0:T(8,128)} %bitcast.2), calls=%async_computation.1 | async-start | bytes 2097152 | tf_op jit(solution)/shard_map/all_to_all | solution.py:744
  107.4 0.8 copy-start.3
  108.2 25.7 %collective-permute-start.8 = (bf16[18,96,128]{2,1,0:T(8,128)(2,1)}, bf16[18,96,128]{2,1,0:T(8,128)(2,1)S(1)}, u32[]{:S(2)}, u32[]{:S(2)}) collective-permute-start(bf16[18,96,128]{2,1,0:T(8,128)(2,1)} %get-tuple-element.70), channel_id=1, source_target_pairs={{0,1},{1,2},{2,3},{4,5},{5,6},{6,7},{8,9},{9,10},{10,11},{12,13},{... | collective-permute-start | bytes 1327112 | tf_op jit(solution)/shard_map/ppermute | solution.py:738
  111.5 22.4 %collective-permute-start.9 = (bf16[18,96,128]{2,1,0:T(8,128)(2,1)}, bf16[18,96,128]{2,1,0:T(8,128)(2,1)S(1)}, u32[]{:S(2)}, u32[]{:S(2)}) collective-permute-start(bf16[18,96,128]{2,1,0:T(8,128)(2,1)} %copy-done.3), channel_id=1, source_target_pairs={{1,0},{2,1},{3,2},{5,4},{6,5},{7,6},{9,8},{10,9},{11,10},{13,12},{... | collective-permute-start | bytes 1327112 | tf_op jit(solution)/shard_map/ppermute | solution.py:739
  128.0 23.3 %all-to-all-start.2 = ((bf16[128,16,128]{2,1,0:T(8,128)(2,1)}), bf16[128,16,128]{2,1,0:T(8,128)(2,1)S(1)}, u32[]{:S(2)}, u32[]{:S(2)}) async-start(bf16[128,16,128]{2,1,0:T(8,128)(2,1)} %share.1), calls=%async_computation.2 | async-start | bytes 1048576 | tf_op jit(solution)/shard_map/all_to_all | solution.py:744

commit v4 on v3

--- a/solution.py
+++ b/solution.py
@@ -46,12 +46,14 @@
     return mask[x, pl.ds(y0, BRICK), :].astype(F32)
 
 
-def each_row(occupied, step):
+def each_row(occupied, step, unroll=1):
     for slot in range(SLOTS):
 
         @pl.when(slot < occupied)
         def _():
-            lax.fori_loop(0, BRICK, lambda x, carry: (step(slot, x), carry)[1], 0)
+            lax.fori_loop(
+                0, BRICK, lambda x, carry: (step(slot, x), carry)[1], 0, unroll=unroll
+            )
 
 
 def clear_pillars(meta, field):
@@ -69,35 +71,43 @@
             lax.fori_loop(0, BRICK, clear, 0)
 
 
-def fill_rims(field, rims, sems):
-    xm, xp, ym, yp = rims[:4]
+def near_ends(meta):
+    return 1 - meta[9], 1 - meta[10]
+
+
+def fill_rims(meta, field, rims, sems):
+    x_end, y_end = near_ends(meta)
     side = pl.ds(1, 16) if len(rims) > 4 else pl.ds(0, 18)
-    copies = [
-        pltpu.make_async_copy(xm, field.at[0, pl.ds(1, 16)], sems.at[0]),
-        pltpu.make_async_copy(xp, field.at[17, pl.ds(1, 16)], sems.at[1]),
-        pltpu.make_async_copy(ym, field.at[side, 0], sems.at[2]),
-        pltpu.make_async_copy(yp, field.at[side, 17], sems.at[3]),
-    ]
-    for which, corners in enumerate(rims[4:]):
-        for end in range(2):
-            copies.append(
-                pltpu.make_async_copy(
-                    corners.at[end], field.at[17 * end, 17 * which], sems.at[4 + 2 * which + end]
-                )
-            )
+    copies = []
+    for turn in range(2):
+        row = 17 * (x_end if turn == 0 else 1 - x_end)
+        col = 17 * (y_end if turn == 0 else 1 - y_end)
+        moves = [
+            (rims[turn], field.at[row, pl.ds(1, 16)]),
+            (rims[2 + turn], field.at[side, col]),
+        ]
+        if len(rims) > 4:
+            moves += [(rims[4 + turn].at[end], field.at[17 * end, col]) for end in range(2)]
+        for source, target in moves:
+            copies.append(pltpu.make_async_copy(source, target, sems.at[len(copies)]))
     for copy in copies:
         copy.start()
     return copies
 
 
-def take_rims(field, rims, sems):
+def take_rims(meta, field, rims, sems):
+    x_end, y_end = near_ends(meta)
     inner = pl.ds(1, 16)
-    copies = [
-        pltpu.make_async_copy(field.at[1, inner], rims[0], sems.at[0]),
-        pltpu.make_async_copy(field.at[16, inner], rims[1], sems.at[1]),
-        pltpu.make_async_copy(field.at[inner, 1], rims[2].at[inner], sems.at[2]),
-        pltpu.make_async_copy(field.at[inner, 16], rims[3].at[inner], sems.at[3]),
-    ]
+    copies = []
+    for turn in range(2):
+        row = 1 + 15 * (x_end if turn == 0 else 1 - x_end)
+        col = 1 + 15 * (y_end if turn == 0 else 1 - y_end)
+        copies += [
+            pltpu.make_async_copy(field.at[row, inner], rims[turn], sems.at[turn]),
+            pltpu.make_async_copy(
+                field.at[inner, col], rims[2 + turn].at[inner], sems.at[2 + turn]
+            ),
+        ]
     for copy in copies:
         copy.start()
     for copy in copies:
@@ -108,13 +118,17 @@
 LONG = jax.ShapeDtypeStruct((18, CHANS, DEPTH), BF16)
 
 
-def prepare_kernel(features, mask, x_low, x_high, y_low, y_high, meta, sem_in):
-    faces, sides = (x_low, x_high), (y_low, y_high)
+def prepare_kernel(features, mask, x_even, x_odd, y_even, y_odd, meta, sem_in):
+    faces, sides = (x_even, x_odd), (y_even, y_odd)
+    meta[9] = lax.rem(lax.axis_index("slab"), 2)
+    meta[10] = lax.rem(lax.axis_index("sub"), 2)
+    x_end, y_end = near_ends(meta)
+    rows, cols = (15 * x_end, 15 - 15 * x_end), (15 * y_end, 15 - 15 * y_end)
     loads = [
-        pltpu.make_async_copy(features.at[0], x_low, sem_in.at[0]),
-        pltpu.make_async_copy(features.at[15], x_high, sem_in.at[1]),
-        pltpu.make_async_copy(features.at[:, 0], y_low, sem_in.at[2]),
-        pltpu.make_async_copy(features.at[:, 15], y_high, sem_in.at[3]),
+        pltpu.make_async_copy(features.at[rows[0]], x_even, sem_in.at[0]),
+        pltpu.make_async_copy(features.at[rows[1]], x_odd, sem_in.at[1]),
+        pltpu.make_async_copy(features.at[:, cols[0]], y_even, sem_in.at[2]),
+        pltpu.make_async_copy(features.at[:, cols[1]], y_odd, sem_in.at[3]),
     ]
     for load in loads:
         load.start()
@@ -139,12 +153,12 @@
     for which in range(2):
         loads[which].wait()
         for col in range(16):
-            keep = jnp.broadcast_to(mask[15 * which, col : col + 1, :], (CHANS, DEPTH))
+            keep = jnp.broadcast_to(mask[rows[which], col : col + 1, :], (CHANS, DEPTH))
             faces[which][col] = faces[which][col] * keep.astype(F32).astype(BF16)
     for which in range(2):
         loads[2 + which].wait()
         for row in range(16):
-            keep = jnp.broadcast_to(mask[row, 15 * which : 15 * which + 1, :], (CHANS, DEPTH))
+            keep = jnp.broadcast_to(mask[row, pl.ds(cols[which], 1), :], (CHANS, DEPTH))
             sides[which][row] = sides[which][row] * keep.astype(F32).astype(BF16)
 
 
@@ -152,7 +166,7 @@
     return pl.pallas_call(
         prepare_kernel,
         name="prepare",
-        out_shape=(RIM, RIM, RIM, RIM, jax.ShapeDtypeStruct((9,), jnp.int32)),
+        out_shape=(RIM, RIM, RIM, RIM, jax.ShapeDtypeStruct((11,), jnp.int32)),
         in_specs=[HBM, VMEM],
         out_specs=(VMEM, VMEM, VMEM, VMEM, SMEM),
         scratch_shapes=[pltpu.SemaphoreType.DMA((4,))],
@@ -163,7 +177,7 @@
 
 def build_kernel(meta, features, mask, *refs):
     *rims, field, sem_rim = refs
-    copies = fill_rims(field, rims, sem_rim) if rims else []
+    copies = fill_rims(meta, field, rims, sem_rim) if rims else []
 
     def mask_row(slot, x):
         x0, y0 = corner(meta, slot)
@@ -224,7 +238,7 @@
     def conv_copy(slot, x):
         return pltpu.make_async_copy(convs.at[slot, x], conv_out.at[slot, x], sem_out.at[slot, x])
 
-    rims = fill_rims(field, (xm, xp, ym, yp, cm, cp), sem_rim)
+    rims = fill_rims(meta, field, (xm, xp, ym, yp, cm, cp), sem_rim)
     for copy in rims:
         copy.wait()
     sums[...] = jnp.zeros(sums.shape, F32)
@@ -248,7 +262,7 @@
         sums[4, 0:BRICK] = sums[4, 0:BRICK] + active
         conv_copy(slot, x).start()
 
-    each_row(meta[8], row)
+    each_row(meta[8], row, unroll=2)
 
     ones = jnp.ones((8, DEPTH), F32)
     rows = []
@@ -355,7 +369,7 @@
 
 
 def slope_kernel(
-    meta, gathered, params, conv, grads, mask, field, kept, x_low, x_high, y_low, y_high, sums_out, totals_out, convs, sem_conv, sem_kept, sem_rim
+    meta, gathered, params, conv, grads, mask, field, kept, x_even, x_odd, y_even, y_odd, sums_out, totals_out, convs, sem_conv, sem_kept, sem_rim
 ):
     occupied = meta[8]
 
@@ -396,7 +410,7 @@
         keep_row(slot, x).start()
 
     each_row(occupied, row)
-    take_rims(field, (x_low, x_high, y_low, y_high), sem_rim)
+    take_rims(meta, field, (x_even, x_odd, y_even, y_odd), sem_rim)
     each_row(occupied, lambda slot, x: keep_row(slot, x).wait())
 
 
@@ -496,7 +510,7 @@
             preferred_element_type=F32,
         )
 
-    each_row(meta[8], row)
+    each_row(meta[8], row, unroll=2)
     for tile in range(TILES):
         out[ROWS * tile : ROWS * (tile + 1)] = acc[:, DEPTH * tile : DEPTH * (tile + 1)]
     out[ROWS * TILES :] = jnp.zeros((2048 - ROWS * TILES, DEPTH), F32)
@@ -572,7 +586,7 @@
                     sem_in.at[slot],
                 ).start()
 
-    rims = fill_rims(field, (xm, xp, ym, yp), sem_rim)
+    rims = fill_rims(meta, field, (xm, xp, ym, yp), sem_rim)
     clear_pillars(meta, field)
     for copy in rims:
         copy.wait()
@@ -601,7 +615,7 @@
             results[slot, x, col] = (outs[col] * active[col : col + 1]).astype(BF16)
         copy(slot, x).start()
 
-    each_row(occupied, row)
+    each_row(occupied, row, unroll=2)
     each_row(occupied, lambda slot, x: copy(slot, x).wait())
 
 
@@ -625,58 +639,49 @@
     )(meta, kept, voxel_mask, *rims, taps, base)
 
 
-def corner_kernel(xm, xp, upper, lower, sems):
-    copies = [
-        pltpu.make_async_copy(xm.at[15], upper.at[0], sems.at[0]),
-        pltpu.make_async_copy(xp.at[15], upper.at[1], sems.at[1]),
-        pltpu.make_async_copy(xm.at[0], lower.at[0], sems.at[2]),
-        pltpu.make_async_copy(xp.at[0], lower.at[1], sems.at[3]),
-    ]
+def corner_kernel(stride, meta, *refs):
+    x_even, x_odd, even, odd, sems = refs[-5:]
+    x_end, y_end = near_ends(meta)
+    copies = []
+    for target, line in ((even, 15 * y_end), (odd, 15 - 15 * y_end)):
+        for source, end in ((x_even, x_end), (x_odd, 1 - x_end)):
+            copies.append(
+                pltpu.make_async_copy(
+                    source.at[line], target.at[stride * end], sems.at[len(copies)]
+                )
+            )
     for copy in copies:
         copy.start()
     for copy in copies:
         copy.wait()
 
 
-def corners_of(xm, xp):
+def corners_of(meta, x_even, x_odd):
     pair = jax.ShapeDtypeStruct((2, CHANS, DEPTH), BF16)
     return pl.pallas_call(
-        corner_kernel,
+        functools.partial(corner_kernel, 1),
         name="corners",
         out_shape=(pair, pair),
-        in_specs=[ANY, ANY],
+        in_specs=[SMEM, ANY, ANY],
         out_specs=(ANY, ANY),
         scratch_shapes=[pltpu.SemaphoreType.DMA((4,))],
         compiler_params=params_of(1),
         cost_estimate=cost(1_000, 200_000),
-    )(xm, xp)
-
-
-def stitch_kernel(high, low, xm, xp, upper, lower, sems):
-    copies = [
-        pltpu.make_async_copy(xm.at[15], upper.at[0], sems.at[0]),
-        pltpu.make_async_copy(xp.at[15], upper.at[17], sems.at[1]),
-        pltpu.make_async_copy(xm.at[0], lower.at[0], sems.at[2]),
-        pltpu.make_async_copy(xp.at[0], lower.at[17], sems.at[3]),
-    ]
-    for copy in copies:
-        copy.start()
-    for copy in copies:
-        copy.wait()
-
-
-def stitch(high, low, xm, xp):
-    return pl.pallas_call(
-        stitch_kernel,
+    )(meta, x_even, x_odd)
+
+
+def stitch(meta, y_even, y_odd, x_even, x_odd):
+    return pl.pallas_call(
+        functools.partial(corner_kernel, 17),
         name="stitch",
         out_shape=(LONG, LONG),
-        in_specs=[ANY, ANY, ANY, ANY],
+        in_specs=[SMEM, ANY, ANY, ANY, ANY],
         out_specs=(ANY, ANY),
         scratch_shapes=[pltpu.SemaphoreType.DMA((4,))],
-        input_output_aliases={0: 0, 1: 1},
+        input_output_aliases={1: 0, 2: 1},
         compiler_params=params_of(1),
         cost_estimate=cost(1_000, 200_000),
-    )(high, low, xm, xp)
+    )(meta, y_even, y_odd, x_even, x_odd)
 
 
 def taps_kernel(weight, ahead, back):
@@ -722,22 +727,13 @@
     )(weight)
 
 
-def exchange_slabs(x_low, x_high):
-    slabs = lax.axis_size("slab")
-    xm = lax.ppermute(x_high, "slab", [(i, i + 1) for i in range(slabs - 1)])
-    xp = lax.ppermute(x_low, "slab", [(i + 1, i) for i in range(slabs - 1)])
-    return xm, xp
-
-
-def exchange_subs(xm, xp, y_low, y_high):
-    return shift_subs(*stitch(y_high, y_low, xm, xp))
-
-
-def shift_subs(upper, lower):
-    subs = lax.axis_size("sub")
-    ym = lax.ppermute(upper, "sub", [(i, i + 1) for i in range(subs - 1)])
-    yp = lax.ppermute(lower, "sub", [(i + 1, i) for i in range(subs - 1)])
-    return ym, yp
+def exchange(even, odd, axis):
+    count = lax.axis_size(axis)
+    meets = [(i, i + 1) for i in range(1, count - 1, 2)]
+    return (
+        lax.ppermute(even, axis, [(i, i ^ 1) for i in range(count)]),
+        lax.ppermute(odd, axis, meets + [(j, i) for i, j in meets]),
+    )
 
 
 def swap_all(pieces):
@@ -745,30 +741,34 @@
 
 
 def body(features, voxel_mask, weight, norm_gain, norm_bias, out_grad):
-    x_low, x_high, y_low, y_high, meta = prepare(features, voxel_mask)
-    xm, xp = exchange_slabs(x_low, x_high)
-    ym, yp = shift_subs(y_high, y_low)
-    cm, cp = shift_subs(*corners_of(xm, xp))
-    rims = (xm, xp, ym, yp, cm, cp)
+    x_even, x_odd, y_even, y_odd, meta = prepare(features, voxel_mask)
+    x_rims = exchange(x_even, x_odd, "slab")
+    y_rims = exchange(y_even, y_odd, "sub")
     field = build(meta, features, voxel_mask)
     ahead, back = tap_kernels(weight)
     params = jnp.pad(jnp.stack([norm_gain, norm_bias]), ((0, 6), (0, DEPTH - CHANS)))
-    field, params, back = lax.optimization_barrier((field, params, back))
+    x_rims, field, ahead, back, params = lax.optimization_barrier(
+        (x_rims, field, ahead, back, params)
+    )
+    corners = exchange(*corners_of(meta, *x_rims), "sub")
+    rims = (*x_rims, *y_rims, *corners)
     conv, stats = forward(meta, field, out_grad, voxel_mask, rims, ahead)
-    slope, kept, x_low, x_high, y_low, y_high, sums, totals = slopes(
+    slope, kept, x_even, x_odd, y_even, y_odd, sums, totals = slopes(
         meta, swap_all(stats), params, conv, out_grad, voxel_mask
     )
-    xm, xp = exchange_slabs(x_low, x_high)
-    rims, x_low = lax.optimization_barrier((rims, x_low))
+    x_rims = exchange(x_even, x_odd, "slab")
+    rims, x_even = lax.optimization_barrier((rims, x_even))
     field = build(meta, features, voxel_mask, rims)
-    xm, xp, slope, field = lax.optimization_barrier((xm, xp, slope, field))
-    ym, yp = exchange_subs(xm, xp, y_low, y_high)
+    normed_base, feature_base = blanks(meta)
+    x_rims, slope, field, normed_base, feature_base = lax.optimization_barrier(
+        (x_rims, slope, field, normed_base, feature_base)
+    )
+    y_rims = exchange(*stitch(meta, y_even, y_odd, *x_rims), "sub")
     terms = weight_terms(meta, field, slope)
     parts = swap_all(terms.reshape(DEVICES, 16, DEPTH))
-    normed_base, feature_base = blanks(meta)
     normed_out = normed_values(meta, totals, params, conv, voxel_mask, normed_base)
     shared = swap_all(share(parts))
-    feature_grad = backward(meta, kept, voxel_mask, (xm, xp, ym, yp), back, feature_base)
+    feature_grad = backward(meta, kept, voxel_mask, (*x_rims, *y_rims), back, feature_base)
     weight_grad = arrange(shared.reshape(2048, DEPTH))
     return (normed_out, feature_grad, weight_grad, sums[0, :CHANS], sums[1, :CHANS])
 

time: 153 us -> 137 us (0.90)
  the two profiles are of different devices: /device:TPU:1 before, /device:TPU:3 now
where the time goes in v4:
time: 137 us; the launch traced here: 136 us
  Pallas kernels  69.6 us (51%)
  starting transfers between devices  27 us (20%)
  blocking collectives  23.6 us (17%)
  waiting for transfers between devices  11.9 us (9%)
  local copies, waits for them, and re-layouts  3.32 us (2%)
    all_to_all x1, blocking collectives, swap_all(): return lax.all_to_all(pieces, ('slab', 'sub'), 0, 0, tiled=True)  23.6 us
    pallas_call x1, Pallas kernels, backward(): pl.pallas_call(backward_kernel, name='backward', out_shape=jax.ShapeDtype...  15.2 us
    ppermute x5, starting transfers between devices, exchange(): lax.ppermute(odd, axis, meets + [(j, i) for i, j in meets])  14.9 us
    pallas_call x1, Pallas kernels, forward(): pl.pallas_call(forward_kernel, name='forward', out_shape=(jax.ShapeDtypeS...  14.3 us
    pallas_call x1, Pallas kernels, weight_terms(): pl.pallas_call(weight_kernel, name='weight_terms', out_shape=jax.ShapeDty...  13.2 us
    all_to_all x2, starting transfers between devices, swap_all(): return lax.all_to_all(pieces, ('slab', 'sub'), 0, 0, tiled=True)  10.7 us
    all_to_all x2, waiting for transfers between devices, swap_all(): return lax.all_to_all(pieces, ('slab', 'sub'), 0, 0, tiled=True)  7.58 us
    pallas_call x1, Pallas kernels, slopes(): pl.pallas_call(slope_kernel, name='slopes', out_shape=(jax.ShapeDtypeStru...  5.56 us
  transfers between devices with their start and end apart: 12, of which 5 were waited for; matrix products, arithmetic and copies ran while one was open for 0% of the time, Pallas kernels for 23%

profile of v4, /device:TPU:3, one launch (start us, length us, event | category | flops | bytes accessed | tf_op | source)
XLA Modules:
  0.0 136.4 jit_solution(17965517426287429071)
XLA Ops:
  0.6 0.0 copy-start
  0.6 0.0 copy-start.1
  0.7 4.1 %prepare.1 = (bf16[16,96,128]{2,1,0:T(8,128)(2,1)}, bf16[16,96,128]{2,1,0:T(8,128)(2,1)}, bf16[16,96,128]{2,1,0:T(8,128)(2,1)}, bf16[16,96,128]{2,1,0:T(8,128)(2,1)}, s32[11]{0:T(128)}) custom-call(bf16[16,16,96,128]{3,2,1,0:T(8,128)(2,1)} %features.5, s32[16,16,128]{2,1,0:T(8,128)} %mask.13), custom_call_target="tpu_custom_call" | custom-call | flops 3000000 | bytes 3000000 | tf_op jit(solution)/shard_map/prepare/pallas_call | solution.py:166
  4.7 0.8 collective-permute-start
  5.5 3.4 %collective-permute-start.1 = (bf16[16,96,128]{2,1,0:T(8,128)(2,1)}, bf16[16,96,128]{2,1,0:T(8,128)(2,1)S(1)}, u32[]{:S(2)}, u32[]{:S(2)}) collective-permute-start(bf16[16,96,128]{2,1,0:T(8,128)(2,1)} %get-tuple-element.48), channel_id=1, source_target_pairs={{4,8},{12,16},{20,24},{28,32},{36,40},{44,48},{52,56},{60,64},{68,... | collective-permute-start | bytes 1179656 | tf_op jit(solution)/shard_map/ppermute | solution.py:735
  8.9 0.3 collective-permute-start.2
  9.3 3.8 %collective-permute-start.3 = (bf16[16,96,128]{2,1,0:T(8,128)(2,1)}, bf16[16,96,128]{2,1,0:T(8,128)(2,1)S(1)}, u32[]{:S(2)}, u32[]{:S(2)}) collective-permute-start(bf16[16,96,128]{2,1,0:T(8,128)(2,1)} %get-tuple-element.55), channel_id=1, source_target_pairs={{1,2},{2,1},{5,6},{6,5},{9,10},{10,9},{13,14},{14,13},{17,18},{18,... | collective-permute-start | bytes 1179656 | tf_op jit(solution)/shard_map/ppermute | solution.py:735
  13.1 0.0 copy-start.2
  13.1 1.1 copy-done.2
  14.2 0.0 slice-start
  14.2 0.5 tap_kernels.1
  14.7 0.0 copy-done
  14.7 0.0 copy-done.1
  14.7 0.0 copy-start.4
  14.7 0.9 copy-done.4
  15.6 0.0 copy-start.6
  15.6 0.0 copy-start.7
  15.6 0.0 slice-start.1
  15.6 0.0 copy-start.5
  15.7 1.6 %build.1.before = bf16[18,18,96,128]{3,2,1,0:T(8,128)(2,1)S(1)} custom-call(s32[11]{0:T(128)S(1)} %copy-done.4, bf16[16,16,96,128]{3,2,1,0:T(8,128)(2,1)S(1)} %copy-done, s32[16,16,128]{2,1,0:T(8,128)S(1)} %copy-done.1), custom_call_target="tpu_custom_call" | custom-call | flops 3000000 | bytes 6000000 | tf_op jit(solution)/shard_map/build/pallas_call | solution.py:196
  17.3 0.0 copy-done.6
  17.3 0.0 copy-done.7
  17.3 0.0 collective-permute-done.refs_0_.xm
  17.4 0.0 collective-permute-done.1.refs_1_.xp
  17.4 0.7 corners.1
  18.1 0.1 collective-permute-start.4
  18.2 1.9 %collective-permute-start.5 = (bf16[2,96,128]{2,1,0:T(8,128)(2,1)S(1)}, bf16[2,96,128]{2,1,0:T(8,128)(2,1)S(1)}, u32[]{:S(2)}, u32[]{:S(2)}) collective-permute-start(bf16[2,96,128]{2,1,0:T(8,128)(2,1)S(1)} %get-tuple-element.57), channel_id=1, source_target_pairs={{1,2},{2,1},{5,6},{6,5},{9,10},{10,9},{13,14},{14,13},{17,18},{18,... | collective-permute-start | bytes 147464 | tf_op jit(solution)/shard_map/ppermute | solution.py:735
  20.1 0.0 collective-permute-done.2.ym.refs_2_
  20.1 0.7 collective-permute-done.3.yp.refs_3_
  20.8 0.6 collective-permute-done.4.cm.refs_4_
  21.4 1.6 %collective-permute-done.5.cp.refs_5_ = bf16[2,96,128]{2,1,0:T(8,128)(2,1)S(1)} collective-permute-done((bf16[2,96,128]{2,1,0:T(8,128)(2,1)S(1)}, bf16[2,96,128]{2,1,0:T(8,128)(2,1)S(1)}, u32[]{:S(2)}, u32[]{:S(2)}) %collective-permute-start.5) | collective-permute-done | bytes 49184 | tf_op jit(solution)/shard_map/ppermute | solution.py:735
  23.0 0.0 slice-done
  23.0 0.0 slice-done.1
  23.0 0.0 copy-done.5
  23.0 14.3 %forward.1 = (bf16[18,18,96,128]{3,2,1,0:T(8,128)(2,1)S(1)}, f32[24,8,8,96,128]{4,3,2,1,0:T(8,128)}, f32[128,8,128]{2,1,0:T(8,128)S(1)}) custom-call(s32[11]{0:T(128)S(1)} %copy-done.5, bf16[18,18,96,128]{3,2,1,0:T(8,128)(2,1)S(1)} %build.1.before, bf16[16,16,96,128]{3,2,1,0:T(8,128)(2,1)S(1)} %bitcast.9, ...), custom_call_target="tpu_custom_call", output_to_operand_aliasing={{0}: (1, {})} | custom-call | flops 16000000000 | bytes 4000000 | tf_op jit(solution)/shard_map/forward/pallas_call | solution.py:287
  37.4 23.6 %all_to_all.15.gathered = f32[128,8,128]{2,1,0:T(8,128)S(1)} all-to-all(f32[128,8,128]{2,1,0:T(8,128)S(1)} %get-tuple-element.59), channel_id=1, replica_groups=mesh['slab'=32,'sub'=4] {'slab','sub'}, dimensions={0} | all-to-all | bytes 1048576 | tf_op jit(solution)/shard_map/all_to_all | solution.py:740
  61.0 5.6 %slopes.1 = (bf16[18,18,96,128]{3,2,1,0:T(8,128)(2,1)S(1)}, bf16[48,8,8,96,128]{4,3,2,1,0:T(8,128)(2,1)}, bf16[16,96,128]{2,1,0:T(8,128)(2,1)S(1)}, bf16[16,96,1...) custom-call(s32[11]{0:T(128)S(1)} %copy-done.5, ...), custom_call_target="tpu_custom_call" | custom-call | flops 30000000 | bytes 12000000 | tf_op jit(solution)/shard_map/slopes/pallas_call | solution.py:420
  66.5 0.1 collective-permute-start.6
  66.6 1.9 %collective-permute-start.7 = (bf16[16,96,128]{2,1,0:T(8,128)(2,1)S(1)}, bf16[16,96,128]{2,1,0:T(8,128)(2,1)S(1)}, u32[]{:S(2)}, u32[]{:S(2)}) collective-permute-start(bf16[16,96,128]{2,1,0:T(8,128)(2,1)S(1)} %get-tuple-element.64), channel_id=1, source_target_pairs={{4,8},{12,16},{20,24},{28,32},{36,40},{44,48},{52,56},{60,64},{68,... | collective-permute-start | bytes 1179656 | tf_op jit(solution)/shard_map/ppermute | solution.py:735
  68.6 3.5 %blanks.1 = (bf16[16,16,96,128]{3,2,1,0:T(8,128)(2,1)}, bf16[16,16,96,128]{3,2,1,0:T(8,128)(2,1)}) custom-call(s32[11]{0:T(128)S(1)} %copy-done.5), custom_call_target="tpu_custom_call" | custom-call | flops 1000 | bytes 8000000 | tf_op jit(solution)/shard_map/blanks/pallas_call | solution.py:348
  72.1 2.2 %build_whole.1.field = bf16[18,18,96,128]{3,2,1,0:T(8,128)(2,1)S(1)} custom-call(s32[11]{0:T(128)S(1)} %copy-done.5, bf16[16,16,96,128]{3,2,1,0:T(8,128)(2,1)S(1)} %copy-done, s32[16,16,128]{2,1,0:T(8,128)S(1)} %copy-done.1, bf16[16,96,128]{2,1,0:T(8,128)(2,1)S(1)} %collective-permute-done.refs_0_.xm, ...), custom_call_target="tpu_custom_call" | custom-call | flops 3000000 | bytes 6000000 | tf_op jit(solution)/shard_map/build_whole/pallas_call | solution.py:196
  74.3 0.0 collective-permute-done.6.refs_2_.xm
  74.3 1.4 %collective-permute-done.7.refs_3_.xp = bf16[16,96,128]{2,1,0:T(8,128)(2,1)S(1)} collective-permute-done((bf16[16,96,128]{2,1,0:T(8,128)(2,1)S(1)}, bf16[16,96,128]{2,1,0:T(8,128)(2,1)S(1)}, u32[]{:S(2)}, u32[]{:S(2)}) %collective-permute-start.7) | collective-permute-done | bytes 393248 | tf_op jit(solution)/shard_map/ppermute | solution.py:735
  75.7 13.2 %weight_terms.1 = f32[2048,128]{1,0:T(8,128)} custom-call(s32[11]{0:T(128)S(1)} %copy-done.5, bf16[18,18,96,128]{3,2,1,0:T(8,128)(2,1)S(1)} %build_whole.1.field, bf16[18,18,96,128]{3,2,1,0:T(8,128)(2,1)S(1)} %get-tuple-element.85.slope), custom_call_target="tpu_custom_call" | custom-call | flops 16000000000 | bytes 2000000 | tf_op jit(solution)/shard_map/weight_terms/pallas_call | solution.py:520
  88.9 6.4 %all-to-all-start.1 = ((f32[128,16,128]{2,1,0:T(8,128)}), f32[128,16,128]{2,1,0:T(8,128)S(1)}, u32[]{:S(2)}, u32[]{:S(2)}) async-start(f32[128,16,128]{2,1,0:T(8,128)} %bitcast.2), calls=%async_computation.1 | async-start | bytes 2097152 | tf_op jit(solution)/shard_map/all_to_all | solution.py:740
  95.3 1.2 stitch.1
  96.5 0.0 copy-start.3
  96.6 0.8 copy-done.3
  97.3 0.1 collective-permute-start.8
  97.4 3.9 %collective-permute-start.9 = (bf16[18,96,128]{2,1,0:T(8,128)(2,1)}, bf16[18,96,128]{2,1,0:T(8,128)(2,1)S(1)}, u32[]{:S(2)}, u32[]{:S(2)}) collective-permute-start(bf16[18,96,128]{2,1,0:T(8,128)(2,1)} %copy-done.3), channel_id=1, source_target_pairs={{1,2},{2,1},{5,6},{6,5},{9,10},{10,9},{13,14},{14,13},{17,18},{18,... | collective-permute-start | bytes 1327112 | tf_op jit(solution)/shard_map/ppermute | solution.py:735
  101.3 0.5 slice_bitcast_fusion
  101.8 5.1 %normed_values.1 = bf16[16,16,96,128]{3,2,1,0:T(8,128)(2,1)} custom-call(s32[11]{0:T(128)S(1)} %copy-done.5, f32[8,128]{1,0:T(8,128)S(1)} %get-tuple-element.62.totals, f32[8,128]{1,0:T(8,128)S(1)} %select_maximum_fusion.params, f32[24,8,8,96,128]{4,3,2,1,0:T(8,128)} %get-tuple-element.61.conv, ...), custom_call_target="tpu_custom_call", output_to_operand_aliasing={{}: (5, {})} | custom-call | flops 30000000 | bytes 8000000 | tf_op jit(solution)/shard_map/normed_values/pallas_call | solution.py:466
  106.9 7.6 %all-to-all-done.1.parts = f32[128,16,128]{2,1,0:T(8,128)S(1)} async-done(((f32[128,16,128]{2,1,0:T(8,128)}), f32[128,16,128]{2,1,0:T(8,128)S(1)}, u32[]{:S(2)}, u32[]{:S(2)}) %all-to-all-start.1) | async-done | bytes 1048608 | tf_op jit(solution)/shard_map/all_to_all | solution.py:740
  114.5 1.0 share.1
  115.4 4.3 %all-to-all-start.2 = ((bf16[128,16,128]{2,1,0:T(8,128)(2,1)}), bf16[128,16,128]{2,1,0:T(8,128)(2,1)S(1)}, u32[]{:S(2)}, u32[]{:S(2)}) async-start(bf16[128,16,128]{2,1,0:T(8,128)(2,1)} %share.1), calls=%async_computation.2 | async-start | bytes 1048576 | tf_op jit(solution)/shard_map/all_to_all | solution.py:740
  119.8 0.0 collective-permute-done.8.ym
  119.8 0.0 collective-permute-done.9.yp
  119.8 15.2 %backward.1 = bf16[16,16,96,128]{3,2,1,0:T(8,128)(2,1)} custom-call(s32[11]{0:T(128)S(1)} %copy-done.5, bf16[48,8,8,96,128]{4,3,2,1,0:T(8,128)(2,1)} %get-tuple-element.75.kept, s32[16,16,128]{2,1,0:T(8,128)S(1)} %copy-done.1, bf16[16,96,128]{2,1,0:T(8,128)(2,1)S(1)} %collective-permute-done.6.refs_2_.xm, ...), custom_call_target="tpu_custom_call", output_to_operand_aliasing={{}: (8, {})} | custom-call | flops 16000000000 | bytes 5000000 | tf_op jit(solution)/shard_map/backward/pallas_call | solution.py:623
  135.0 0.0 all-to-all-done.2
  135.0 1.4 arrange.1
  (2 shorter events, 0.0 us)
Async XLA Ops:
  0.6 14.1 %copy-start = (bf16[16,16,96,128]{3,2,1,0:T(8,128)(2,1)S(1)}, bf16[16,16,96,128]{3,2,1,0:T(8,128)(2,1)}, u32[]{:S(2)}) copy-start(bf16[16,16,96,128]{3,2,1,0:T(8,128)(2,1)} %features.5) | copy-start | bytes 18874372
  0.6 14.1 %copy-start.1 = (s32[16,16,128]{2,1,0:T(8,128)S(1)}, s32[16,16,128]{2,1,0:T(8,128)}, u32[]{:S(2)}) copy-start(s32[16,16,128]{2,1,0:T(8,128)} %mask.13) | copy-start | bytes 393220
  4.7 12.6 %collective-permute-start = (bf16[16,96,128]{2,1,0:T(8,128)(2,1)}, bf16[16,96,128]{2,1,0:T(8,128)(2,1)S(1)}, u32[]{:S(2)}, u32[]{:S(2)}) collective-permute-start(bf16[16,96,128]{2,1,0:T(8,128)(2,1)} %get-tuple-element.47), channel_id=1, source_target_pairs={{0,4},{4,0},{8,12},{12,8},{16,20},{20,16},{24,28},{28,24},{32,36},... | collective-permute-start | bytes 1179656 | tf_op jit(solution)/shard_map/ppermute | solution.py:734
  5.5 11.9 %collective-permute-start.1 = (bf16[16,96,128]{2,1,0:T(8,128)(2,1)}, bf16[16,96,128]{2,1,0:T(8,128)(2,1)S(1)}, u32[]{:S(2)}, u32[]{:S(2)}) collective-permute-start(bf16[16,96,128]{2,1,0:T(8,128)(2,1)} %get-tuple-element.48), channel_id=1, source_target_pairs={{4,8},{12,16},{20,24},{28,32},{36,40},{44,48},{52,56},{60,64},{68,... | collective-permute-start | bytes 1179656 | tf_op jit(solution)/shard_map/ppermute | solution.py:735
  8.9 11.2 %collective-permute-start.2 = (bf16[16,96,128]{2,1,0:T(8,128)(2,1)}, bf16[16,96,128]{2,1,0:T(8,128)(2,1)S(1)}, u32[]{:S(2)}, u32[]{:S(2)}) collective-permute-start(bf16[16,96,128]{2,1,0:T(8,128)(2,1)} %get-tuple-element.54), channel_id=1, source_target_pairs={{0,1},{1,0},{2,3},{3,2},{4,5},{5,4},{6,7},{7,6},{8,9},{9,8},{10,11... | collective-permute-start | bytes 1179656 | tf_op jit(solution)/shard_map/ppermute | solution.py:734
  9.3 11.5 %collective-permute-start.3 = (bf16[16,96,128]{2,1,0:T(8,128)(2,1)}, bf16[16,96,128]{2,1,0:T(8,128)(2,1)S(1)}, u32[]{:S(2)}, u32[]{:S(2)}) collective-permute-start(bf16[16,96,128]{2,1,0:T(8,128)(2,1)} %get-tuple-element.55), channel_id=1, source_target_pairs={{1,2},{2,1},{5,6},{6,5},{9,10},{10,9},{13,14},{14,13},{17,18},{18,... | collective-permute-start | bytes 1179656 | tf_op jit(solution)/shard_map/ppermute | solution.py:735
  13.1 1.1 copy-start.2
  14.2 8.9 %slice-start = ((s8[6291456]{0:T(1024)(128)(4,1)}), s8[4194304]{0:T(1024)(128)(4,1)S(1)}, s32[]{:S(2)}) async-start(s8[6291456]{0:T(1024)(128)(4,1)} %bitcast.8), calls=%async_computation.3 | async-start | bytes 8388608
  14.7 0.9 copy-start.4
  15.6 1.7 %copy-start.6 = (f32[96]{0:T(128)S(1)}, f32[96]{0:T(128)}, u32[]{:S(2)}) copy-start(f32[96]{0:T(128)} %param.10) | copy-start | bytes 1156
  15.6 1.7 %copy-start.7 = (f32[96]{0:T(128)S(1)}, f32[96]{0:T(128)}, u32[]{:S(2)}) copy-start(f32[96]{0:T(128)} %param.9) | copy-start | bytes 1156
  15.6 7.4 %slice-start.1 = ((s8[6291456]{0:T(1024)(128)(4,1)}), s8[2097152]{0:T(1024)(128)(4,1)S(1)}, s32[]{:S(2)}) async-start(s8[6291456]{0:T(1024)(128)(4,1)} %bitcast.8), calls=%async_computation.4 | async-start | bytes 4194304
  15.6 7.4 %copy-start.5 = (s32[11]{0:T(128)S(1)}, s32[11]{0:T(128)}, u32[]{:S(2)}) copy-start(s32[11]{0:T(128)} %get-tuple-element.46.meta) | copy-start | bytes 136
  18.1 3.3 %collective-permute-start.4 = (bf16[2,96,128]{2,1,0:T(8,128)(2,1)S(1)}, bf16[2,96,128]{2,1,0:T(8,128)(2,1)S(1)}, u32[]{:S(2)}, u32[]{:S(2)}) collective-permute-start(bf16[2,96,128]{2,1,0:T(8,128)(2,1)S(1)} %get-tuple-element.56), channel_id=1, source_target_pairs={{0,1},{1,0},{2,3},{3,2},{4,5},{5,4},{6,7},{7,6},{8,9},{9,8},{10,11... | collective-permute-start | bytes 147464 | tf_op jit(solution)/shard_map/ppermute | solution.py:734
  18.2 4.8 %collective-permute-start.5 = (bf16[2,96,128]{2,1,0:T(8,128)(2,1)S(1)}, bf16[2,96,128]{2,1,0:T(8,128)(2,1)S(1)}, u32[]{:S(2)}, u32[]{:S(2)}) collective-permute-start(bf16[2,96,128]{2,1,0:T(8,128)(2,1)S(1)} %get-tuple-element.57), channel_id=1, source_target_pairs={{1,2},{2,1},{5,6},{6,5},{9,10},{10,9},{13,14},{14,13},{17,18},{18,... | collective-permute-start | bytes 147464 | tf_op jit(solution)/shard_map/ppermute | solution.py:735
  66.5 7.8 %collective-permute-start.6 = (bf16[16,96,128]{2,1,0:T(8,128)(2,1)S(1)}, bf16[16,96,128]{2,1,0:T(8,128)(2,1)S(1)}, u32[]{:S(2)}, u32[]{:S(2)}) collective-permute-start(bf16[16,96,128]{2,1,0:T(8,128)(2,1)S(1)} %get-tuple-element.63), channel_id=1, source_target_pairs={{0,4},{4,0},{8,12},{12,8},{16,20},{20,16},{24,28},{28,24},{32,36},... | collective-permute-start | bytes 1179656 | tf_op jit(solution)/shard_map/ppermute | solution.py:734
  66.6 9.1 %collective-permute-start.7 = (bf16[16,96,128]{2,1,0:T(8,128)(2,1)S(1)}, bf16[16,96,128]{2,1,0:T(8,128)(2,1)S(1)}, u32[]{:S(2)}, u32[]{:S(2)}) collective-permute-start(bf16[16,96,128]{2,1,0:T(8,128)(2,1)S(1)} %get-tuple-element.64), channel_id=1, source_target_pairs={{4,8},{12,16},{20,24},{28,32},{36,40},{44,48},{52,56},{60,64},{68,... | collective-permute-start | bytes 1179656 | tf_op jit(solution)/shard_map/ppermute | solution.py:735
  88.9 25.6 %all-to-all-start.1 = ((f32[128,16,128]{2,1,0:T(8,128)}), f32[128,16,128]{2,1,0:T(8,128)S(1)}, u32[]{:S(2)}, u32[]{:S(2)}) async-start(f32[128,16,128]{2,1,0:T(8,128)} %bitcast.2), calls=%async_computation.1 | async-start | bytes 2097152 | tf_op jit(solution)/shard_map/all_to_all | solution.py:740
  96.5 0.8 copy-start.3
  97.3 22.5 %collective-permute-start.8 = (bf16[18,96,128]{2,1,0:T(8,128)(2,1)}, bf16[18,96,128]{2,1,0:T(8,128)(2,1)S(1)}, u32[]{:S(2)}, u32[]{:S(2)}) collective-permute-start(bf16[18,96,128]{2,1,0:T(8,128)(2,1)} %get-tuple-element.80), channel_id=1, source_target_pairs={{0,1},{1,0},{2,3},{3,2},{4,5},{5,4},{6,7},{7,6},{8,9},{9,8},{10,11... | collective-permute-start | bytes 1327112 | tf_op jit(solution)/shard_map/ppermute | solution.py:734
  97.4 22.4 %collective-permute-start.9 = (bf16[18,96,128]{2,1,0:T(8,128)(2,1)}, bf16[18,96,128]{2,1,0:T(8,128)(2,1)S(1)}, u32[]{:S(2)}, u32[]{:S(2)}) collective-permute-start(bf16[18,96,128]{2,1,0:T(8,128)(2,1)} %copy-done.3), channel_id=1, source_target_pairs={{1,2},{2,1},{5,6},{6,5},{9,10},{10,9},{13,14},{14,13},{17,18},{18,... | collective-permute-start | bytes 1327112 | tf_op jit(solution)/shard_map/ppermute | solution.py:735
  115.4 19.6 %all-to-all-start.2 = ((bf16[128,16,128]{2,1,0:T(8,128)(2,1)}), bf16[128,16,128]{2,1,0:T(8,128)(2,1)S(1)}, u32[]{:S(2)}, u32[]{:S(2)}) async-start(bf16[128,16,128]{2,1,0:T(8,128)(2,1)} %share.1), calls=%async_computation.2 | async-start | bytes 1048576 | tf_op jit(solution)/shard_map/all_to_all | solution.py:740

commit v5 on v4

--- a/solution.py
+++ b/solution.py
@@ -120,7 +120,7 @@
 
 def prepare_kernel(features, mask, x_even, x_odd, y_even, y_odd, meta, sem_in):
     faces, sides = (x_even, x_odd), (y_even, y_odd)
-    meta[9] = lax.rem(lax.axis_index("slab"), 2)
+    meta[9] = lax.axis_index("core")
     meta[10] = lax.rem(lax.axis_index("sub"), 2)
     x_end, y_end = near_ends(meta)
     rows, cols = (15 * x_end, 15 - 15 * x_end), (15 * y_end, 15 - 15 * y_end)
@@ -262,7 +262,7 @@
         sums[4, 0:BRICK] = sums[4, 0:BRICK] + active
         conv_copy(slot, x).start()
 
-    each_row(meta[8], row, unroll=2)
+    each_row(meta[8], row, unroll=4)
 
     ones = jnp.ones((8, DEPTH), F32)
     rows = []
@@ -409,7 +409,7 @@
             ).astype(BF16)
         keep_row(slot, x).start()
 
-    each_row(occupied, row)
+    each_row(occupied, row, unroll=2)
     take_rims(meta, field, (x_even, x_odd, y_even, y_odd), sem_rim)
     each_row(occupied, lambda slot, x: keep_row(slot, x).wait())
 
@@ -458,7 +458,7 @@
             ys[slot, x, col] = ((gain_c * normed + bias_c) * active[col : col + 1]).astype(BF16)
         copy(slot, x).start()
 
-    each_row(meta[8], row)
+    each_row(meta[8], row, unroll=2)
     each_row(meta[8], lambda slot, x: copy(slot, x).wait())
 
 
@@ -481,7 +481,7 @@
     )(meta, totals, params, convs, voxel_mask, base)
 
 
-def weight_kernel(meta, field, slope, out, acc):
+def weight_kernel(meta, field, slope, mine, other, acc, out):
     acc[...] = jnp.zeros(acc.shape, F32)
     lane = lax.broadcasted_iota(jnp.int32, (CHANS, DEPTH), 1)
 
@@ -510,21 +510,26 @@
             preferred_element_type=F32,
         )
 
-    each_row(meta[8], row, unroll=2)
+    each_row(meta[8], row, unroll=4)
     for tile in range(TILES):
         out[ROWS * tile : ROWS * (tile + 1)] = acc[:, DEPTH * tile : DEPTH * (tile + 1)]
     out[ROWS * TILES :] = jnp.zeros((2048 - ROWS * TILES, DEPTH), F32)
+    for pair in range(16):
+        for target, core in ((mine, meta[9]), (other, 1 - meta[9])):
+            start = pl.multiple_of(128 * pair + 64 * core, 64)
+            target[pair] = out[pl.ds(start, 64)]
 
 
 def weight_terms(meta, field, slope):
+    half = jax.ShapeDtypeStruct((16, 64, DEPTH), F32)
     return pl.pallas_call(
         weight_kernel,
         name="weight_terms",
-        out_shape=jax.ShapeDtypeStruct((2048, DEPTH), F32),
+        out_shape=(half, half),
         in_specs=[SMEM, VMEM, VMEM],
-        out_specs=VMEM,
-        scratch_shapes=[pltpu.VMEM((ROWS, COLS), F32)],
-        compiler_params=params_of(4),
+        out_specs=(VMEM, VMEM),
+        scratch_shapes=[pltpu.VMEM((ROWS, COLS), F32), pltpu.VMEM((2048, DEPTH), F32)],
+        compiler_params=params_of(6),
         cost_estimate=cost(16_000_000_000, 2_000_000),
     )(meta, field, slope)
 
@@ -615,7 +620,7 @@
             results[slot, x, col] = (outs[col] * active[col : col + 1]).astype(BF16)
         copy(slot, x).start()
 
-    each_row(occupied, row, unroll=2)
+    each_row(occupied, row, unroll=4)
     each_row(occupied, lambda slot, x: copy(slot, x).wait())
 
 
@@ -727,8 +732,7 @@
     )(weight)
 
 
-def exchange(even, odd, axis):
-    count = lax.axis_size(axis)
+def exchange(even, odd, axis, count):
     meets = [(i, i + 1) for i in range(1, count - 1, 2)]
     return (
         lax.ppermute(even, axis, [(i, i ^ 1) for i in range(count)]),
@@ -737,35 +741,41 @@
 
 
 def swap_all(pieces):
-    return lax.all_to_all(pieces, ("slab", "sub"), 0, 0, tiled=True)
+    return lax.all_to_all(pieces, ("pair", "core", "sub"), 0, 0, tiled=True)
+
+
+def reduce_pieces(mine, other):
+    half = mine + lax.ppermute(other, "core", [(0, 1), (1, 0)])
+    pieces = half.reshape(DEVICES // 2, 16, DEPTH)
+    return lax.all_to_all(pieces, ("pair", "sub"), 0, 0, tiled=True)
 
 
 def body(features, voxel_mask, weight, norm_gain, norm_bias, out_grad):
+    slabs, subs = lax.axis_size("pair") * 2, lax.axis_size("sub")
     x_even, x_odd, y_even, y_odd, meta = prepare(features, voxel_mask)
-    x_rims = exchange(x_even, x_odd, "slab")
-    y_rims = exchange(y_even, y_odd, "sub")
+    x_rims = exchange(x_even, x_odd, ("pair", "core"), slabs)
+    y_rims = exchange(y_even, y_odd, "sub", subs)
     field = build(meta, features, voxel_mask)
     ahead, back = tap_kernels(weight)
     params = jnp.pad(jnp.stack([norm_gain, norm_bias]), ((0, 6), (0, DEPTH - CHANS)))
     x_rims, field, ahead, back, params = lax.optimization_barrier(
         (x_rims, field, ahead, back, params)
     )
-    corners = exchange(*corners_of(meta, *x_rims), "sub")
+    corners = exchange(*corners_of(meta, *x_rims), "sub", subs)
     rims = (*x_rims, *y_rims, *corners)
     conv, stats = forward(meta, field, out_grad, voxel_mask, rims, ahead)
     slope, kept, x_even, x_odd, y_even, y_odd, sums, totals = slopes(
         meta, swap_all(stats), params, conv, out_grad, voxel_mask
     )
-    x_rims = exchange(x_even, x_odd, "slab")
+    x_rims = exchange(x_even, x_odd, ("pair", "core"), slabs)
     rims, x_even = lax.optimization_barrier((rims, x_even))
     field = build(meta, features, voxel_mask, rims)
     normed_base, feature_base = blanks(meta)
     x_rims, slope, field, normed_base, feature_base = lax.optimization_barrier(
         (x_rims, slope, field, normed_base, feature_base)
     )
-    y_rims = exchange(*stitch(meta, y_even, y_odd, *x_rims), "sub")
-    terms = weight_terms(meta, field, slope)
-    parts = swap_all(terms.reshape(DEVICES, 16, DEPTH))
+    y_rims = exchange(*stitch(meta, y_even, y_odd, *x_rims), "sub", subs)
+    parts = reduce_pieces(*weight_terms(meta, field, slope))
     normed_out = normed_values(meta, totals, params, conv, voxel_mask, normed_base)
     shared = swap_all(share(parts))
     feature_grad = backward(meta, kept, voxel_mask, (*x_rims, *y_rims), back, feature_base)
@@ -774,18 +784,23 @@
 
 
 def solution(mesh):
+    slabs, subs = mesh.devices.shape
+    paired = jax.sharding.Mesh(
+        mesh.devices.reshape(slabs // 2, 2, subs), ("pair", "core", "sub")
+    )
+    slab = ("pair", "core")
     placed = (
-        P("slab", "sub", None, None),
-        P("slab", "sub", None),
+        P(slab, "sub", None, None),
+        P(slab, "sub", None),
         P(),
         P(),
         P(),
-        P("slab", "sub", None, None),
+        P(slab, "sub", None, None),
     )
     return jax.shard_map(
         body,
-        mesh=mesh,
+        mesh=paired,
         in_specs=placed,
-        out_specs=(P("slab", "sub", None, None), P("slab", "sub", None, None), P(), P(), P()),
+        out_specs=(P(slab, "sub", None, None), P(slab, "sub", None, None), P(), P(), P()),
         check_vma=False,
     )

time: 137 us -> 132 us (0.964)
  waiting for transfers between devices: 11.9 us -> 6.31 us
  starting transfers between devices: 27 us -> 31.6 us
  Pallas kernels: 69.6 us -> 65 us
    all_to_all x2, waiting for transfers between devices: 7.58 us -> 0.78 us  [the longest x1 0.78 us: reduce_pieces(): return lax.all_to_all(pieces, ('pair', 'sub'), 0, 0, tiled=True)]
    all_to_all x2, starting transfers between devices: 10.7 us -> 14.6 us  [the longest x1 7.73 us: swap_all(): return lax.all_to_all(pieces, ('pair', 'core', 'sub'), 0, 0, tiled=True)]
    ppermute x0 -> x1, waiting for transfers between devices: none -> 1.9 us  [reduce_pieces(): half = mine + lax.ppermute(other, 'core', [(0, 1), (1, 0)])]
    pallas_call x1, Pallas kernels: 13.2 us -> 11.6 us  [weight_terms(): pl.pallas_call(weight_kernel, name='weight_terms', out_shape=(half, half)...]
  transfers between devices with their start and end apart: 12 -> 13, of which waited for: 5 -> 6; matrix products, arithmetic and copies ran while one was open for 0% -> 0% of each run, Pallas kernels for 23% -> 22%
where the time goes in v5:
time: 132 us; the launch traced here: 131 us
  Pallas kernels  65 us (49%)
  starting transfers between devices  31.6 us (24%)
  blocking collectives  23.3 us (18%)
  waiting for transfers between devices  6.31 us (5%)
  local copies, waits for them, and re-layouts  3.32 us (3%)
    all_to_all x1, blocking collectives, swap_all(): return lax.all_to_all(pieces, ('pair', 'core', 'sub'), 0, 0, tiled=True)  23.3 us
    ppermute x5, starting transfers between devices, exchange(): lax.ppermute(odd, axis, meets + [(j, i) for i, j in meets])  15.2 us
    pallas_call x1, Pallas kernels, backward(): pl.pallas_call(backward_kernel, name='backward', out_shape=jax.ShapeDtype...  14.1 us
    pallas_call x1, Pallas kernels, forward(): pl.pallas_call(forward_kernel, name='forward', out_shape=(jax.ShapeDtypeS...  13.3 us
    pallas_call x1, Pallas kernels, weight_terms(): pl.pallas_call(weight_kernel, name='weight_terms', out_shape=(half, half)...  11.6 us
    all_to_all x1, starting transfers between devices, swap_all(): return lax.all_to_all(pieces, ('pair', 'core', 'sub'), 0, 0, tiled=True)  7.73 us
    all_to_all x1, starting transfers between devices, reduce_pieces(): return lax.all_to_all(pieces, ('pair', 'sub'), 0, 0, tiled=True)  6.88 us
    pallas_call x1, Pallas kernels, slopes(): pl.pallas_call(slope_kernel, name='slopes', out_shape=(jax.ShapeDtypeStru...  5.21 us
  transfers between devices with their start and end apart: 13, of which 6 were waited for; matrix products, arithmetic and copies ran while one was open for 0% of the time, Pallas kernels for 22%

profile of v5, /device:TPU:3, one launch (start us, length us, event | category | flops | bytes accessed | tf_op | source)
XLA Modules:
  0.0 131.4 jit_solution(7868007618707385525)
XLA Ops:
  0.6 0.0 copy-start
  0.6 0.0 copy-start.1
  0.7 4.1 %prepare.1 = (bf16[16,96,128]{2,1,0:T(8,128)(2,1)}, bf16[16,96,128]{2,1,0:T(8,128)(2,1)}, bf16[16,96,128]{2,1,0:T(8,128)(2,1)}, bf16[16,96,128]{2,1,0:T(8,128)(2,1)}, s32[11]{0:T(128)}) custom-call(bf16[16,16,96,128]{3,2,1,0:T(8,128)(2,1)} %features.5, s32[16,16,128]{2,1,0:T(8,128)} %mask.13), custom_call_target="tpu_custom_call" | custom-call | flops 3000000 | bytes 3000000 | tf_op jit(solution)/shard_map/prepare/pallas_call | solution.py:166
  4.7 0.8 collective-permute-start
  5.5 3.4 %collective-permute-start.1 = (bf16[16,96,128]{2,1,0:T(8,128)(2,1)}, bf16[16,96,128]{2,1,0:T(8,128)(2,1)S(1)}, u32[]{:S(2)}, u32[]{:S(2)}) collective-permute-start(bf16[16,96,128]{2,1,0:T(8,128)(2,1)} %get-tuple-element.50), channel_id=1, source_target_pairs={{4,8},{12,16},{20,24},{28,32},{36,40},{44,48},{52,56},{60,64},{68,... | collective-permute-start | bytes 1179656 | tf_op jit(solution)/shard_map/ppermute | solution.py:739
  8.9 0.3 collective-permute-start.2
  9.3 3.8 %collective-permute-start.3 = (bf16[16,96,128]{2,1,0:T(8,128)(2,1)}, bf16[16,96,128]{2,1,0:T(8,128)(2,1)S(1)}, u32[]{:S(2)}, u32[]{:S(2)}) collective-permute-start(bf16[16,96,128]{2,1,0:T(8,128)(2,1)} %get-tuple-element.57), channel_id=1, source_target_pairs={{1,2},{2,1},{5,6},{6,5},{9,10},{10,9},{13,14},{14,13},{17,18},{18,... | collective-permute-start | bytes 1179656 | tf_op jit(solution)/shard_map/ppermute | solution.py:739
  13.1 0.0 copy-start.2
  13.1 1.1 copy-done.2
  14.2 0.0 slice-start
  14.2 0.5 tap_kernels.1
  14.7 0.0 copy-done
  14.7 0.0 copy-done.1
  14.7 0.0 copy-start.4
  14.7 0.9 copy-done.4
  15.6 0.0 copy-start.6
  15.6 0.0 copy-start.7
  15.6 0.0 slice-start.1
  15.7 1.6 %build.1.before = bf16[18,18,96,128]{3,2,1,0:T(8,128)(2,1)S(1)} custom-call(s32[11]{0:T(128)S(1)} %copy-done.4, bf16[16,16,96,128]{3,2,1,0:T(8,128)(2,1)S(1)} %copy-done, s32[16,16,128]{2,1,0:T(8,128)S(1)} %copy-done.1), custom_call_target="tpu_custom_call" | custom-call | flops 3000000 | bytes 6000000 | tf_op jit(solution)/shard_map/build/pallas_call | solution.py:196
  17.3 0.0 copy-done.6
  17.3 0.0 copy-done.7
  17.3 0.0 collective-permute-done.refs_0_.xm
  17.4 0.0 collective-permute-done.1.refs_1_.xp
  17.4 0.7 corners.1
  18.1 0.1 collective-permute-start.4
  18.2 0.0 copy-start.5
  18.2 1.9 %collective-permute-start.5 = (bf16[2,96,128]{2,1,0:T(8,128)(2,1)S(1)}, bf16[2,96,128]{2,1,0:T(8,128)(2,1)S(1)}, u32[]{:S(2)}, u32[]{:S(2)}) collective-permute-start(bf16[2,96,128]{2,1,0:T(8,128)(2,1)S(1)} %get-tuple-element.59), channel_id=1, source_target_pairs={{1,2},{2,1},{5,6},{6,5},{9,10},{10,9},{13,14},{14,13},{17,18},{18,... | collective-permute-start | bytes 147464 | tf_op jit(solution)/shard_map/ppermute | solution.py:739
  20.1 0.0 collective-permute-done.2.ym.refs_2_
  20.1 0.7 collective-permute-done.3.yp.refs_3_
  20.8 0.6 collective-permute-done.4.cm.refs_4_
  21.4 1.6 %collective-permute-done.5.cp.refs_5_ = bf16[2,96,128]{2,1,0:T(8,128)(2,1)S(1)} collective-permute-done((bf16[2,96,128]{2,1,0:T(8,128)(2,1)S(1)}, bf16[2,96,128]{2,1,0:T(8,128)(2,1)S(1)}, u32[]{:S(2)}, u32[]{:S(2)}) %collective-permute-start.5) | collective-permute-done | bytes 49184 | tf_op jit(solution)/shard_map/ppermute | solution.py:739
  23.0 0.0 slice-done
  23.0 0.0 slice-done.1
  23.0 13.3 %forward.1 = (bf16[18,18,96,128]{3,2,1,0:T(8,128)(2,1)S(1)}, f32[24,8,8,96,128]{4,3,2,1,0:T(8,128)}, f32[128,8,128]{2,1,0:T(8,128)S(1)}) custom-call(s32[11]{0:T(128)S(1)} %copy-done.4, bf16[18,18,96,128]{3,2,1,0:T(8,128)(2,1)S(1)} %build.1.before, bf16[16,16,96,128]{3,2,1,0:T(8,128)(2,1)S(1)} %bitcast.9, ...), custom_call_target="tpu_custom_call", output_to_operand_aliasing={{0}: (1, {})} | custom-call | flops 16000000000 | bytes 4000000 | tf_op jit(solution)/shard_map/forward/pallas_call | solution.py:287
  36.4 23.3 %all_to_all.15.gathered = f32[128,8,128]{2,1,0:T(8,128)S(1)} all-to-all(f32[128,8,128]{2,1,0:T(8,128)S(1)} %get-tuple-element.61), channel_id=1, replica_groups=mesh['pair'=16,'core'=2,'sub'=4] {'pair','core','sub'}, dimensions={0} | all-to-all | bytes 1048576 | tf_op jit(solution)/shard_map/all_to_all | solution.py:744
  59.6 0.0 copy-done.5
  59.6 5.2 %slopes.1 = (bf16[18,18,96,128]{3,2,1,0:T(8,128)(2,1)S(1)}, bf16[48,8,8,96,128]{4,3,2,1,0:T(8,128)(2,1)}, bf16[16,96,128]{2,1,0:T(8,128)(2,1)S(1)}, bf16[16,96,1...) custom-call(s32[11]{0:T(128)S(1)} %copy-done.5, ...), custom_call_target="tpu_custom_call" | custom-call | flops 30000000 | bytes 12000000 | tf_op jit(solution)/shard_map/slopes/pallas_call | solution.py:420
  64.9 0.1 collective-permute-start.6
  65.0 2.6 %collective-permute-start.7 = (bf16[16,96,128]{2,1,0:T(8,128)(2,1)S(1)}, bf16[16,96,128]{2,1,0:T(8,128)(2,1)S(1)}, u32[]{:S(2)}, u32[]{:S(2)}) collective-permute-start(bf16[16,96,128]{2,1,0:T(8,128)(2,1)S(1)} %get-tuple-element.66), channel_id=1, source_target_pairs={{4,8},{12,16},{20,24},{28,32},{36,40},{44,48},{52,56},{60,64},{68,... | collective-permute-start | bytes 1179656 | tf_op jit(solution)/shard_map/ppermute | solution.py:739
  67.6 3.5 %blanks.1 = (bf16[16,16,96,128]{3,2,1,0:T(8,128)(2,1)}, bf16[16,16,96,128]{3,2,1,0:T(8,128)(2,1)}) custom-call(s32[11]{0:T(128)S(1)} %copy-done.5), custom_call_target="tpu_custom_call" | custom-call | flops 1000 | bytes 8000000 | tf_op jit(solution)/shard_map/blanks/pallas_call | solution.py:348
  71.1 2.2 %build_whole.1.field = bf16[18,18,96,128]{3,2,1,0:T(8,128)(2,1)S(1)} custom-call(s32[11]{0:T(128)S(1)} %copy-done.5, bf16[16,16,96,128]{3,2,1,0:T(8,128)(2,1)S(1)} %copy-done, s32[16,16,128]{2,1,0:T(8,128)S(1)} %copy-done.1, bf16[16,96,128]{2,1,0:T(8,128)(2,1)S(1)} %collective-permute-done.refs_0_.xm, ...), custom_call_target="tpu_custom_call" | custom-call | flops 3000000 | bytes 6000000 | tf_op jit(solution)/shard_map/build_whole/pallas_call | solution.py:196
  73.3 0.0 collective-permute-done.6.refs_2_.xm
  73.3 0.7 collective-permute-done.7.refs_3_.xp
  74.1 11.6 %weight_terms.1 = (f32[16,64,128]{2,1,0:T(8,128)S(1)}, f32[16,64,128]{2,1,0:T(8,128)S(1)}) custom-call(s32[11]{0:T(128)S(1)} %copy-done.5, bf16[18,18,96,128]{3,2,1,0:T(8,128)(2,1)S(1)} %build_whole.1.field, bf16[18,18,96,128]{3,2,1,0:T(8,128)(2,1)S(1)} %get-tuple-element.87.slope), custom_call_target="tpu_custom_call" | custom-call | flops 16000000000 | bytes 2000000 | tf_op jit(solution)/shard_map/weight_terms/pallas_call | solution.py:525
  85.6 0.1 collective-permute-start.10
  85.7 1.9 %collective-permute-done.10 = f32[16,64,128]{2,1,0:T(8,128)S(1)} collective-permute-done((f32[16,64,128]{2,1,0:T(8,128)S(1)}, f32[16,64,128]{2,1,0:T(8,128)S(1)}, u32[]{:S(2)}, u32[]{:S(2)}) %collective-permute-start.10) | collective-permute-done | bytes 524320 | tf_op jit(solution)/shard_map/ppermute | solution.py:748
  87.6 0.9 add.5
  88.5 6.9 %all-to-all-start.1 = ((f32[64,16,128]{2,1,0:T(8,128)}), f32[64,16,128]{2,1,0:T(8,128)S(1)}, u32[]{:S(2)}, u32[]{:S(2)}) async-start(f32[64,16,128]{2,1,0:T(8,128)} %bitcast.11), calls=%async_computation.1 | async-start | bytes 1048576 | tf_op jit(solution)/shard_map/all_to_all | solution.py:750
  95.4 0.7 stitch.1
  96.1 0.0 copy-start.3
  96.1 0.8 copy-done.3
  96.9 0.5 collective-permute-start.8
  97.3 3.5 %collective-permute-start.9 = (bf16[18,96,128]{2,1,0:T(8,128)(2,1)}, bf16[18,96,128]{2,1,0:T(8,128)(2,1)S(1)}, u32[]{:S(2)}, u32[]{:S(2)}) collective-permute-start(bf16[18,96,128]{2,1,0:T(8,128)(2,1)} %copy-done.3), channel_id=1, source_target_pairs={{1,2},{2,1},{5,6},{6,5},{9,10},{10,9},{13,14},{14,13},{17,18},{18,... | collective-permute-start | bytes 1327112 | tf_op jit(solution)/shard_map/ppermute | solution.py:739
  100.8 0.5 slice_bitcast_fusion
  101.4 5.1 %normed_values.1 = bf16[16,16,96,128]{3,2,1,0:T(8,128)(2,1)} custom-call(s32[11]{0:T(128)S(1)} %copy-done.5, f32[8,128]{1,0:T(8,128)S(1)} %get-tuple-element.64.totals, f32[8,128]{1,0:T(8,128)S(1)} %select_maximum_fusion.params, f32[24,8,8,96,128]{4,3,2,1,0:T(8,128)} %get-tuple-element.63.conv, ...), custom_call_target="tpu_custom_call", output_to_operand_aliasing={{}: (5, {})} | custom-call | flops 30000000 | bytes 8000000 | tf_op jit(solution)/shard_map/normed_values/pallas_call | solution.py:466
  106.4 0.8 all-to-all-done.1.parts
  107.2 0.9 share.1
  108.1 7.7 %all-to-all-start.2 = ((bf16[128,16,128]{2,1,0:T(8,128)(2,1)}), bf16[128,16,128]{2,1,0:T(8,128)(2,1)S(1)}, u32[]{:S(2)}, u32[]{:S(2)}) async-start(bf16[128,16,128]{2,1,0:T(8,128)(2,1)} %share.1), calls=%async_computation.2 | async-start | bytes 1048576 | tf_op jit(solution)/shard_map/all_to_all | solution.py:744
  115.9 0.0 collective-permute-done.8.ym
  115.9 0.0 collective-permute-done.9.yp
  115.9 14.1 %backward.1 = bf16[16,16,96,128]{3,2,1,0:T(8,128)(2,1)} custom-call(s32[11]{0:T(128)S(1)} %copy-done.5, bf16[48,8,8,96,128]{4,3,2,1,0:T(8,128)(2,1)} %get-tuple-element.77.kept, s32[16,16,128]{2,1,0:T(8,128)S(1)} %copy-done.1, bf16[16,96,128]{2,1,0:T(8,128)(2,1)S(1)} %collective-permute-done.6.refs_2_.xm, ...), custom_call_target="tpu_custom_call", output_to_operand_aliasing={{}: (8, {})} | custom-call | flops 16000000000 | bytes 5000000 | tf_op jit(solution)/shard_map/backward/pallas_call | solution.py:628
  130.0 0.0 all-to-all-done.2
  130.0 1.4 %arrange.1 = f32[27,96,96]{2,1,0:T(8,128)} custom-call(bf16[2048,128]{1,0:T(8,128)(2,1)S(1)} %bitcast.10), custom_call_target="tpu_custom_call" | custom-call | flops 300000 | bytes 1500000 | tf_op jit(solution)/shard_map/arrange/pallas_call | solution.py:566
  (2 shorter events, 0.0 us)
Async XLA Ops:
  0.6 14.1 %copy-start = (bf16[16,16,96,128]{3,2,1,0:T(8,128)(2,1)S(1)}, bf16[16,16,96,128]{3,2,1,0:T(8,128)(2,1)}, u32[]{:S(2)}) copy-start(bf16[16,16,96,128]{3,2,1,0:T(8,128)(2,1)} %features.5) | copy-start | bytes 18874372
  0.6 14.1 %copy-start.1 = (s32[16,16,128]{2,1,0:T(8,128)S(1)}, s32[16,16,128]{2,1,0:T(8,128)}, u32[]{:S(2)}) copy-start(s32[16,16,128]{2,1,0:T(8,128)} %mask.13) | copy-start | bytes 393220
  4.7 12.6 %collective-permute-start = (bf16[16,96,128]{2,1,0:T(8,128)(2,1)}, bf16[16,96,128]{2,1,0:T(8,128)(2,1)S(1)}, u32[]{:S(2)}, u32[]{:S(2)}) collective-permute-start(bf16[16,96,128]{2,1,0:T(8,128)(2,1)} %get-tuple-element.49), channel_id=1, source_target_pairs={{0,4},{4,0},{8,12},{12,8},{16,20},{20,16},{24,28},{28,24},{32,36},... | collective-permute-start | bytes 1179656 | tf_op jit(solution)/shard_map/ppermute | solution.py:738
  5.5 11.9 %collective-permute-start.1 = (bf16[16,96,128]{2,1,0:T(8,128)(2,1)}, bf16[16,96,128]{2,1,0:T(8,128)(2,1)S(1)}, u32[]{:S(2)}, u32[]{:S(2)}) collective-permute-start(bf16[16,96,128]{2,1,0:T(8,128)(2,1)} %get-tuple-element.50), channel_id=1, source_target_pairs={{4,8},{12,16},{20,24},{28,32},{36,40},{44,48},{52,56},{60,64},{68,... | collective-permute-start | bytes 1179656 | tf_op jit(solution)/shard_map/ppermute | solution.py:739
  8.9 11.2 %collective-permute-start.2 = (bf16[16,96,128]{2,1,0:T(8,128)(2,1)}, bf16[16,96,128]{2,1,0:T(8,128)(2,1)S(1)}, u32[]{:S(2)}, u32[]{:S(2)}) collective-permute-start(bf16[16,96,128]{2,1,0:T(8,128)(2,1)} %get-tuple-element.56), channel_id=1, source_target_pairs={{0,1},{1,0},{2,3},{3,2},{4,5},{5,4},{6,7},{7,6},{8,9},{9,8},{10,11... | collective-permute-start | bytes 1179656 | tf_op jit(solution)/shard_map/ppermute | solution.py:738
  9.3 11.5 %collective-permute-start.3 = (bf16[16,96,128]{2,1,0:T(8,128)(2,1)}, bf16[16,96,128]{2,1,0:T(8,128)(2,1)S(1)}, u32[]{:S(2)}, u32[]{:S(2)}) collective-permute-start(bf16[16,96,128]{2,1,0:T(8,128)(2,1)} %get-tuple-element.57), channel_id=1, source_target_pairs={{1,2},{2,1},{5,6},{6,5},{9,10},{10,9},{13,14},{14,13},{17,18},{18,... | collective-permute-start | bytes 1179656 | tf_op jit(solution)/shard_map/ppermute | solution.py:739
  13.1 1.1 copy-start.2
  14.2 8.9 %slice-start = ((s8[6291456]{0:T(1024)(128)(4,1)}), s8[4194304]{0:T(1024)(128)(4,1)S(1)}, s32[]{:S(2)}) async-start(s8[6291456]{0:T(1024)(128)(4,1)} %bitcast.8), calls=%async_computation.3 | async-start | bytes 8388608
  14.7 0.9 copy-start.4
  15.6 1.7 %copy-start.6 = (f32[96]{0:T(128)S(1)}, f32[96]{0:T(128)}, u32[]{:S(2)}) copy-start(f32[96]{0:T(128)} %param.10) | copy-start | bytes 1156
  15.6 1.7 %copy-start.7 = (f32[96]{0:T(128)S(1)}, f32[96]{0:T(128)}, u32[]{:S(2)}) copy-start(f32[96]{0:T(128)} %param.9) | copy-start | bytes 1156
  15.6 7.4 %slice-start.1 = ((s8[6291456]{0:T(1024)(128)(4,1)}), s8[2097152]{0:T(1024)(128)(4,1)S(1)}, s32[]{:S(2)}) async-start(s8[6291456]{0:T(1024)(128)(4,1)} %bitcast.8), calls=%async_computation.4 | async-start | bytes 4194304
  18.1 3.3 %collective-permute-start.4 = (bf16[2,96,128]{2,1,0:T(8,128)(2,1)S(1)}, bf16[2,96,128]{2,1,0:T(8,128)(2,1)S(1)}, u32[]{:S(2)}, u32[]{:S(2)}) collective-permute-start(bf16[2,96,128]{2,1,0:T(8,128)(2,1)S(1)} %get-tuple-element.58), channel_id=1, source_target_pairs={{0,1},{1,0},{2,3},{3,2},{4,5},{5,4},{6,7},{7,6},{8,9},{9,8},{10,11... | collective-permute-start | bytes 147464 | tf_op jit(solution)/shard_map/ppermute | solution.py:738
  18.2 41.5 %copy-start.5 = (s32[11]{0:T(128)S(1)}, s32[11]{0:T(128)}, u32[]{:S(2)}) copy-start(s32[11]{0:T(128)} %get-tuple-element.48.meta) | copy-start | bytes 136
  18.2 4.8 %collective-permute-start.5 = (bf16[2,96,128]{2,1,0:T(8,128)(2,1)S(1)}, bf16[2,96,128]{2,1,0:T(8,128)(2,1)S(1)}, u32[]{:S(2)}, u32[]{:S(2)}) collective-permute-start(bf16[2,96,128]{2,1,0:T(8,128)(2,1)S(1)} %get-tuple-element.59), channel_id=1, source_target_pairs={{1,2},{2,1},{5,6},{6,5},{9,10},{10,9},{13,14},{14,13},{17,18},{18,... | collective-permute-start | bytes 147464 | tf_op jit(solution)/shard_map/ppermute | solution.py:739
  64.9 8.5 %collective-permute-start.6 = (bf16[16,96,128]{2,1,0:T(8,128)(2,1)S(1)}, bf16[16,96,128]{2,1,0:T(8,128)(2,1)S(1)}, u32[]{:S(2)}, u32[]{:S(2)}) collective-permute-start(bf16[16,96,128]{2,1,0:T(8,128)(2,1)S(1)} %get-tuple-element.65), channel_id=1, source_target_pairs={{0,4},{4,0},{8,12},{12,8},{16,20},{20,16},{24,28},{28,24},{32,36},... | collective-permute-start | bytes 1179656 | tf_op jit(solution)/shard_map/ppermute | solution.py:738
  65.0 9.1 %collective-permute-start.7 = (bf16[16,96,128]{2,1,0:T(8,128)(2,1)S(1)}, bf16[16,96,128]{2,1,0:T(8,128)(2,1)S(1)}, u32[]{:S(2)}, u32[]{:S(2)}) collective-permute-start(bf16[16,96,128]{2,1,0:T(8,128)(2,1)S(1)} %get-tuple-element.66), channel_id=1, source_target_pairs={{4,8},{12,16},{20,24},{28,32},{36,40},{44,48},{52,56},{60,64},{68,... | collective-permute-start | bytes 1179656 | tf_op jit(solution)/shard_map/ppermute | solution.py:739
  85.6 2.0 %collective-permute-start.10 = (f32[16,64,128]{2,1,0:T(8,128)S(1)}, f32[16,64,128]{2,1,0:T(8,128)S(1)}, u32[]{:S(2)}, u32[]{:S(2)}) collective-permute-start(f32[16,64,128]{2,1,0:T(8,128)S(1)} %get-tuple-element.89), channel_id=1, source_target_pairs={{0,4},{4,0},{1,5},{5,1},{2,6},{6,2},{3,7},{7,3},{8,12},{12,8},{9,1... | collective-permute-start | bytes 1572872 | tf_op jit(solution)/shard_map/ppermute | solution.py:748
  88.5 18.7 %all-to-all-start.1 = ((f32[64,16,128]{2,1,0:T(8,128)}), f32[64,16,128]{2,1,0:T(8,128)S(1)}, u32[]{:S(2)}, u32[]{:S(2)}) async-start(f32[64,16,128]{2,1,0:T(8,128)} %bitcast.11), calls=%async_computation.1 | async-start | bytes 1048576 | tf_op jit(solution)/shard_map/all_to_all | solution.py:750
  96.1 0.8 copy-start.3
  96.9 19.0 %collective-permute-start.8 = (bf16[18,96,128]{2,1,0:T(8,128)(2,1)S(1)}, bf16[18,96,128]{2,1,0:T(8,128)(2,1)S(1)}, u32[]{:S(2)}, u32[]{:S(2)}) collective-permute-start(bf16[18,96,128]{2,1,0:T(8,128)(2,1)S(1)} %get-tuple-element.82), channel_id=1, source_target_pairs={{0,1},{1,0},{2,3},{3,2},{4,5},{5,4},{6,7},{7,6},{8,9},{9,8},{10,11... | collective-permute-start | bytes 1327112 | tf_op jit(solution)/shard_map/ppermute | solution.py:738
  97.3 18.6 %collective-permute-start.9 = (bf16[18,96,128]{2,1,0:T(8,128)(2,1)}, bf16[18,96,128]{2,1,0:T(8,128)(2,1)S(1)}, u32[]{:S(2)}, u32[]{:S(2)}) collective-permute-start(bf16[18,96,128]{2,1,0:T(8,128)(2,1)} %copy-done.3), channel_id=1, source_target_pairs={{1,2},{2,1},{5,6},{6,5},{9,10},{10,9},{13,14},{14,13},{17,18},{18,... | collective-permute-start | bytes 1327112 | tf_op jit(solution)/shard_map/ppermute | solution.py:739
  108.1 21.9 %all-to-all-start.2 = ((bf16[128,16,128]{2,1,0:T(8,128)(2,1)}), bf16[128,16,128]{2,1,0:T(8,128)(2,1)S(1)}, u32[]{:S(2)}, u32[]{:S(2)}) async-start(bf16[128,16,128]{2,1,0:T(8,128)(2,1)} %share.1), calls=%async_computation.2 | async-start | bytes 1048576 | tf_op jit(solution)/shard_map/all_to_all | solution.py:744

commit v6 on v5

--- a/solution.py
+++ b/solution.py
@@ -262,7 +262,7 @@
         sums[4, 0:BRICK] = sums[4, 0:BRICK] + active
         conv_copy(slot, x).start()
 
-    each_row(meta[8], row, unroll=4)
+    each_row(meta[8], row, unroll=8)
 
     ones = jnp.ones((8, DEPTH), F32)
     rows = []
@@ -409,7 +409,7 @@
             ).astype(BF16)
         keep_row(slot, x).start()
 
-    each_row(occupied, row, unroll=2)
+    each_row(occupied, row, unroll=4)
     take_rims(meta, field, (x_even, x_odd, y_even, y_odd), sem_rim)
     each_row(occupied, lambda slot, x: keep_row(slot, x).wait())
 
@@ -458,7 +458,7 @@
             ys[slot, x, col] = ((gain_c * normed + bias_c) * active[col : col + 1]).astype(BF16)
         copy(slot, x).start()
 
-    each_row(meta[8], row, unroll=2)
+    each_row(meta[8], row, unroll=4)
     each_row(meta[8], lambda slot, x: copy(slot, x).wait())
 
 
@@ -510,7 +510,7 @@
             preferred_element_type=F32,
         )
 
-    each_row(meta[8], row, unroll=4)
+    each_row(meta[8], row, unroll=8)
     for tile in range(TILES):
         out[ROWS * tile : ROWS * (tile + 1)] = acc[:, DEPTH * tile : DEPTH * (tile + 1)]
     out[ROWS * TILES :] = jnp.zeros((2048 - ROWS * TILES, DEPTH), F32)
@@ -620,7 +620,7 @@
             results[slot, x, col] = (outs[col] * active[col : col + 1]).astype(BF16)
         copy(slot, x).start()
 
-    each_row(occupied, row, unroll=4)
+    each_row(occupied, row, unroll=8)
     each_row(occupied, lambda slot, x: copy(slot, x).wait())
 
 

time: 132 us -> 131 us (level)
  Pallas kernels: 65 us -> 63.3 us
where the time goes in v6:
time: 131 us; the launch traced here: 129 us
  Pallas kernels  63.3 us (48%)
  starting transfers between devices  31.5 us (24%)
  blocking collectives  22.7 us (17%)
  waiting for transfers between devices  6.45 us (5%)
  local copies, waits for them, and re-layouts  3.32 us (3%)
    all_to_all x1, blocking collectives, swap_all(): return lax.all_to_all(pieces, ('pair', 'core', 'sub'), 0, 0, tiled=True)  22.7 us
    ppermute x5, starting transfers between devices, exchange(): lax.ppermute(odd, axis, meets + [(j, i) for i, j in meets])  15.2 us
    pallas_call x1, Pallas kernels, backward(): pl.pallas_call(backward_kernel, name='backward', out_shape=jax.ShapeDtype...  13.6 us
    pallas_call x1, Pallas kernels, forward(): pl.pallas_call(forward_kernel, name='forward', out_shape=(jax.ShapeDtypeS...  12.8 us
    pallas_call x1, Pallas kernels, weight_terms(): pl.pallas_call(weight_kernel, name='weight_terms', out_shape=(half, half)...  10.9 us
    all_to_all x1, starting transfers between devices, swap_all(): return lax.all_to_all(pieces, ('pair', 'core', 'sub'), 0, 0, tiled=True)  7.48 us
    all_to_all x1, starting transfers between devices, reduce_pieces(): return lax.all_to_all(pieces, ('pair', 'sub'), 0, 0, tiled=True)  6.97 us
    pallas_call x1, Pallas kernels, slopes(): pl.pallas_call(slope_kernel, name='slopes', out_shape=(jax.ShapeDtypeStru...  5.21 us
  transfers between devices with their start and end apart: 13, of which 6 were waited for; matrix products, arithmetic and copies ran while one was open for 0% of the time, Pallas kernels for 22%

profile of v6, /device:TPU:3, one launch (start us, length us, event | category | flops | bytes accessed | tf_op | source)
XLA Modules:
  0.0 129.1 jit_solution(17338634316462462390)
XLA Ops:
  0.6 0.0 copy-start
  0.6 0.0 copy-start.1
  0.7 4.1 %prepare.1 = (bf16[16,96,128]{2,1,0:T(8,128)(2,1)}, bf16[16,96,128]{2,1,0:T(8,128)(2,1)}, bf16[16,96,128]{2,1,0:T(8,128)(2,1)}, bf16[16,96,128]{2,1,0:T(8,128)(2,1)}, s32[11]{0:T(128)}) custom-call(bf16[16,16,96,128]{3,2,1,0:T(8,128)(2,1)} %features.5, s32[16,16,128]{2,1,0:T(8,128)} %mask.13), custom_call_target="tpu_custom_call" | custom-call | flops 3000000 | bytes 3000000 | tf_op jit(solution)/shard_map/prepare/pallas_call | solution.py:166
  4.7 0.8 collective-permute-start
  5.5 3.4 %collective-permute-start.1 = (bf16[16,96,128]{2,1,0:T(8,128)(2,1)}, bf16[16,96,128]{2,1,0:T(8,128)(2,1)S(1)}, u32[]{:S(2)}, u32[]{:S(2)}) collective-permute-start(bf16[16,96,128]{2,1,0:T(8,128)(2,1)} %get-tuple-element.50), channel_id=1, source_target_pairs={{4,8},{12,16},{20,24},{28,32},{36,40},{44,48},{52,56},{60,64},{68,... | collective-permute-start | bytes 1179656 | tf_op jit(solution)/shard_map/ppermute | solution.py:739
  8.9 0.3 collective-permute-start.2
  9.3 3.8 %collective-permute-start.3 = (bf16[16,96,128]{2,1,0:T(8,128)(2,1)}, bf16[16,96,128]{2,1,0:T(8,128)(2,1)S(1)}, u32[]{:S(2)}, u32[]{:S(2)}) collective-permute-start(bf16[16,96,128]{2,1,0:T(8,128)(2,1)} %get-tuple-element.57), channel_id=1, source_target_pairs={{1,2},{2,1},{5,6},{6,5},{9,10},{10,9},{13,14},{14,13},{17,18},{18,... | collective-permute-start | bytes 1179656 | tf_op jit(solution)/shard_map/ppermute | solution.py:739
  13.1 0.0 copy-start.2
  13.1 1.1 copy-done.2
  14.2 0.0 slice-start
  14.2 0.5 tap_kernels.1
  14.7 0.0 copy-done
  14.7 0.0 copy-done.1
  14.7 0.0 copy-start.4
  14.7 0.9 copy-done.4
  15.6 0.0 copy-start.6
  15.6 0.0 copy-start.7
  15.6 0.0 slice-start.1
  15.7 1.6 %build.1.before = bf16[18,18,96,128]{3,2,1,0:T(8,128)(2,1)S(1)} custom-call(s32[11]{0:T(128)S(1)} %copy-done.4, bf16[16,16,96,128]{3,2,1,0:T(8,128)(2,1)S(1)} %copy-done, s32[16,16,128]{2,1,0:T(8,128)S(1)} %copy-done.1), custom_call_target="tpu_custom_call" | custom-call | flops 3000000 | bytes 6000000 | tf_op jit(solution)/shard_map/build/pallas_call | solution.py:196
  17.3 0.0 copy-done.6
  17.3 0.0 copy-done.7
  17.3 0.0 collective-permute-done.refs_0_.xm
  17.4 0.0 collective-permute-done.1.refs_1_.xp
  17.4 0.7 corners.1
  18.1 0.1 collective-permute-start.4
  18.2 0.0 copy-start.5
  18.2 1.9 %collective-permute-start.5 = (bf16[2,96,128]{2,1,0:T(8,128)(2,1)S(1)}, bf16[2,96,128]{2,1,0:T(8,128)(2,1)S(1)}, u32[]{:S(2)}, u32[]{:S(2)}) collective-permute-start(bf16[2,96,128]{2,1,0:T(8,128)(2,1)S(1)} %get-tuple-element.59), channel_id=1, source_target_pairs={{1,2},{2,1},{5,6},{6,5},{9,10},{10,9},{13,14},{14,13},{17,18},{18,... | collective-permute-start | bytes 147464 | tf_op jit(solution)/shard_map/ppermute | solution.py:739
  20.1 0.0 collective-permute-done.2.ym.refs_2_
  20.1 0.7 collective-permute-done.3.yp.refs_3_
  20.8 0.6 collective-permute-done.4.cm.refs_4_
  21.4 1.6 %collective-permute-done.5.cp.refs_5_ = bf16[2,96,128]{2,1,0:T(8,128)(2,1)S(1)} collective-permute-done((bf16[2,96,128]{2,1,0:T(8,128)(2,1)S(1)}, bf16[2,96,128]{2,1,0:T(8,128)(2,1)S(1)}, u32[]{:S(2)}, u32[]{:S(2)}) %collective-permute-start.5) | collective-permute-done | bytes 49184 | tf_op jit(solution)/shard_map/ppermute | solution.py:739
  23.0 0.0 slice-done
  23.0 0.0 slice-done.1
  23.0 12.8 %forward.1 = (bf16[18,18,96,128]{3,2,1,0:T(8,128)(2,1)S(1)}, f32[24,8,8,96,128]{4,3,2,1,0:T(8,128)}, f32[128,8,128]{2,1,0:T(8,128)S(1)}) custom-call(s32[11]{0:T(128)S(1)} %copy-done.4, bf16[18,18,96,128]{3,2,1,0:T(8,128)(2,1)S(1)} %build.1.before, bf16[16,16,96,128]{3,2,1,0:T(8,128)(2,1)S(1)} %bitcast.9, ...), custom_call_target="tpu_custom_call", output_to_operand_aliasing={{0}: (1, {})} | custom-call | flops 16000000000 | bytes 4000000 | tf_op jit(solution)/shard_map/forward/pallas_call | solution.py:287
  35.8 22.7 %all_to_all.15.gathered = f32[128,8,128]{2,1,0:T(8,128)S(1)} all-to-all(f32[128,8,128]{2,1,0:T(8,128)S(1)} %get-tuple-element.61), channel_id=1, replica_groups=mesh['pair'=16,'core'=2,'sub'=4] {'pair','core','sub'}, dimensions={0} | all-to-all | bytes 1048576 | tf_op jit(solution)/shard_map/all_to_all | solution.py:744
  58.6 0.0 copy-done.5
  58.6 5.2 %slopes.1 = (bf16[18,18,96,128]{3,2,1,0:T(8,128)(2,1)S(1)}, bf16[48,8,8,96,128]{4,3,2,1,0:T(8,128)(2,1)}, bf16[16,96,128]{2,1,0:T(8,128)(2,1)S(1)}, bf16[16,96,1...) custom-call(s32[11]{0:T(128)S(1)} %copy-done.5, ...), custom_call_target="tpu_custom_call" | custom-call | flops 30000000 | bytes 12000000 | tf_op jit(solution)/shard_map/slopes/pallas_call | solution.py:420
  63.8 0.1 collective-permute-start.6
  63.9 2.6 %collective-permute-start.7 = (bf16[16,96,128]{2,1,0:T(8,128)(2,1)S(1)}, bf16[16,96,128]{2,1,0:T(8,128)(2,1)S(1)}, u32[]{:S(2)}, u32[]{:S(2)}) collective-permute-start(bf16[16,96,128]{2,1,0:T(8,128)(2,1)S(1)} %get-tuple-element.66), channel_id=1, source_target_pairs={{4,8},{12,16},{20,24},{28,32},{36,40},{44,48},{52,56},{60,64},{68,... | collective-permute-start | bytes 1179656 | tf_op jit(solution)/shard_map/ppermute | solution.py:739
  66.5 3.5 %blanks.1 = (bf16[16,16,96,128]{3,2,1,0:T(8,128)(2,1)}, bf16[16,16,96,128]{3,2,1,0:T(8,128)(2,1)}) custom-call(s32[11]{0:T(128)S(1)} %copy-done.5), custom_call_target="tpu_custom_call" | custom-call | flops 1000 | bytes 8000000 | tf_op jit(solution)/shard_map/blanks/pallas_call | solution.py:348
  70.0 2.2 %build_whole.1.field = bf16[18,18,96,128]{3,2,1,0:T(8,128)(2,1)S(1)} custom-call(s32[11]{0:T(128)S(1)} %copy-done.5, bf16[16,16,96,128]{3,2,1,0:T(8,128)(2,1)S(1)} %copy-done, s32[16,16,128]{2,1,0:T(8,128)S(1)} %copy-done.1, bf16[16,96,128]{2,1,0:T(8,128)(2,1)S(1)} %collective-permute-done.refs_0_.xm, ...), custom_call_target="tpu_custom_call" | custom-call | flops 3000000 | bytes 6000000 | tf_op jit(solution)/shard_map/build_whole/pallas_call | solution.py:196
  72.3 0.0 collective-permute-done.6.refs_2_.xm
  72.3 0.7 collective-permute-done.7.refs_3_.xp
  73.0 10.9 %weight_terms.1 = (f32[16,64,128]{2,1,0:T(8,128)S(1)}, f32[16,64,128]{2,1,0:T(8,128)S(1)}) custom-call(s32[11]{0:T(128)S(1)} %copy-done.5, bf16[18,18,96,128]{3,2,1,0:T(8,128)(2,1)S(1)} %build_whole.1.field, bf16[18,18,96,128]{3,2,1,0:T(8,128)(2,1)S(1)} %get-tuple-element.87.slope), custom_call_target="tpu_custom_call" | custom-call | flops 16000000000 | bytes 2000000 | tf_op jit(solution)/shard_map/weight_terms/pallas_call | solution.py:525
  83.9 0.1 collective-permute-start.10
  84.0 1.9 %collective-permute-done.10 = f32[16,64,128]{2,1,0:T(8,128)S(1)} collective-permute-done((f32[16,64,128]{2,1,0:T(8,128)S(1)}, f32[16,64,128]{2,1,0:T(8,128)S(1)}, u32[]{:S(2)}, u32[]{:S(2)}) %collective-permute-start.10) | collective-permute-done | bytes 524320 | tf_op jit(solution)/shard_map/ppermute | solution.py:748
  85.9 0.9 add.5
  86.8 7.0 %all-to-all-start.1 = ((f32[64,16,128]{2,1,0:T(8,128)}), f32[64,16,128]{2,1,0:T(8,128)S(1)}, u32[]{:S(2)}, u32[]{:S(2)}) async-start(f32[64,16,128]{2,1,0:T(8,128)} %bitcast.11), calls=%async_computation.1 | async-start | bytes 1048576 | tf_op jit(solution)/shard_map/all_to_all | solution.py:750
  93.7 0.7 stitch.1
  94.5 0.0 copy-start.3
  94.5 0.8 copy-done.3
  95.2 0.5 collective-permute-start.8
  95.7 3.5 %collective-permute-start.9 = (bf16[18,96,128]{2,1,0:T(8,128)(2,1)}, bf16[18,96,128]{2,1,0:T(8,128)(2,1)S(1)}, u32[]{:S(2)}, u32[]{:S(2)}) collective-permute-start(bf16[18,96,128]{2,1,0:T(8,128)(2,1)} %copy-done.3), channel_id=1, source_target_pairs={{1,2},{2,1},{5,6},{6,5},{9,10},{10,9},{13,14},{14,13},{17,18},{18,... | collective-permute-start | bytes 1327112 | tf_op jit(solution)/shard_map/ppermute | solution.py:739
  99.2 0.5 slice_bitcast_fusion
  99.7 5.1 %normed_values.1 = bf16[16,16,96,128]{3,2,1,0:T(8,128)(2,1)} custom-call(s32[11]{0:T(128)S(1)} %copy-done.5, f32[8,128]{1,0:T(8,128)S(1)} %get-tuple-element.64.totals, f32[8,128]{1,0:T(8,128)S(1)} %select_maximum_fusion.params, f32[24,8,8,96,128]{4,3,2,1,0:T(8,128)} %get-tuple-element.63.conv, ...), custom_call_target="tpu_custom_call", output_to_operand_aliasing={{}: (5, {})} | custom-call | flops 30000000 | bytes 8000000 | tf_op jit(solution)/shard_map/normed_values/pallas_call | solution.py:466
  104.8 0.9 all-to-all-done.1.parts
  105.7 0.9 share.1
  106.6 7.5 %all-to-all-start.2 = ((bf16[128,16,128]{2,1,0:T(8,128)(2,1)}), bf16[128,16,128]{2,1,0:T(8,128)(2,1)S(1)}, u32[]{:S(2)}, u32[]{:S(2)}) async-start(bf16[128,16,128]{2,1,0:T(8,128)(2,1)} %share.1), calls=%async_computation.2 | async-start | bytes 1048576 | tf_op jit(solution)/shard_map/all_to_all | solution.py:744
  114.1 0.0 collective-permute-done.8.ym
  114.1 0.0 collective-permute-done.9.yp
  114.1 13.6 %backward.1 = bf16[16,16,96,128]{3,2,1,0:T(8,128)(2,1)} custom-call(s32[11]{0:T(128)S(1)} %copy-done.5, bf16[48,8,8,96,128]{4,3,2,1,0:T(8,128)(2,1)} %get-tuple-element.77.kept, s32[16,16,128]{2,1,0:T(8,128)S(1)} %copy-done.1, bf16[16,96,128]{2,1,0:T(8,128)(2,1)S(1)} %collective-permute-done.6.refs_2_.xm, ...), custom_call_target="tpu_custom_call", output_to_operand_aliasing={{}: (8, {})} | custom-call | flops 16000000000 | bytes 5000000 | tf_op jit(solution)/shard_map/backward/pallas_call | solution.py:628
  127.7 0.0 all-to-all-done.2
  127.7 1.4 %arrange.1 = f32[27,96,96]{2,1,0:T(8,128)} custom-call(bf16[2048,128]{1,0:T(8,128)(2,1)S(1)} %bitcast.10), custom_call_target="tpu_custom_call" | custom-call | flops 300000 | bytes 1500000 | tf_op jit(solution)/shard_map/arrange/pallas_call | solution.py:566
  (2 shorter events, 0.0 us)
Async XLA Ops:
  0.6 14.1 %copy-start = (bf16[16,16,96,128]{3,2,1,0:T(8,128)(2,1)S(1)}, bf16[16,16,96,128]{3,2,1,0:T(8,128)(2,1)}, u32[]{:S(2)}) copy-start(bf16[16,16,96,128]{3,2,1,0:T(8,128)(2,1)} %features.5) | copy-start | bytes 18874372
  0.6 14.1 %copy-start.1 = (s32[16,16,128]{2,1,0:T(8,128)S(1)}, s32[16,16,128]{2,1,0:T(8,128)}, u32[]{:S(2)}) copy-start(s32[16,16,128]{2,1,0:T(8,128)} %mask.13) | copy-start | bytes 393220
  4.7 12.6 %collective-permute-start = (bf16[16,96,128]{2,1,0:T(8,128)(2,1)}, bf16[16,96,128]{2,1,0:T(8,128)(2,1)S(1)}, u32[]{:S(2)}, u32[]{:S(2)}) collective-permute-start(bf16[16,96,128]{2,1,0:T(8,128)(2,1)} %get-tuple-element.49), channel_id=1, source_target_pairs={{0,4},{4,0},{8,12},{12,8},{16,20},{20,16},{24,28},{28,24},{32,36},... | collective-permute-start | bytes 1179656 | tf_op jit(solution)/shard_map/ppermute | solution.py:738
  5.5 11.9 %collective-permute-start.1 = (bf16[16,96,128]{2,1,0:T(8,128)(2,1)}, bf16[16,96,128]{2,1,0:T(8,128)(2,1)S(1)}, u32[]{:S(2)}, u32[]{:S(2)}) collective-permute-start(bf16[16,96,128]{2,1,0:T(8,128)(2,1)} %get-tuple-element.50), channel_id=1, source_target_pairs={{4,8},{12,16},{20,24},{28,32},{36,40},{44,48},{52,56},{60,64},{68,... | collective-permute-start | bytes 1179656 | tf_op jit(solution)/shard_map/ppermute | solution.py:739
  8.9 11.2 %collective-permute-start.2 = (bf16[16,96,128]{2,1,0:T(8,128)(2,1)}, bf16[16,96,128]{2,1,0:T(8,128)(2,1)S(1)}, u32[]{:S(2)}, u32[]{:S(2)}) collective-permute-start(bf16[16,96,128]{2,1,0:T(8,128)(2,1)} %get-tuple-element.56), channel_id=1, source_target_pairs={{0,1},{1,0},{2,3},{3,2},{4,5},{5,4},{6,7},{7,6},{8,9},{9,8},{10,11... | collective-permute-start | bytes 1179656 | tf_op jit(solution)/shard_map/ppermute | solution.py:738
  9.3 11.5 %collective-permute-start.3 = (bf16[16,96,128]{2,1,0:T(8,128)(2,1)}, bf16[16,96,128]{2,1,0:T(8,128)(2,1)S(1)}, u32[]{:S(2)}, u32[]{:S(2)}) collective-permute-start(bf16[16,96,128]{2,1,0:T(8,128)(2,1)} %get-tuple-element.57), channel_id=1, source_target_pairs={{1,2},{2,1},{5,6},{6,5},{9,10},{10,9},{13,14},{14,13},{17,18},{18,... | collective-permute-start | bytes 1179656 | tf_op jit(solution)/shard_map/ppermute | solution.py:739
  13.1 1.1 copy-start.2
  14.2 8.9 %slice-start = ((s8[6291456]{0:T(1024)(128)(4,1)}), s8[4194304]{0:T(1024)(128)(4,1)S(1)}, s32[]{:S(2)}) async-start(s8[6291456]{0:T(1024)(128)(4,1)} %bitcast.8), calls=%async_computation.3 | async-start | bytes 8388608
  14.7 0.9 copy-start.4
  15.6 1.7 %copy-start.6 = (f32[96]{0:T(128)S(1)}, f32[96]{0:T(128)}, u32[]{:S(2)}) copy-start(f32[96]{0:T(128)} %param.10) | copy-start | bytes 1156
  15.6 1.7 %copy-start.7 = (f32[96]{0:T(128)S(1)}, f32[96]{0:T(128)}, u32[]{:S(2)}) copy-start(f32[96]{0:T(128)} %param.9) | copy-start | bytes 1156
  15.6 7.4 %slice-start.1 = ((s8[6291456]{0:T(1024)(128)(4,1)}), s8[2097152]{0:T(1024)(128)(4,1)S(1)}, s32[]{:S(2)}) async-start(s8[6291456]{0:T(1024)(128)(4,1)} %bitcast.8), calls=%async_computation.4 | async-start | bytes 4194304
  18.1 3.3 %collective-permute-start.4 = (bf16[2,96,128]{2,1,0:T(8,128)(2,1)S(1)}, bf16[2,96,128]{2,1,0:T(8,128)(2,1)S(1)}, u32[]{:S(2)}, u32[]{:S(2)}) collective-permute-start(bf16[2,96,128]{2,1,0:T(8,128)(2,1)S(1)} %get-tuple-element.58), channel_id=1, source_target_pairs={{0,1},{1,0},{2,3},{3,2},{4,5},{5,4},{6,7},{7,6},{8,9},{9,8},{10,11... | collective-permute-start | bytes 147464 | tf_op jit(solution)/shard_map/ppermute | solution.py:738
  18.2 40.4 %copy-start.5 = (s32[11]{0:T(128)S(1)}, s32[11]{0:T(128)}, u32[]{:S(2)}) copy-start(s32[11]{0:T(128)} %get-tuple-element.48.meta) | copy-start | bytes 136
  18.2 4.8 %collective-permute-start.5 = (bf16[2,96,128]{2,1,0:T(8,128)(2,1)S(1)}, bf16[2,96,128]{2,1,0:T(8,128)(2,1)S(1)}, u32[]{:S(2)}, u32[]{:S(2)}) collective-permute-start(bf16[2,96,128]{2,1,0:T(8,128)(2,1)S(1)} %get-tuple-element.59), channel_id=1, source_target_pairs={{1,2},{2,1},{5,6},{6,5},{9,10},{10,9},{13,14},{14,13},{17,18},{18,... | collective-permute-start | bytes 147464 | tf_op jit(solution)/shard_map/ppermute | solution.py:739
  63.8 8.5 %collective-permute-start.6 = (bf16[16,96,128]{2,1,0:T(8,128)(2,1)S(1)}, bf16[16,96,128]{2,1,0:T(8,128)(2,1)S(1)}, u32[]{:S(2)}, u32[]{:S(2)}) collective-permute-start(bf16[16,96,128]{2,1,0:T(8,128)(2,1)S(1)} %get-tuple-element.65), channel_id=1, source_target_pairs={{0,4},{4,0},{8,12},{12,8},{16,20},{20,16},{24,28},{28,24},{32,36},... | collective-permute-start | bytes 1179656 | tf_op jit(solution)/shard_map/ppermute | solution.py:738
  63.9 9.1 %collective-permute-start.7 = (bf16[16,96,128]{2,1,0:T(8,128)(2,1)S(1)}, bf16[16,96,128]{2,1,0:T(8,128)(2,1)S(1)}, u32[]{:S(2)}, u32[]{:S(2)}) collective-permute-start(bf16[16,96,128]{2,1,0:T(8,128)(2,1)S(1)} %get-tuple-element.66), channel_id=1, source_target_pairs={{4,8},{12,16},{20,24},{28,32},{36,40},{44,48},{52,56},{60,64},{68,... | collective-permute-start | bytes 1179656 | tf_op jit(solution)/shard_map/ppermute | solution.py:739
  83.9 2.0 %collective-permute-start.10 = (f32[16,64,128]{2,1,0:T(8,128)S(1)}, f32[16,64,128]{2,1,0:T(8,128)S(1)}, u32[]{:S(2)}, u32[]{:S(2)}) collective-permute-start(f32[16,64,128]{2,1,0:T(8,128)S(1)} %get-tuple-element.89), channel_id=1, source_target_pairs={{0,4},{4,0},{1,5},{5,1},{2,6},{6,2},{3,7},{7,3},{8,12},{12,8},{9,1... | collective-permute-start | bytes 1572872 | tf_op jit(solution)/shard_map/ppermute | solution.py:748
  86.8 19.0 %all-to-all-start.1 = ((f32[64,16,128]{2,1,0:T(8,128)}), f32[64,16,128]{2,1,0:T(8,128)S(1)}, u32[]{:S(2)}, u32[]{:S(2)}) async-start(f32[64,16,128]{2,1,0:T(8,128)} %bitcast.11), calls=%async_computation.1 | async-start | bytes 1048576 | tf_op jit(solution)/shard_map/all_to_all | solution.py:750
  94.5 0.8 copy-start.3
  95.2 18.9 %collective-permute-start.8 = (bf16[18,96,128]{2,1,0:T(8,128)(2,1)S(1)}, bf16[18,96,128]{2,1,0:T(8,128)(2,1)S(1)}, u32[]{:S(2)}, u32[]{:S(2)}) collective-permute-start(bf16[18,96,128]{2,1,0:T(8,128)(2,1)S(1)} %get-tuple-element.82), channel_id=1, source_target_pairs={{0,1},{1,0},{2,3},{3,2},{4,5},{5,4},{6,7},{7,6},{8,9},{9,8},{10,11... | collective-permute-start | bytes 1327112 | tf_op jit(solution)/shard_map/ppermute | solution.py:738
  95.7 18.4 %collective-permute-start.9 = (bf16[18,96,128]{2,1,0:T(8,128)(2,1)}, bf16[18,96,128]{2,1,0:T(8,128)(2,1)S(1)}, u32[]{:S(2)}, u32[]{:S(2)}) collective-permute-start(bf16[18,96,128]{2,1,0:T(8,128)(2,1)} %copy-done.3), channel_id=1, source_target_pairs={{1,2},{2,1},{5,6},{6,5},{9,10},{10,9},{13,14},{14,13},{17,18},{18,... | collective-permute-start | bytes 1327112 | tf_op jit(solution)/shard_map/ppermute | solution.py:739
  106.6 21.1 %all-to-all-start.2 = ((bf16[128,16,128]{2,1,0:T(8,128)(2,1)}), bf16[128,16,128]{2,1,0:T(8,128)(2,1)S(1)}, u32[]{:S(2)}, u32[]{:S(2)}) async-start(bf16[128,16,128]{2,1,0:T(8,128)(2,1)} %share.1), calls=%async_computation.2 | async-start | bytes 1048576 | tf_op jit(solution)/shard_map/all_to_all | solution.py:744
